TPU v7x, 256 devices: a whole 4x4x8 slice. The times are simulated.
256 devices in a mesh: hst: 64 (over z, x, core), chip: 4 (over y).
Axes of the slice: x: 4, y: 4, z: 8, core: 2. Of those that a mesh axis runs over, the one named last changes fastest.
Arguments:
- data: bfloat16 [262144, 4096], P(('hst', 'chip')), as said below
- sketch: bfloat16 [4096, 128], replicated, may hold values from -0.09375 to 0.09375
Outputs:
- first_basis: float32 [262144, 128], P(('hst', 'chip'))
- basis: float32 [262144, 128], P(('hst', 'chip'))
- projected: float32 [128, 4096], replicated
Inputs may be any that keep to these rules, and one draw needn't show every extreme that they name: `data`: rows and columns have unequal scales; the matrix has full column rank.
All inputs are finite; a program needn't handle non-finite values.
Results may differ from a plain program's by a relative error of at most 0.0029.
Values sent between devices are 32-bit elements; how exact they have to be, the bound alone decides.
No kernel may reach another device: no remote copies, remote signals or barrier semaphores. Data moves between devices by JAX's collectives and lax.ppermute only.
A program may use at most 128 MiB of HBM per device.

v0:
```python
import functools

import jax
import jax.numpy as jnp
from jax import lax
from jax.experimental import pallas as pl
from jax.experimental.pallas import tpu as pltpu
from jax.sharding import Mesh, PartitionSpec as P

D = 4096
K = 128
Z, X, C, Y = 8, 4, 2, 4
AXES = ("z", "x", "core", "y")
PLANE = X * Y
HALF = D // C
WIDE = HALF // PLANE
THIN = K // PLANE
ROWS = K + THIN
ROOT_ROWS = 512.0
BLOCK = 256
STEPS = 4
VMEM = 48 * 2**20


def device_number(z, x, core, y):
    return ((z * X + x) * C + core) * Y + y


def exchange(value, partner):
    pairs = []
    for z in range(Z):
        for x in range(X):
            for core in range(C):
                for y in range(Y):
                    pairs.append((device_number(z, x, core, y), device_number(*partner(z, x, core, y))))
    return lax.ppermute(value, AXES, pairs)


def other_core(value):
    return exchange(value, lambda z, x, core, y: (z, x, 1 - core, y))


def sum_everywhere(give, keep):
    half = keep + other_core(give)
    part = lax.all_to_all(half, ("x", "y"), split_axis=0, concat_axis=0, tiled=True)
    part = jnp.sum(part, axis=0)
    for mask in (1, 3, 7):
        part = part + exchange(part, lambda z, x, core, y: (z ^ mask, x, core, y))
    half = lax.all_to_all(
        jnp.broadcast_to(part, (PLANE,) + part.shape), ("x", "y"), split_axis=0, concat_axis=0, tiled=True
    )
    return half, other_core(half)


def exact_dot(left, right, dims):
    return lax.dot_general(
        left, right, (dims, ((), ())), precision=lax.Precision.HIGHEST, preferred_element_type=jnp.float32
    )


def quick_dot(left, right, dims=((1,), (0,))):
    return lax.dot_general(left, right, (dims, ((), ())), preferred_element_type=jnp.float32)


def two_terms(value):
    high = value.astype(jnp.bfloat16)
    return high, (value - high.astype(jnp.float32)).astype(jnp.bfloat16)


def inverse_factor(gram):
    row = lax.broadcasted_iota(jnp.int32, (K, K), 0)
    column = lax.broadcasted_iota(jnp.int32, (K, K), 1)
    diagonal = jnp.where(row == column, gram, 0.0)
    across = lax.rsqrt(jnp.sum(diagonal, axis=0, keepdims=True))
    down = lax.rsqrt(jnp.sum(diagonal, axis=1, keepdims=True))
    scaled = gram * across * down
    groups = [scaled[8 * g : 8 * g + 8] for g in range(K // 8)]
    lane = lax.broadcasted_iota(jnp.int32, (8, K), 1)
    sub = lax.broadcasted_iota(jnp.int32, (8, K), 0)

    def spread(value, k):
        return jnp.broadcast_to(value[:, k : k + 1], (8, K))

    for k in range(0, K, 4):
        g0, off = k // 8, k % 8
        mine = groups[g0]
        raw = [jnp.broadcast_to(mine[off + t : off + t + 1], (8, K)) for t in range(4)]
        s = {(i, j): spread(raw[i], k + j) for i in range(4) for j in range(i + 1)}
        inside = (lane >= k) & (lane < k + 4)
        e = [jnp.where(inside, jnp.where(lane == k + t, 1.0, 0.0), raw[t]) for t in range(4)]
        a, b, c = s[0, 0], s[1, 0], s[1, 1]
        turn = 1.0 / (a * c - b * b)
        ca, cb, cc = a * turn, b * turn, c * turn
        u0 = cc * e[0] - cb * e[1]
        u1 = ca * e[1] - cb * e[0]
        v20 = cc * s[2, 0] - cb * s[2, 1]
        v21 = ca * s[2, 1] - cb * s[2, 0]
        v30 = cc * s[3, 0] - cb * s[3, 1]
        v31 = ca * s[3, 1] - cb * s[3, 0]
        p = s[2, 2] - s[2, 0] * v20 - s[2, 1] * v21
        q = s[3, 2] - s[3, 0] * v20 - s[3, 1] * v21
        r = s[3, 3] - s[3, 0] * v30 - s[3, 1] * v31
        e2 = e[2] - s[2, 0] * u0 - s[2, 1] * u1
        e3 = e[3] - s[3, 0] * u0 - s[3, 1] * u1
        turn = 1.0 / (p * r - q * q)
        u2 = (r * turn) * e2 - (q * turn) * e3
        u3 = (p * turn) * e3 - (q * turn) * e2
        u0 = u0 - v20 * u2 - v30 * u3
        u1 = u1 - v21 * u2 - v31 * u3
        upper, lower = b / a, q / p
        done = [
            e[0] * lax.rsqrt(a),
            (e[1] - upper * e[0]) * lax.rsqrt(c - upper * b),
            e2 * lax.rsqrt(p),
            (e3 - lower * e2) * lax.rsqrt(r - lower * q),
        ]
        for g in range(g0 + (off == 4), K // 8):
            value = groups[g]
            change = spread(value, k) * u0 + spread(value, k + 1) * u1
            change = change + spread(value, k + 2) * u2 + spread(value, k + 3) * u3
            groups[g] = jnp.where(inside, 0.0, value) - change
        value = groups[g0]
        for t in range(4):
            value = jnp.where(sub == off + t, done[t], value)
        groups[g0] = value
    full = jnp.concatenate(groups, axis=0)
    return jnp.where(row >= column, full, 0.0) * across


def add_rows(block, part, gram, total):
    gram[...] += exact_dot(part, part, ((0,), (0,)))
    high, low = two_terms(part)
    both = jnp.concatenate([high, low], axis=1).T
    total[...] += quick_dot(both, block)


def clear(gram, total):
    gram[...] = jnp.zeros_like(gram)
    total[...] = jnp.zeros_like(total)


def hand_over(core, gram, total, give, keep):
    for ref, start in ((give, (1 - core) * HALF), (keep, core * HALF)):
        for j in range(PLANE):
            columns = pl.ds(pl.multiple_of(start + WIDE * j, WIDE), WIDE)
            ref[j, :K, :] = total[:K, columns] + total[K:, columns]
            ref[j, K:, :] = gram[THIN * j : THIN * (j + 1), :]


def start_kernel(core, data, sketch, first, give, keep, gram, total):
    step = pl.program_id(0)

    @pl.when(step == 0)
    def _():
        clear(gram, total)

    part = quick_dot(data[...], sketch[...])
    first[...] = part
    add_rows(data[...], part, gram, total)

    @pl.when(step == STEPS - 1)
    def _():
        hand_over(core[0], gram, total, give, keep)


def all_terms(core, own, other):
    for ref, start in ((own, core * HALF), (other, (1 - core) * HALF)):
        for j in range(0, PLANE, 2):
            yield pl.multiple_of(start + WIDE * j, 2 * WIDE), jnp.concatenate([ref[j, :K, :], ref[j + 1, :K, :]], axis=1)


def apply_factor(inverse, terms):
    high, low = two_terms(inverse)
    left = jnp.concatenate(
        [jnp.concatenate([high, high], axis=1), jnp.concatenate([low, jnp.zeros_like(low)], axis=1)], axis=0
    )
    both = quick_dot(left, jnp.concatenate(two_terms(terms), axis=0))
    return both[:K] + both[K:]


def summed_gram(own):
    return jnp.concatenate([own[j, K:, :] for j in range(PLANE)], axis=0)


def middle_kernel(core, own, other, data, inverse, second, give, keep, held, back, gram, total, arrived):
    copies = [
        pltpu.make_async_copy(data.at[pl.ds(b * BLOCK, BLOCK)], held.at[pl.ds(b * BLOCK, BLOCK)], arrived.at[b])
        for b in range(STEPS)
    ]
    for copy in copies:
        copy.start()
    clear(gram, total)
    inverse[...] = inverse_factor(summed_gram(own))
    scaled = inverse[...] * (1.0 / ROOT_ROWS)
    for start, terms in all_terms(core[0], own, other):
        back[:, pl.ds(start, 2 * WIDE)] = apply_factor(scaled, terms).astype(jnp.bfloat16)
    for b in range(STEPS):
        copies[b].wait()
        rows = pl.ds(b * BLOCK, BLOCK)
        part = quick_dot(held[rows, :], back[...], ((1,), (1,)))
        second[rows, :] = part
        add_rows(held[rows, :], part, gram, total)
    hand_over(core[0], gram, total, give, keep)


def final_kernel(core, own, other, inverse, projected):
    inverse[...] = inverse_factor(summed_gram(own))
    scaled = inverse[...] * (D**0.5 / ROOT_ROWS)
    for start, terms in all_terms(core[0], own, other):
        projected[:, pl.ds(start, 2 * WIDE)] = apply_factor(scaled, terms)


def params():
    return pltpu.CompilerParams(vmem_limit_bytes=VMEM)


VM = pl.BlockSpec(memory_space=pltpu.VMEM)
SM = pl.BlockSpec(memory_space=pltpu.SMEM)
MESSAGE = jax.ShapeDtypeStruct((PLANE, ROWS, K), jnp.float32)
SQUARE = jax.ShapeDtypeStruct((K, K), jnp.float32)
SUMS = [pltpu.VMEM((K, K), jnp.float32), pltpu.VMEM((2 * K, D), jnp.float32)]


def start_call(core, data, sketch):
    tall = jax.ShapeDtypeStruct((data.shape[0], K), jnp.float32)
    whole = pl.BlockSpec((PLANE, ROWS, K), lambda i: (0, 0, 0))
    return pl.pallas_call(
        start_kernel,
        grid=(STEPS,),
        out_shape=(tall, MESSAGE, MESSAGE),
        in_specs=[SM, pl.BlockSpec((BLOCK, D), lambda i: (i, 0)), pl.BlockSpec((D, K), lambda i: (0, 0))],
        out_specs=(pl.BlockSpec((BLOCK, K), lambda i: (i, 0)), whole, whole),
        scratch_shapes=SUMS,
        compiler_params=params(),
        name="start",
    )(core, data, sketch)


def middle_call(core, own, other, data):
    tall = jax.ShapeDtypeStruct((data.shape[0], K), jnp.float32)
    return pl.pallas_call(
        middle_kernel,
        out_shape=(SQUARE, tall, MESSAGE, MESSAGE),
        in_specs=[SM, VM, VM, pl.BlockSpec(memory_space=pl.ANY)],
        out_specs=(VM, VM, VM, VM),
        scratch_shapes=[pltpu.VMEM(data.shape, jnp.bfloat16), pltpu.VMEM((K, D), jnp.bfloat16)]
        + SUMS
        + [pltpu.SemaphoreType.DMA((STEPS,))],
        compiler_params=params(),
        name="middle",
    )(core, own, other, data)


def final_call(core, own, other):
    return pl.pallas_call(
        final_kernel,
        out_shape=(SQUARE, jax.ShapeDtypeStruct((K, D), jnp.float32)),
        in_specs=[SM, VM, VM],
        out_specs=(VM, VM),
        compiler_params=params(),
        name="final",
    )(core, own, other)


def on_device(data, sketch):
    core = lax.axis_index("core").astype(jnp.int32).reshape(1)
    first, give, keep = start_call(core, data, sketch)
    own, other = sum_everywhere(give, keep)
    inverse, second, give, keep = middle_call(core, own, other, data)
    first_basis = exact_dot(first, ROOT_ROWS * inverse, ((1,), (1,)))
    own, other = sum_everywhere(give, keep)
    inverse, projected = final_call(core, own, other)
    basis = exact_dot(second, ROOT_ROWS * inverse, ((1,), (1,)))
    return (first_basis, basis, projected)


def solution(mesh):
    split = Mesh(mesh.devices.reshape(Z, X, C, Y), AXES)
    return jax.shard_map(
        on_device,
        mesh=split,
        in_specs=(P(AXES, None), P()),
        out_specs=(P(AXES, None), P(AXES, None), P()),
        check_vma=False,
    )
```

profile of v0, /device:TPU:1, one launch (start us, length us, event | category | flops | bytes accessed | tf_op | source)
XLA Modules:
  0.0 166.4 jit_solution(2619863918319554121)
XLA Ops:
  0.6 0.0 copy-start
  0.6 1.2 copy-done
  1.9 8.7 %start.1 = (f32[1024,128]{1,0:T(8,128)S(1)}, f32[16,136,128]{2,1,0:T(8,128)S(1)}, f32[16,136,128]{2,1,0:T(8,128)S(1)}) custom-call(s32[1]{0:T(128)} %bitcast.core, bf16[1024,4096]{1,0:T(8,128)(2,1)} %data.3, bf16[4096,128]{1,0:T(8,128)(2,1)S(1)} %copy-done), custom_call_target="tpu_custom_call" | custom-call | tf_op jit(solution)/shard_map/start/pallas_call | solution.py:227
  10.5 3.3 %collective-permute-start = (f32[16,136,128]{2,1,0:T(8,128)S(1)}, f32[16,136,128]{2,1,0:T(8,128)S(1)}, u32[]{:S(2)}, u32[]{:S(2)}) collective-permute-start(f32[16,136,128]{2,1,0:T(8,128)S(1)} %get-tuple-element.14), channel_id=1, source_target_pairs={{0,4},{1,5},{2,6},{3,7},{4,0},{5,1},{6,2},{7,3},{8,12},{9,13},{10,... | collective-permute-start | bytes 3342344 | tf_op jit(solution)/shard_map/ppermute | solution.py:36
  13.8 2.4 %collective-permute-done = f32[16,136,128]{2,1,0:T(8,128)S(1)} collective-permute-done((f32[16,136,128]{2,1,0:T(8,128)S(1)}, f32[16,136,128]{2,1,0:T(8,128)S(1)}, u32[]{:S(2)}, u32[]{:S(2)}) %collective-permute-start) | collective-permute-done | bytes 1114144 | tf_op jit(solution)/shard_map/ppermute | solution.py:36
  16.2 0.1 add.24
  16.3 21.9 %all_to_all.20 = f32[16,136,128]{2,1,0:T(8,128)S(1)} all-to-all(f32[16,136,128]{2,1,0:T(8,128)S(1)} %add.24), channel_id=1, replica_groups=mesh['z'=8,'x'=4,'core'=2,'y'=4] {'x','y'}, dimensions={0} | all-to-all | bytes 2228224 | tf_op jit(solution)/shard_map/all_to_all | solution.py:45
  38.3 0.1 reduce_sum.18
  38.3 1.7 %collective-permute-start.1 = (f32[136,128]{1,0:T(8,128)S(1)}, f32[136,128]{1,0:T(8,128)S(1)}, u32[]{:S(2)}, u32[]{:S(2)}) collective-permute-start(f32[136,128]{1,0:T(8,128)S(1)} %reduce_sum.18), channel_id=1, source_target_pairs={{0,32},{1,33},{2,34},{3,35},{4,36},{5,37},{6,38},{7,39},{8,40},{9,... | collective-permute-start | bytes 208904 | tf_op jit(solution)/shard_map/ppermute | solution.py:36
  40.1 1.7 %collective-permute-done.1 = f32[136,128]{1,0:T(8,128)S(1)} collective-permute-done((f32[136,128]{1,0:T(8,128)S(1)}, f32[136,128]{1,0:T(8,128)S(1)}, u32[]{:S(2)}, u32[]{:S(2)}) %collective-permute-start.1) | collective-permute-done | bytes 69664 | tf_op jit(solution)/shard_map/ppermute | solution.py:36
  41.8 4.2 %collective-permute-start.2 = (f32[136,128]{1,0:T(8,128)S(1)}, f32[136,128]{1,0:T(8,128)S(1)}, u32[]{:S(2)}, u32[]{:S(2)}) collective-permute-start(f32[136,128]{1,0:T(8,128)S(1)} %add.25), channel_id=1, source_target_pairs={{0,96},{1,97},{2,98},{3,99},{4,100},{5,101},{6,102},{7,103},{8,104... | collective-permute-start | bytes 208904 | tf_op jit(solution)/shard_map/ppermute | solution.py:36
  46.0 1.7 %collective-permute-done.2 = f32[136,128]{1,0:T(8,128)S(1)} collective-permute-done((f32[136,128]{1,0:T(8,128)S(1)}, f32[136,128]{1,0:T(8,128)S(1)}, u32[]{:S(2)}, u32[]{:S(2)}) %collective-permute-start.2) | collective-permute-done | bytes 69664 | tf_op jit(solution)/shard_map/ppermute | solution.py:36
  47.8 4.6 %collective-permute-start.3 = (f32[136,128]{1,0:T(8,128)S(1)}, f32[136,128]{1,0:T(8,128)S(1)}, u32[]{:S(2)}, u32[]{:S(2)}) collective-permute-start(f32[136,128]{1,0:T(8,128)S(1)} %add.26), channel_id=1, source_target_pairs={{0,224},{1,225},{2,226},{3,227},{4,228},{5,229},{6,230},{7,231},{8... | collective-permute-start | bytes 208904 | tf_op jit(solution)/shard_map/ppermute | solution.py:36
  52.3 1.7 %collective-permute-done.3 = f32[136,128]{1,0:T(8,128)S(1)} collective-permute-done((f32[136,128]{1,0:T(8,128)S(1)}, f32[136,128]{1,0:T(8,128)S(1)}, u32[]{:S(2)}, u32[]{:S(2)}) %collective-permute-start.3) | collective-permute-done | bytes 69664 | tf_op jit(solution)/shard_map/ppermute | solution.py:36
  54.0 0.1 broadcast_in_dim.6
  54.1 15.6 %all_to_all.21.own = f32[16,136,128]{2,1,0:T(8,128)S(1)} all-to-all(f32[16,136,128]{2,1,0:T(8,128)S(1)} %broadcast_in_dim.6), channel_id=1, replica_groups=mesh['z'=8,'x'=4,'core'=2,'y'=4] {'x','y'}, dimensions={0} | all-to-all | bytes 2228224 | tf_op jit(solution)/shard_map/all_to_all | solution.py:49
  69.8 6.3 %collective-permute-start.4 = (f32[16,136,128]{2,1,0:T(8,128)S(1)}, f32[16,136,128]{2,1,0:T(8,128)S(1)}, u32[]{:S(2)}, u32[]{:S(2)}) collective-permute-start(f32[16,136,128]{2,1,0:T(8,128)S(1)} %all_to_all.21.own), channel_id=1, source_target_pairs={{0,4},{1,5},{2,6},{3,7},{4,0},{5,1},{6,2},{7,3},{8,12},{9,13},{10,... | collective-permute-start | bytes 3342344 | tf_op jit(solution)/shard_map/ppermute | solution.py:36
  76.0 2.4 %collective-permute-done.4.other = f32[16,136,128]{2,1,0:T(8,128)S(1)} collective-permute-done((f32[16,136,128]{2,1,0:T(8,128)S(1)}, f32[16,136,128]{2,1,0:T(8,128)S(1)}, u32[]{:S(2)}, u32[]{:S(2)}) %collective-permute-start.4) | collective-permute-done | bytes 1114144 | tf_op jit(solution)/shard_map/ppermute | solution.py:36
  78.4 18.0 %middle.1 = (f32[128,128]{1,0:T(8,128)S(1)}, f32[1024,128]{1,0:T(8,128)S(1)}, f32[16,136,128]{2,1,0:T(8,128)S(1)}, f32[16,136,128]{2,1,0:T(8,128)S(1)}) custom-call(s32[1]{0:T(128)} %bitcast.core, f32[16,136,128]{2,1,0:T(8,128)S(1)} %all_to_all.21.own, f32[16,136,128]{2,1,0:T(8,128)S(1)} %collective-permute-done.4.other, bf16[1024,4096]{1,0:T(8,128)(2,1)} %data.3), custom_call_target="tpu_custom_call" | custom-call | tf_op jit(solution)/shard_map/middle/pallas_call | solution.py:241
  96.4 0.5 collective-permute-start.5
  96.9 2.4 %collective-permute-done.5 = f32[16,136,128]{2,1,0:T(8,128)S(1)} collective-permute-done((f32[16,136,128]{2,1,0:T(8,128)S(1)}, f32[16,136,128]{2,1,0:T(8,128)S(1)}, u32[]{:S(2)}, u32[]{:S(2)}) %collective-permute-start.5) | collective-permute-done | bytes 1114144 | tf_op jit(solution)/shard_map/ppermute | solution.py:36
  99.3 0.1 add.28
  99.4 20.1 %all_to_all.22 = f32[16,136,128]{2,1,0:T(8,128)S(1)} all-to-all(f32[16,136,128]{2,1,0:T(8,128)S(1)} %add.28), channel_id=1, replica_groups=mesh['z'=8,'x'=4,'core'=2,'y'=4] {'x','y'}, dimensions={0} | all-to-all | bytes 2228224 | tf_op jit(solution)/shard_map/all_to_all | solution.py:45
  119.5 0.1 reduce_sum.19
  119.5 0.1 collective-permute-start.6
  119.6 3.1 %collective-permute-done.6 = f32[136,128]{1,0:T(8,128)S(1)} collective-permute-done((f32[136,128]{1,0:T(8,128)S(1)}, f32[136,128]{1,0:T(8,128)S(1)}, u32[]{:S(2)}, u32[]{:S(2)}) %collective-permute-start.6) | collective-permute-done | bytes 69664 | tf_op jit(solution)/shard_map/ppermute | solution.py:36
  122.8 1.7 %collective-permute-start.7 = (f32[136,128]{1,0:T(8,128)S(1)}, f32[136,128]{1,0:T(8,128)S(1)}, u32[]{:S(2)}, u32[]{:S(2)}) collective-permute-start(f32[136,128]{1,0:T(8,128)S(1)} %add.29), channel_id=1, source_target_pairs={{0,96},{1,97},{2,98},{3,99},{4,100},{5,101},{6,102},{7,103},{8,104... | collective-permute-start | bytes 208904 | tf_op jit(solution)/shard_map/ppermute | solution.py:36
  124.5 3.3 %collective-permute-done.7 = f32[136,128]{1,0:T(8,128)S(1)} collective-permute-done((f32[136,128]{1,0:T(8,128)S(1)}, f32[136,128]{1,0:T(8,128)S(1)}, u32[]{:S(2)}, u32[]{:S(2)}) %collective-permute-start.7) | collective-permute-done | bytes 69664 | tf_op jit(solution)/shard_map/ppermute | solution.py:36
  127.8 3.1 %collective-permute-start.8 = (f32[136,128]{1,0:T(8,128)S(1)}, f32[136,128]{1,0:T(8,128)S(1)}, u32[]{:S(2)}, u32[]{:S(2)}) collective-permute-start(f32[136,128]{1,0:T(8,128)S(1)} %add.30), channel_id=1, source_target_pairs={{0,224},{1,225},{2,226},{3,227},{4,228},{5,229},{6,230},{7,231},{8... | collective-permute-start | bytes 208904 | tf_op jit(solution)/shard_map/ppermute | solution.py:36
  130.9 1.7 %collective-permute-done.8 = f32[136,128]{1,0:T(8,128)S(1)} collective-permute-done((f32[136,128]{1,0:T(8,128)S(1)}, f32[136,128]{1,0:T(8,128)S(1)}, u32[]{:S(2)}, u32[]{:S(2)}) %collective-permute-start.8) | collective-permute-done | bytes 69664 | tf_op jit(solution)/shard_map/ppermute | solution.py:36
  132.6 0.1 broadcast_in_dim.7
  132.7 15.6 %all_to_all.23.own = f32[16,136,128]{2,1,0:T(8,128)S(1)} all-to-all(f32[16,136,128]{2,1,0:T(8,128)S(1)} %broadcast_in_dim.7), channel_id=1, replica_groups=mesh['z'=8,'x'=4,'core'=2,'y'=4] {'x','y'}, dimensions={0} | all-to-all | bytes 2228224 | tf_op jit(solution)/shard_map/all_to_all | solution.py:49
  148.3 6.2 %collective-permute-start.9 = (f32[16,136,128]{2,1,0:T(8,128)S(1)}, f32[16,136,128]{2,1,0:T(8,128)S(1)}, u32[]{:S(2)}, u32[]{:S(2)}) collective-permute-start(f32[16,136,128]{2,1,0:T(8,128)S(1)} %all_to_all.23.own), channel_id=1, source_target_pairs={{0,4},{1,5},{2,6},{3,7},{4,0},{5,1},{6,2},{7,3},{8,12},{9,13},{10,... | collective-permute-start | bytes 3342344 | tf_op jit(solution)/shard_map/ppermute | solution.py:36
  154.6 1.4 fusion.2
  155.9 1.0 collective-permute-done.9.other
  157.0 8.1 %final.1 = (f32[128,128]{1,0:T(8,128)S(1)}, f32[128,4096]{1,0:T(8,128)}) custom-call(s32[1]{0:T(128)} %bitcast.core, f32[16,136,128]{2,1,0:T(8,128)S(1)} %all_to_all.23.own, f32[16,136,128]{2,1,0:T(8,128)S(1)} %collective-permute-done.9.other), custom_call_target="tpu_custom_call" | custom-call | tf_op jit(solution)/shard_map/final/pallas_call | solution.py:255
  165.0 1.4 fusion
  (6 shorter events, 0.1 us)
Async XLA Ops:
  0.6 1.2 copy-start
  10.5 5.7 %collective-permute-start = (f32[16,136,128]{2,1,0:T(8,128)S(1)}, f32[16,136,128]{2,1,0:T(8,128)S(1)}, u32[]{:S(2)}, u32[]{:S(2)}) collective-permute-start(f32[16,136,128]{2,1,0:T(8,128)S(1)} %get-tuple-element.14), channel_id=1, source_target_pairs={{0,4},{1,5},{2,6},{3,7},{4,0},{5,1},{6,2},{7,3},{8,12},{9,13},{10,... | collective-permute-start | bytes 3342344 | tf_op jit(solution)/shard_map/ppermute | solution.py:36
  38.3 3.4 %collective-permute-start.1 = (f32[136,128]{1,0:T(8,128)S(1)}, f32[136,128]{1,0:T(8,128)S(1)}, u32[]{:S(2)}, u32[]{:S(2)}) collective-permute-start(f32[136,128]{1,0:T(8,128)S(1)} %reduce_sum.18), channel_id=1, source_target_pairs={{0,32},{1,33},{2,34},{3,35},{4,36},{5,37},{6,38},{7,39},{8,40},{9,... | collective-permute-start | bytes 208904 | tf_op jit(solution)/shard_map/ppermute | solution.py:36
  41.8 5.9 %collective-permute-start.2 = (f32[136,128]{1,0:T(8,128)S(1)}, f32[136,128]{1,0:T(8,128)S(1)}, u32[]{:S(2)}, u32[]{:S(2)}) collective-permute-start(f32[136,128]{1,0:T(8,128)S(1)} %add.25), channel_id=1, source_target_pairs={{0,96},{1,97},{2,98},{3,99},{4,100},{5,101},{6,102},{7,103},{8,104... | collective-permute-start | bytes 208904 | tf_op jit(solution)/shard_map/ppermute | solution.py:36
  47.8 6.3 %collective-permute-start.3 = (f32[136,128]{1,0:T(8,128)S(1)}, f32[136,128]{1,0:T(8,128)S(1)}, u32[]{:S(2)}, u32[]{:S(2)}) collective-permute-start(f32[136,128]{1,0:T(8,128)S(1)} %add.26), channel_id=1, source_target_pairs={{0,224},{1,225},{2,226},{3,227},{4,228},{5,229},{6,230},{7,231},{8... | collective-permute-start | bytes 208904 | tf_op jit(solution)/shard_map/ppermute | solution.py:36
  69.8 8.6 %collective-permute-start.4 = (f32[16,136,128]{2,1,0:T(8,128)S(1)}, f32[16,136,128]{2,1,0:T(8,128)S(1)}, u32[]{:S(2)}, u32[]{:S(2)}) collective-permute-start(f32[16,136,128]{2,1,0:T(8,128)S(1)} %all_to_all.21.own), channel_id=1, source_target_pairs={{0,4},{1,5},{2,6},{3,7},{4,0},{5,1},{6,2},{7,3},{8,12},{9,13},{10,... | collective-permute-start | bytes 3342344 | tf_op jit(solution)/shard_map/ppermute | solution.py:36
  96.4 2.8 %collective-permute-start.5 = (f32[16,136,128]{2,1,0:T(8,128)S(1)}, f32[16,136,128]{2,1,0:T(8,128)S(1)}, u32[]{:S(2)}, u32[]{:S(2)}) collective-permute-start(f32[16,136,128]{2,1,0:T(8,128)S(1)} %get-tuple-element.18), channel_id=1, source_target_pairs={{0,4},{1,5},{2,6},{3,7},{4,0},{5,1},{6,2},{7,3},{8,12},{9,13},{10,... | collective-permute-start | bytes 3342344 | tf_op jit(solution)/shard_map/ppermute | solution.py:36
  119.5 3.2 %collective-permute-start.6 = (f32[136,128]{1,0:T(8,128)S(1)}, f32[136,128]{1,0:T(8,128)S(1)}, u32[]{:S(2)}, u32[]{:S(2)}) collective-permute-start(f32[136,128]{1,0:T(8,128)S(1)} %reduce_sum.19), channel_id=1, source_target_pairs={{0,32},{1,33},{2,34},{3,35},{4,36},{5,37},{6,38},{7,39},{8,40},{9,... | collective-permute-start | bytes 208904 | tf_op jit(solution)/shard_map/ppermute | solution.py:36
  122.8 5.0 %collective-permute-start.7 = (f32[136,128]{1,0:T(8,128)S(1)}, f32[136,128]{1,0:T(8,128)S(1)}, u32[]{:S(2)}, u32[]{:S(2)}) collective-permute-start(f32[136,128]{1,0:T(8,128)S(1)} %add.29), channel_id=1, source_target_pairs={{0,96},{1,97},{2,98},{3,99},{4,100},{5,101},{6,102},{7,103},{8,104... | collective-permute-start | bytes 208904 | tf_op jit(solution)/shard_map/ppermute | solution.py:36
  127.8 4.8 %collective-permute-start.8 = (f32[136,128]{1,0:T(8,128)S(1)}, f32[136,128]{1,0:T(8,128)S(1)}, u32[]{:S(2)}, u32[]{:S(2)}) collective-permute-start(f32[136,128]{1,0:T(8,128)S(1)} %add.30), channel_id=1, source_target_pairs={{0,224},{1,225},{2,226},{3,227},{4,228},{5,229},{6,230},{7,231},{8... | collective-permute-start | bytes 208904 | tf_op jit(solution)/shard_map/ppermute | solution.py:36
  148.3 8.6 %collective-permute-start.9 = (f32[16,136,128]{2,1,0:T(8,128)S(1)}, f32[16,136,128]{2,1,0:T(8,128)S(1)}, u32[]{:S(2)}, u32[]{:S(2)}) collective-permute-start(f32[16,136,128]{2,1,0:T(8,128)S(1)} %all_to_all.23.own), channel_id=1, source_target_pairs={{0,4},{1,5},{2,6},{3,7},{4,0},{5,1},{6,2},{7,3},{8,12},{9,13},{10,... | collective-permute-start | bytes 3342344 | tf_op jit(solution)/shard_map/ppermute | solution.py:36
where the time goes:
time: 167 us; the launch traced here: 166 us
  blocking collectives  73.3 us (44%)
  Pallas kernels  34.8 us (21%)
  starting transfers between devices  31.7 us (19%)
  waiting for transfers between devices  21.4 us (13%)
  matrix products  2.75 us (2%)
    all_to_all x2, blocking collectives, sum_everywhere(): lax.all_to_all(half, ('x', 'y'), split_axis=0, concat_axis=0, tiled=True)  42 us
    ppermute x10, starting transfers between devices, exchange(): return lax.ppermute(value, AXES, pairs)  31.7 us
    all_to_all x2, blocking collectives, sum_everywhere(): lax.all_to_all(jnp.broadcast_to(part, (PLANE,) + part.shape), ('x', 'y'),...  31.3 us
    ppermute x10, waiting for transfers between devices, exchange(): return lax.ppermute(value, AXES, pairs)  21.4 us
    pallas_call x1, Pallas kernels, middle_call(): pl.pallas_call(middle_kernel, out_shape=(SQUARE, tall, MESSAGE, MESSAGE),...  18 us
    pallas_call x1, Pallas kernels, start_call(): pl.pallas_call(start_kernel, grid=(STEPS,), out_shape=(tall, MESSAGE, MES...  8.65 us
    pallas_call x1, Pallas kernels, final_call(): pl.pallas_call(final_kernel, out_shape=(SQUARE, jax.ShapeDtypeStruct((K,...  8.09 us
  transfers between devices with their start and end apart: 10, of which 10 were waited for; matrix products, arithmetic and copies ran while one was open for 1% of the time, Pallas kernels for 0%

commit v1 on v0

v1 whole, which is shorter than its diff:
```python
import jax
import jax.numpy as jnp
from jax import lax
from jax.experimental import pallas as pl
from jax.experimental.pallas import tpu as pltpu
from jax.sharding import Mesh, PartitionSpec as P

D = 4096
K = 128
Z, X, C, Y = 8, 4, 2, 4
AXES = ("z", "x", "core", "y")
PLANE = X * Y
HALF = D // C
WIDE = HALF // PLANE
THIN = K // PLANE
ROWS = K + THIN
ROOT_ROWS = 512.0
BLOCK = 256
COLUMNS = 512
STEPS = 4
VMEM = 48 * 2**20


def device_number(z, x, core, y):
    return ((z * X + x) * C + core) * Y + y


def exchange(value, partner):
    pairs = []
    for z in range(Z):
        for x in range(X):
            for core in range(C):
                for y in range(Y):
                    pairs.append((device_number(z, x, core, y), device_number(*partner(z, x, core, y))))
    return lax.ppermute(value, AXES, pairs)


def other_core(value):
    return exchange(value, lambda z, x, core, y: (z, x, 1 - core, y))


def sum_everywhere(give, keep):
    half = keep + other_core(give)
    part = lax.all_to_all(half, ("x", "y"), split_axis=0, concat_axis=0, tiled=True)
    part = jnp.sum(part, axis=0)
    for mask in (1, 2, 6):
        part = part + exchange(part, lambda z, x, core, y: (z ^ mask, x, core, y))
    half = lax.all_to_all(
        jnp.broadcast_to(part, (PLANE,) + part.shape), ("x", "y"), split_axis=0, concat_axis=0, tiled=True
    )
    return half, other_core(half)


def exact_dot(left, right, dims):
    return lax.dot_general(
        left, right, (dims, ((), ())), precision=lax.Precision.HIGHEST, preferred_element_type=jnp.float32
    )


def quick_dot(left, right, dims=((1,), (0,))):
    return lax.dot_general(left, right, (dims, ((), ())), preferred_element_type=jnp.float32)


def two_terms(value):
    high = value.astype(jnp.bfloat16)
    return high, (value - high.astype(jnp.float32)).astype(jnp.bfloat16)


def reciprocal(value):
    rough = pl.reciprocal(value, approx=True)
    return rough * (2.0 - value * rough)


def inverse_factor(gram):
    row = lax.broadcasted_iota(jnp.int32, (K, K), 0)
    column = lax.broadcasted_iota(jnp.int32, (K, K), 1)
    diagonal = jnp.where(row == column, gram, 0.0)
    across = lax.rsqrt(jnp.sum(diagonal, axis=0, keepdims=True))
    down = lax.rsqrt(jnp.sum(diagonal, axis=1, keepdims=True))
    scaled = gram * across * down
    groups = [scaled[8 * g : 8 * g + 8] for g in range(K // 8)]
    lane = lax.broadcasted_iota(jnp.int32, (8, K), 1)
    sub = lax.broadcasted_iota(jnp.int32, (8, K), 0)

    def spread(value, k):
        return jnp.broadcast_to(value[:, k : k + 1], (8, K))

    for g0 in range(K // 8):
        k = 8 * g0
        mine = groups[g0]
        columns = [spread(mine, k + t) for t in range(8)]
        s = {(i, j): jnp.broadcast_to(columns[j][i : i + 1], (8, K)) for i in range(8) for j in range(i + 1)}
        inside = (lane >= k) & (lane < k + 8)
        e = [
            jnp.where(inside, jnp.where(lane == k + t, 1.0, 0.0), jnp.broadcast_to(mine[t : t + 1], (8, K)))
            for t in range(8)
        ]
        u, v, done = [None] * 8, {}, [None] * 8
        for h in (0, 2, 4, 6):
            a, b, c = s[h, h], s[h + 1, h], s[h + 1, h + 1]
            turn = reciprocal(a * c - b * b)
            n0, n1 = c * e[h] - b * e[h + 1], a * e[h + 1] - b * e[h]
            root = lax.rsqrt(a)
            ratio = b * (root * root)
            done[h] = e[h] * root
            done[h + 1] = (e[h + 1] - ratio * e[h]) * lax.rsqrt(c - ratio * b)
            u[h], u[h + 1] = n0 * turn, n1 * turn
            m = {}
            for i in range(h + 2, 8):
                m[i] = (c * s[i, h] - b * s[i, h + 1], a * s[i, h + 1] - b * s[i, h])
                v[i, h] = (m[i][0] * turn, m[i][1] * turn)
                e[i] = e[i] - (s[i, h] * n0 + s[i, h + 1] * n1) * turn
                for j in range(h + 2, i + 1):
                    s[i, j] = s[i, j] - (s[i, h] * m[j][0] + s[i, h + 1] * m[j][1]) * turn
        for h in (4, 2, 0):
            for i in range(h + 2, 8):
                u[h] = u[h] - v[i, h][0] * u[i]
                u[h + 1] = u[h + 1] - v[i, h][1] * u[i]
        for g in range(g0 + 1, K // 8):
            value = jnp.where(inside, 0.0, groups[g])
            for t in (6, 4, 2, 0):
                value = value - (spread(groups[g], k + t) * u[t] + spread(groups[g], k + t + 1) * u[t + 1])
            groups[g] = value
        value = done[0]
        for t in range(1, 8):
            value = jnp.where(sub == t, done[t], value)
        groups[g0] = value
    full = jnp.concatenate(groups, axis=0)
    return jnp.where(row >= column, full, 0.0) * across


def three_term_gram(block):
    high, low = two_terms(block)
    rest = (block - high.astype(jnp.float32) - low.astype(jnp.float32)).astype(jnp.bfloat16)
    both = jnp.concatenate([high, low], axis=1)
    main = quick_dot(both, both, ((0,), (0,)))
    side = quick_dot(high, rest, ((0,), (0,)))
    return main[:K, :K] + (main[:K, K:] + main[K:, :K]) + (main[K:, K:] + side + side.T)


def apply_factor(inverse, terms):
    high, low = two_terms(inverse)
    left = jnp.concatenate(
        [jnp.concatenate([high, high], axis=1), jnp.concatenate([low, jnp.zeros_like(low)], axis=1)], axis=0
    )
    both = quick_dot(left, jnp.concatenate(two_terms(terms), axis=0))
    return both[:K] + both[K:]


def apply_everywhere(core, own, other, inverse, store):
    def step(n, _):
        for ref, start in ((own, core * HALF), (other, (1 - core) * HALF)):
            terms = jnp.concatenate([ref[2 * n, :K, :], ref[2 * n + 1, :K, :]], axis=1)
            store(pl.multiple_of(start + 2 * WIDE * n, 2 * WIDE), apply_factor(inverse, terms))
        return 0

    lax.fori_loop(0, PLANE // 2, step, 0)


def fetch(data, held, arrived):
    copies = [
        pltpu.make_async_copy(data.at[pl.ds(b * BLOCK, BLOCK)], held.at[pl.ds(b * BLOCK, BLOCK)], arrived.at[b])
        for b in range(STEPS)
    ]
    for copy in copies:
        copy.start()
    return copies


def make_message(core, held, tall, give, keep, turned):
    gram = three_term_gram(tall[...])
    for j in range(PLANE):
        rows = gram[THIN * j : THIN * (j + 1), :]
        give[j, K:, :] = rows
        keep[j, K:, :] = rows
    turned[...] = jnp.concatenate(two_terms(tall[...]), axis=1).T

    def step(n, _):
        for ref, start in ((give, (1 - core) * HALF), (keep, core * HALF)):
            columns = pl.ds(pl.multiple_of(start + COLUMNS * n, COLUMNS), COLUMNS)
            both = quick_dot(turned[...], held[:, columns])
            terms = both[:K] + both[K:]
            for i in range(COLUMNS // WIDE):
                ref[COLUMNS // WIDE * n + i, :K, :] = terms[:, WIDE * i : WIDE * (i + 1)]
        return 0

    lax.fori_loop(0, HALF // COLUMNS, step, 0)


def start_kernel(core, data, sketch, first, give, keep, held, weights, turned, arrived, ready):
    copies = fetch(data, held, arrived)
    get = pltpu.make_async_copy(sketch, weights, ready)
    get.start()
    get.wait()
    for b in range(STEPS):
        copies[b].wait()
        rows = pl.ds(b * BLOCK, BLOCK)
        first[rows, :] = quick_dot(held[rows, :], weights[...])
    make_message(core[0], held, first, give, keep, turned)


def factor_kernel(own, inverse):
    inverse[...] = inverse_factor(jnp.concatenate([own[j, K:, :] for j in range(PLANE)], axis=0))


def middle_kernel(core, own, other, inverse, data, second, give, keep, held, back, turned, arrived):
    copies = fetch(data, held, arrived)
    scaled = inverse[...] * (1.0 / ROOT_ROWS)

    def store(start, terms):
        back[:, pl.ds(start, 2 * WIDE)] = terms.astype(jnp.bfloat16)

    apply_everywhere(core[0], own, other, scaled, store)
    for b in range(STEPS):
        copies[b].wait()
        rows = pl.ds(b * BLOCK, BLOCK)
        second[rows, :] = quick_dot(held[rows, :], back[...], ((1,), (1,)))
    make_message(core[0], held, second, give, keep, turned)


def final_kernel(core, own, other, inverse, tall, projected, basis):
    scaled = inverse[...] * (D**0.5 / ROOT_ROWS)

    def store(start, terms):
        projected[:, pl.ds(start, 2 * WIDE)] = terms

    apply_everywhere(core[0], own, other, scaled, store)
    basis[...] = exact_dot(tall[...], inverse[...] * ROOT_ROWS, ((1,), (1,)))


def params():
    return pltpu.CompilerParams(vmem_limit_bytes=VMEM)


VM = pl.BlockSpec(memory_space=pltpu.VMEM)
SM = pl.BlockSpec(memory_space=pltpu.SMEM)
ANY = pl.BlockSpec(memory_space=pl.ANY)
MESSAGE = jax.ShapeDtypeStruct((PLANE, ROWS, K), jnp.float32)
SQUARE = jax.ShapeDtypeStruct((K, K), jnp.float32)


def start_call(core, data, sketch):
    rows = data.shape[0]
    return pl.pallas_call(
        start_kernel,
        out_shape=(jax.ShapeDtypeStruct((rows, K), jnp.float32), MESSAGE, MESSAGE),
        in_specs=[SM, ANY, ANY],
        out_specs=(VM, VM, VM),
        scratch_shapes=[
            pltpu.VMEM(data.shape, jnp.bfloat16),
            pltpu.VMEM(sketch.shape, jnp.bfloat16),
            pltpu.VMEM((2 * K, rows), jnp.bfloat16),
            pltpu.SemaphoreType.DMA((STEPS,)),
            pltpu.SemaphoreType.DMA,
        ],
        compiler_params=params(),
        name="start",
    )(core, data, sketch)


def factor_call(own):
    return pl.pallas_call(
        factor_kernel,
        out_shape=SQUARE,
        in_specs=[VM],
        out_specs=VM,
        compiler_params=params(),
        cost_estimate=pl.CostEstimate(flops=K**3, bytes_accessed=10**6, transcendentals=0),
        name="factor",
    )(own)


def middle_call(core, own, other, inverse, data):
    rows = data.shape[0]
    return pl.pallas_call(
        middle_kernel,
        out_shape=(jax.ShapeDtypeStruct((rows, K), jnp.float32), MESSAGE, MESSAGE),
        in_specs=[SM, VM, VM, VM, ANY],
        out_specs=(VM, VM, VM),
        scratch_shapes=[
            pltpu.VMEM(data.shape, jnp.bfloat16),
            pltpu.VMEM((K, D), jnp.bfloat16),
            pltpu.VMEM((2 * K, rows), jnp.bfloat16),
            pltpu.SemaphoreType.DMA((STEPS,)),
        ],
        compiler_params=params(),
        name="middle",
    )(core, own, other, inverse, data)


def final_call(core, own, other, inverse, tall):
    return pl.pallas_call(
        final_kernel,
        out_shape=(jax.ShapeDtypeStruct((K, D), jnp.float32), jax.ShapeDtypeStruct(tall.shape, jnp.float32)),
        in_specs=[SM, VM, VM, VM, VM],
        out_specs=(VM, VM),
        compiler_params=params(),
        name="final",
    )(core, own, other, inverse, tall)


def on_device(data, sketch):
    core = lax.axis_index("core").astype(jnp.int32).reshape(1)
    first, give, keep = start_call(core, data, sketch)
    own, other = sum_everywhere(give, keep)
    inverse = factor_call(own)
    second, give, keep = middle_call(core, own, other, inverse, data)
    first_basis = exact_dot(first, ROOT_ROWS * inverse, ((1,), (1,)))
    own, other = sum_everywhere(give, keep)
    inverse = factor_call(own)
    projected, basis = final_call(core, own, other, inverse, second)
    return (first_basis, basis, projected)


def solution(mesh):
    split = Mesh(mesh.devices.reshape(Z, X, C, Y), AXES)
    return jax.shard_map(
        on_device,
        mesh=split,
        in_specs=(P(AXES, None), P()),
        out_specs=(P(AXES, None), P(AXES, None), P()),
        check_vma=False,
    )
```

time: 167 us -> 157 us (0.940)
  Pallas kernels: 34.8 us -> 29.7 us
  waiting for transfers between devices: 21.4 us -> 16.9 us
    pallas_call x3 -> x5, Pallas kernels: 34.8 us -> 29.7 us  [the longest x1 9.98 us: middle_call(): pl.pallas_call(middle_kernel, out_shape=(jax.ShapeDtypeStruct((rows, K),...]
    ppermute x10, waiting for transfers between devices: 21.4 us -> 16.9 us  [exchange(): return lax.ppermute(value, AXES, pairs)]
  transfers between devices with their start and end apart: 10 -> 10, of which waited for: 10 -> 8; matrix products, arithmetic and copies ran while one was open for 1% -> 1% of each run, Pallas kernels for 0% -> 5%
where the time goes in v1:
time: 157 us
  blocking collectives  74.8 us (48%)
  starting transfers between devices  31.6 us (20%)
  Pallas kernels  29.7 us (19%)
  waiting for transfers between devices  16.9 us (11%)
    all_to_all x2, blocking collectives, sum_everywhere(): lax.all_to_all(half, ('x', 'y'), split_axis=0, concat_axis=0, tiled=True)  42.2 us
    all_to_all x2, blocking collectives, sum_everywhere(): lax.all_to_all(jnp.broadcast_to(part, (PLANE,) + part.shape), ('x', 'y'),...  32.6 us
    ppermute x10, starting transfers between devices, exchange(): return lax.ppermute(value, AXES, pairs)  31.6 us
    ppermute x10, waiting for transfers between devices, exchange(): return lax.ppermute(value, AXES, pairs)  16.9 us
    pallas_call x1, Pallas kernels, middle_call(): pl.pallas_call(middle_kernel, out_shape=(jax.ShapeDtypeStruct((rows, K),...  9.98 us
    pallas_call x2, Pallas kernels, factor_call(): pl.pallas_call(factor_kernel, out_shape=SQUARE, in_specs=[VM], out_specs=...  8.5 us
    pallas_call x1, Pallas kernels, start_call(): pl.pallas_call(start_kernel, out_shape=(jax.ShapeDtypeStruct((rows, K), j...  7.66 us
    pallas_call x1, Pallas kernels, final_call(): pl.pallas_call(final_kernel, out_shape=(jax.ShapeDtypeStruct((K, D), jnp....  3.58 us
  transfers between devices with their start and end apart: 10, of which 8 were waited for; matrix products, arithmetic and copies ran while one was open for 1% of the time, Pallas kernels for 5%

profile of v1, /device:TPU:1, one launch (start us, length us, event | category | flops | bytes accessed | tf_op | source)
XLA Modules:
  0.0 156.8 jit_solution(5607134554362522140)
XLA Ops:
  0.6 0.0 copy-start
  0.6 1.2 copy-done
  1.9 7.7 %start.1 = (f32[1024,128]{1,0:T(8,128)S(1)}, f32[16,136,128]{2,1,0:T(8,128)S(1)}, f32[16,136,128]{2,1,0:T(8,128)S(1)}) custom-call(s32[1]{0:T(128)} %bitcast.core, bf16[1024,4096]{1,0:T(8,128)(2,1)} %data.3, bf16[4096,128]{1,0:T(8,128)(2,1)S(1)} %copy-done), custom_call_target="tpu_custom_call" | custom-call | tf_op jit(solution)/shard_map/start/pallas_call | solution.py:244
  9.5 3.3 %collective-permute-start = (f32[16,136,128]{2,1,0:T(8,128)S(1)}, f32[16,136,128]{2,1,0:T(8,128)S(1)}, u32[]{:S(2)}, u32[]{:S(2)}) collective-permute-start(f32[16,136,128]{2,1,0:T(8,128)S(1)} %get-tuple-element.13), channel_id=1, source_target_pairs={{0,4},{1,5},{2,6},{3,7},{4,0},{5,1},{6,2},{7,3},{8,12},{9,13},{10,... | collective-permute-start | bytes 3342344 | tf_op jit(solution)/shard_map/ppermute | solution.py:35
  12.9 2.4 %collective-permute-done = f32[16,136,128]{2,1,0:T(8,128)S(1)} collective-permute-done((f32[16,136,128]{2,1,0:T(8,128)S(1)}, f32[16,136,128]{2,1,0:T(8,128)S(1)}, u32[]{:S(2)}, u32[]{:S(2)}) %collective-permute-start) | collective-permute-done | bytes 1114144 | tf_op jit(solution)/shard_map/ppermute | solution.py:35
  15.2 0.1 add.24
  15.4 21.9 %all_to_all.20 = f32[16,136,128]{2,1,0:T(8,128)S(1)} all-to-all(f32[16,136,128]{2,1,0:T(8,128)S(1)} %add.24), channel_id=1, replica_groups=mesh['z'=8,'x'=4,'core'=2,'y'=4] {'x','y'}, dimensions={0} | all-to-all | bytes 2228224 | tf_op jit(solution)/shard_map/all_to_all | solution.py:44
  37.3 0.1 reduce_sum.18
  37.4 1.7 %collective-permute-start.1 = (f32[136,128]{1,0:T(8,128)S(1)}, f32[136,128]{1,0:T(8,128)S(1)}, u32[]{:S(2)}, u32[]{:S(2)}) collective-permute-start(f32[136,128]{1,0:T(8,128)S(1)} %reduce_sum.18), channel_id=1, source_target_pairs={{0,32},{1,33},{2,34},{3,35},{4,36},{5,37},{6,38},{7,39},{8,40},{9,... | collective-permute-start | bytes 208904 | tf_op jit(solution)/shard_map/ppermute | solution.py:35
  39.1 1.7 %collective-permute-done.1 = f32[136,128]{1,0:T(8,128)S(1)} collective-permute-done((f32[136,128]{1,0:T(8,128)S(1)}, f32[136,128]{1,0:T(8,128)S(1)}, u32[]{:S(2)}, u32[]{:S(2)}) %collective-permute-start.1) | collective-permute-done | bytes 69664 | tf_op jit(solution)/shard_map/ppermute | solution.py:35
  40.8 3.1 %collective-permute-start.2 = (f32[136,128]{1,0:T(8,128)S(1)}, f32[136,128]{1,0:T(8,128)S(1)}, u32[]{:S(2)}, u32[]{:S(2)}) collective-permute-start(f32[136,128]{1,0:T(8,128)S(1)} %add.25), channel_id=1, source_target_pairs={{0,64},{1,65},{2,66},{3,67},{4,68},{5,69},{6,70},{7,71},{8,72},{9,... | collective-permute-start | bytes 208904 | tf_op jit(solution)/shard_map/ppermute | solution.py:35
  43.9 1.7 %collective-permute-done.2 = f32[136,128]{1,0:T(8,128)S(1)} collective-permute-done((f32[136,128]{1,0:T(8,128)S(1)}, f32[136,128]{1,0:T(8,128)S(1)}, u32[]{:S(2)}, u32[]{:S(2)}) %collective-permute-start.2) | collective-permute-done | bytes 69664 | tf_op jit(solution)/shard_map/ppermute | solution.py:35
  45.6 5.4 %collective-permute-start.3 = (f32[136,128]{1,0:T(8,128)S(1)}, f32[136,128]{1,0:T(8,128)S(1)}, u32[]{:S(2)}, u32[]{:S(2)}) collective-permute-start(f32[136,128]{1,0:T(8,128)S(1)} %add.26), channel_id=1, source_target_pairs={{0,192},{1,193},{2,194},{3,195},{4,196},{5,197},{6,198},{7,199},{8... | collective-permute-start | bytes 208904 | tf_op jit(solution)/shard_map/ppermute | solution.py:35
  51.0 1.8 %collective-permute-done.3 = f32[136,128]{1,0:T(8,128)S(1)} collective-permute-done((f32[136,128]{1,0:T(8,128)S(1)}, f32[136,128]{1,0:T(8,128)S(1)}, u32[]{:S(2)}, u32[]{:S(2)}) %collective-permute-start.3) | collective-permute-done | bytes 69664 | tf_op jit(solution)/shard_map/ppermute | solution.py:35
  52.8 0.1 broadcast_in_dim.6
  52.8 16.9 %all_to_all.21.own = f32[16,136,128]{2,1,0:T(8,128)S(1)} all-to-all(f32[16,136,128]{2,1,0:T(8,128)S(1)} %broadcast_in_dim.6), channel_id=1, replica_groups=mesh['z'=8,'x'=4,'core'=2,'y'=4] {'x','y'}, dimensions={0} | all-to-all | bytes 2228224 | tf_op jit(solution)/shard_map/all_to_all | solution.py:48
  69.7 5.5 %collective-permute-start.4 = (f32[16,136,128]{2,1,0:T(8,128)S(1)}, f32[16,136,128]{2,1,0:T(8,128)S(1)}, u32[]{:S(2)}, u32[]{:S(2)}) collective-permute-start(f32[16,136,128]{2,1,0:T(8,128)S(1)} %all_to_all.21.own), channel_id=1, source_target_pairs={{0,4},{1,5},{2,6},{3,7},{4,0},{5,1},{6,2},{7,3},{8,12},{9,13},{10,... | collective-permute-start | bytes 3342344 | tf_op jit(solution)/shard_map/ppermute | solution.py:35
  75.2 4.3 %factor.2.inverse = f32[128,128]{1,0:T(8,128)S(1)} custom-call(f32[16,136,128]{2,1,0:T(8,128)S(1)} %all_to_all.21.own), custom_call_target="tpu_custom_call" | custom-call | flops 2097152 | bytes 1000000 | tf_op jit(solution)/shard_map/factor/pallas_call | solution.py:262
  79.5 0.0 collective-permute-done.4.other
  79.5 10.0 %middle.1 = (f32[1024,128]{1,0:T(8,128)S(1)}, f32[16,136,128]{2,1,0:T(8,128)S(1)}, f32[16,136,128]{2,1,0:T(8,128)S(1)}) custom-call(s32[1]{0:T(128)} %bitcast.core, f32[16,136,128]{2,1,0:T(8,128)S(1)} %all_to_all.21.own, f32[16,136,128]{2,1,0:T(8,128)S(1)} %collective-permute-done.4.other, f32[128,128]{1,0:T(8,128)S(1)} %factor.2.inverse, ...), custom_call_target="tpu_custom_call" | custom-call | tf_op jit(solution)/shard_map/middle/pallas_call | solution.py:275
  89.5 0.1 collective-permute-start.5
  89.6 2.7 %collective-permute-done.5 = f32[16,136,128]{2,1,0:T(8,128)S(1)} collective-permute-done((f32[16,136,128]{2,1,0:T(8,128)S(1)}, f32[16,136,128]{2,1,0:T(8,128)S(1)}, u32[]{:S(2)}, u32[]{:S(2)}) %collective-permute-start.5) | collective-permute-done | bytes 1114144 | tf_op jit(solution)/shard_map/ppermute | solution.py:35
  92.3 0.1 add.28
  92.4 20.3 %all_to_all.22 = f32[16,136,128]{2,1,0:T(8,128)S(1)} all-to-all(f32[16,136,128]{2,1,0:T(8,128)S(1)} %add.28), channel_id=1, replica_groups=mesh['z'=8,'x'=4,'core'=2,'y'=4] {'x','y'}, dimensions={0} | all-to-all | bytes 2228224 | tf_op jit(solution)/shard_map/all_to_all | solution.py:44
  112.7 0.1 reduce_sum.19
  112.7 1.5 collective-permute-start.6
  114.2 1.8 %collective-permute-done.6 = f32[136,128]{1,0:T(8,128)S(1)} collective-permute-done((f32[136,128]{1,0:T(8,128)S(1)}, f32[136,128]{1,0:T(8,128)S(1)}, u32[]{:S(2)}, u32[]{:S(2)}) %collective-permute-start.6) | collective-permute-done | bytes 69664 | tf_op jit(solution)/shard_map/ppermute | solution.py:35
  116.0 1.6 %collective-permute-start.7 = (f32[136,128]{1,0:T(8,128)S(1)}, f32[136,128]{1,0:T(8,128)S(1)}, u32[]{:S(2)}, u32[]{:S(2)}) collective-permute-start(f32[136,128]{1,0:T(8,128)S(1)} %add.29), channel_id=1, source_target_pairs={{0,64},{1,65},{2,66},{3,67},{4,68},{5,69},{6,70},{7,71},{8,72},{9,... | collective-permute-start | bytes 208904 | tf_op jit(solution)/shard_map/ppermute | solution.py:35
  117.6 2.6 %collective-permute-done.7 = f32[136,128]{1,0:T(8,128)S(1)} collective-permute-done((f32[136,128]{1,0:T(8,128)S(1)}, f32[136,128]{1,0:T(8,128)S(1)}, u32[]{:S(2)}, u32[]{:S(2)}) %collective-permute-start.7) | collective-permute-done | bytes 69664 | tf_op jit(solution)/shard_map/ppermute | solution.py:35
  120.2 3.2 %collective-permute-start.8 = (f32[136,128]{1,0:T(8,128)S(1)}, f32[136,128]{1,0:T(8,128)S(1)}, u32[]{:S(2)}, u32[]{:S(2)}) collective-permute-start(f32[136,128]{1,0:T(8,128)S(1)} %add.30), channel_id=1, source_target_pairs={{0,192},{1,193},{2,194},{3,195},{4,196},{5,197},{6,198},{7,199},{8... | collective-permute-start | bytes 208904 | tf_op jit(solution)/shard_map/ppermute | solution.py:35
  123.3 2.2 %collective-permute-done.8 = f32[136,128]{1,0:T(8,128)S(1)} collective-permute-done((f32[136,128]{1,0:T(8,128)S(1)}, f32[136,128]{1,0:T(8,128)S(1)}, u32[]{:S(2)}, u32[]{:S(2)}) %collective-permute-start.8) | collective-permute-done | bytes 69664 | tf_op jit(solution)/shard_map/ppermute | solution.py:35
  125.6 0.1 broadcast_in_dim.7
  125.7 15.7 %all_to_all.23.own = f32[16,136,128]{2,1,0:T(8,128)S(1)} all-to-all(f32[16,136,128]{2,1,0:T(8,128)S(1)} %broadcast_in_dim.7), channel_id=1, replica_groups=mesh['z'=8,'x'=4,'core'=2,'y'=4] {'x','y'}, dimensions={0} | all-to-all | bytes 2228224 | tf_op jit(solution)/shard_map/all_to_all | solution.py:48
  141.4 6.3 %collective-permute-start.9 = (f32[16,136,128]{2,1,0:T(8,128)S(1)}, f32[16,136,128]{2,1,0:T(8,128)S(1)}, u32[]{:S(2)}, u32[]{:S(2)}) collective-permute-start(f32[16,136,128]{2,1,0:T(8,128)S(1)} %all_to_all.23.own), channel_id=1, source_target_pairs={{0,4},{1,5},{2,6},{3,7},{4,0},{5,1},{6,2},{7,3},{8,12},{9,13},{10,... | collective-permute-start | bytes 3342344 | tf_op jit(solution)/shard_map/ppermute | solution.py:35
  147.6 1.4 fusion
  149.0 4.3 %factor.3.inverse = f32[128,128]{1,0:T(8,128)S(1)} custom-call(f32[16,136,128]{2,1,0:T(8,128)S(1)} %all_to_all.23.own), custom_call_target="tpu_custom_call" | custom-call | flops 2097152 | bytes 1000000 | tf_op jit(solution)/shard_map/factor/pallas_call | solution.py:262
  153.2 0.0 collective-permute-done.9.other
  153.3 3.6 %final.1 = (f32[128,4096]{1,0:T(8,128)}, f32[1024,128]{1,0:T(8,128)}) custom-call(s32[1]{0:T(128)} %bitcast.core, f32[16,136,128]{2,1,0:T(8,128)S(1)} %all_to_all.23.own, f32[16,136,128]{2,1,0:T(8,128)S(1)} %collective-permute-done.9.other, f32[128,128]{1,0:T(8,128)S(1)} %factor.3.inverse, f32[1024,128]{1,0:T(8,128)S(1)} %get-tuple-element.16.tall), custom_call_target="tpu_custom_call" | custom-call | tf_op jit(solution)/shard_map/final/pallas_call | solution.py:292
  (6 shorter events, 0.1 us)
Async XLA Ops:
  0.6 1.2 copy-start
  9.5 5.7 %collective-permute-start = (f32[16,136,128]{2,1,0:T(8,128)S(1)}, f32[16,136,128]{2,1,0:T(8,128)S(1)}, u32[]{:S(2)}, u32[]{:S(2)}) collective-permute-start(f32[16,136,128]{2,1,0:T(8,128)S(1)} %get-tuple-element.13), channel_id=1, source_target_pairs={{0,4},{1,5},{2,6},{3,7},{4,0},{5,1},{6,2},{7,3},{8,12},{9,13},{10,... | collective-permute-start | bytes 3342344 | tf_op jit(solution)/shard_map/ppermute | solution.py:35
  37.4 3.4 %collective-permute-start.1 = (f32[136,128]{1,0:T(8,128)S(1)}, f32[136,128]{1,0:T(8,128)S(1)}, u32[]{:S(2)}, u32[]{:S(2)}) collective-permute-start(f32[136,128]{1,0:T(8,128)S(1)} %reduce_sum.18), channel_id=1, source_target_pairs={{0,32},{1,33},{2,34},{3,35},{4,36},{5,37},{6,38},{7,39},{8,40},{9,... | collective-permute-start | bytes 208904 | tf_op jit(solution)/shard_map/ppermute | solution.py:35
  40.8 4.8 %collective-permute-start.2 = (f32[136,128]{1,0:T(8,128)S(1)}, f32[136,128]{1,0:T(8,128)S(1)}, u32[]{:S(2)}, u32[]{:S(2)}) collective-permute-start(f32[136,128]{1,0:T(8,128)S(1)} %add.25), channel_id=1, source_target_pairs={{0,64},{1,65},{2,66},{3,67},{4,68},{5,69},{6,70},{7,71},{8,72},{9,... | collective-permute-start | bytes 208904 | tf_op jit(solution)/shard_map/ppermute | solution.py:35
  45.6 7.1 %collective-permute-start.3 = (f32[136,128]{1,0:T(8,128)S(1)}, f32[136,128]{1,0:T(8,128)S(1)}, u32[]{:S(2)}, u32[]{:S(2)}) collective-permute-start(f32[136,128]{1,0:T(8,128)S(1)} %add.26), channel_id=1, source_target_pairs={{0,192},{1,193},{2,194},{3,195},{4,196},{5,197},{6,198},{7,199},{8... | collective-permute-start | bytes 208904 | tf_op jit(solution)/shard_map/ppermute | solution.py:35
  69.7 9.7 %collective-permute-start.4 = (f32[16,136,128]{2,1,0:T(8,128)S(1)}, f32[16,136,128]{2,1,0:T(8,128)S(1)}, u32[]{:S(2)}, u32[]{:S(2)}) collective-permute-start(f32[16,136,128]{2,1,0:T(8,128)S(1)} %all_to_all.21.own), channel_id=1, source_target_pairs={{0,4},{1,5},{2,6},{3,7},{4,0},{5,1},{6,2},{7,3},{8,12},{9,13},{10,... | collective-permute-start | bytes 3342344 | tf_op jit(solution)/shard_map/ppermute | solution.py:35
  89.5 2.8 %collective-permute-start.5 = (f32[16,136,128]{2,1,0:T(8,128)S(1)}, f32[16,136,128]{2,1,0:T(8,128)S(1)}, u32[]{:S(2)}, u32[]{:S(2)}) collective-permute-start(f32[16,136,128]{2,1,0:T(8,128)S(1)} %get-tuple-element.15), channel_id=1, source_target_pairs={{0,4},{1,5},{2,6},{3,7},{4,0},{5,1},{6,2},{7,3},{8,12},{9,13},{10,... | collective-permute-start | bytes 3342344 | tf_op jit(solution)/shard_map/ppermute | solution.py:35
  112.7 3.2 %collective-permute-start.6 = (f32[136,128]{1,0:T(8,128)S(1)}, f32[136,128]{1,0:T(8,128)S(1)}, u32[]{:S(2)}, u32[]{:S(2)}) collective-permute-start(f32[136,128]{1,0:T(8,128)S(1)} %reduce_sum.19), channel_id=1, source_target_pairs={{0,32},{1,33},{2,34},{3,35},{4,36},{5,37},{6,38},{7,39},{8,40},{9,... | collective-permute-start | bytes 208904 | tf_op jit(solution)/shard_map/ppermute | solution.py:35
  116.0 4.1 %collective-permute-start.7 = (f32[136,128]{1,0:T(8,128)S(1)}, f32[136,128]{1,0:T(8,128)S(1)}, u32[]{:S(2)}, u32[]{:S(2)}) collective-permute-start(f32[136,128]{1,0:T(8,128)S(1)} %add.29), channel_id=1, source_target_pairs={{0,64},{1,65},{2,66},{3,67},{4,68},{5,69},{6,70},{7,71},{8,72},{9,... | collective-permute-start | bytes 208904 | tf_op jit(solution)/shard_map/ppermute | solution.py:35
  120.2 5.4 %collective-permute-start.8 = (f32[136,128]{1,0:T(8,128)S(1)}, f32[136,128]{1,0:T(8,128)S(1)}, u32[]{:S(2)}, u32[]{:S(2)}) collective-permute-start(f32[136,128]{1,0:T(8,128)S(1)} %add.30), channel_id=1, source_target_pairs={{0,192},{1,193},{2,194},{3,195},{4,196},{5,197},{6,198},{7,199},{8... | collective-permute-start | bytes 208904 | tf_op jit(solution)/shard_map/ppermute | solution.py:35
  141.4 11.9 %collective-permute-start.9 = (f32[16,136,128]{2,1,0:T(8,128)S(1)}, f32[16,136,128]{2,1,0:T(8,128)S(1)}, u32[]{:S(2)}, u32[]{:S(2)}) collective-permute-start(f32[16,136,128]{2,1,0:T(8,128)S(1)} %all_to_all.23.own), channel_id=1, source_target_pairs={{0,4},{1,5},{2,6},{3,7},{4,0},{5,1},{6,2},{7,3},{8,12},{9,13},{10,... | collective-permute-start | bytes 3342344 | tf_op jit(solution)/shard_map/ppermute | solution.py:35

commit v2 on v1

--- a/solution.py
+++ b/solution.py
@@ -16,9 +16,7 @@
 ROWS = K + THIN
 ROOT_ROWS = 512.0
 BLOCK = 256
-COLUMNS = 512
 STEPS = 4
-VMEM = 48 * 2**20
 
 
 def device_number(z, x, core, y):
@@ -39,16 +37,28 @@
     return exchange(value, lambda z, x, core, y: (z, x, 1 - core, y))
 
 
-def sum_everywhere(give, keep):
+def plane_partner(mask, first):
+    def partner(z, x, core, y):
+        return (z, x, core, y ^ mask) if (core == 0) == first else (z, x ^ mask, core, y)
+
+    return partner
+
+
+def sum_everywhere(give, keep, beside=()):
     half = keep + other_core(give)
-    part = lax.all_to_all(half, ("x", "y"), split_axis=0, concat_axis=0, tiled=True)
-    part = jnp.sum(part, axis=0)
-    for mask in (1, 2, 6):
-        part = part + exchange(part, lambda z, x, core, y: (z ^ mask, x, core, y))
-    half = lax.all_to_all(
+    for first in (True, False):
+        half = half.reshape((4, -1) + half.shape[1:])
+        arrived = [exchange(half[mask], plane_partner(mask, first)) for mask in (2, 1, 3)]
+        half = half[0] + arrived[0] + arrived[1] + arrived[2]
+    part = half[0]
+    arrived = [exchange(part, lambda z, x, core, y: (z ^ mask, x, core, y)) for mask in (3, 2, 1)]
+    arrived, beside = lax.optimization_barrier((arrived, beside))
+    part = part + arrived[0] + arrived[1] + arrived[2]
+    part = part + exchange(part, lambda z, x, core, y: (z ^ 6, x, core, y))
+    own = lax.all_to_all(
         jnp.broadcast_to(part, (PLANE,) + part.shape), ("x", "y"), split_axis=0, concat_axis=0, tiled=True
     )
-    return half, other_core(half)
+    return own, other_core(own), beside
 
 
 def exact_dot(left, right, dims):
@@ -148,13 +158,10 @@
 
 
 def apply_everywhere(core, own, other, inverse, store):
-    def step(n, _):
+    for n in range(PLANE // 2):
         for ref, start in ((own, core * HALF), (other, (1 - core) * HALF)):
             terms = jnp.concatenate([ref[2 * n, :K, :], ref[2 * n + 1, :K, :]], axis=1)
             store(pl.multiple_of(start + 2 * WIDE * n, 2 * WIDE), apply_factor(inverse, terms))
-        return 0
-
-    lax.fori_loop(0, PLANE // 2, step, 0)
 
 
 def fetch(data, held, arrived):
@@ -167,44 +174,42 @@
     return copies
 
 
-def make_message(core, held, tall, give, keep, turned):
+def make_message(place, held, tall, give, keep, turned):
+    core, x, y = place
+    sides = ((give, 1 - core), (keep, core))
+
+    def slot(side, at_x, at_y):
+        over_x, over_y = at_x ^ x, at_y ^ y
+        return jnp.where(side == 0, 4 * over_y + over_x, 4 * over_x + over_y)
+
     gram = three_term_gram(tall[...])
     for j in range(PLANE):
-        rows = gram[THIN * j : THIN * (j + 1), :]
-        give[j, K:, :] = rows
-        keep[j, K:, :] = rows
+        for ref, side in sides:
+            ref[slot(side, j // Y, j % Y), K:, :] = gram[THIN * j : THIN * (j + 1), :]
     turned[...] = jnp.concatenate(two_terms(tall[...]), axis=1).T
-
-    def step(n, _):
-        for ref, start in ((give, (1 - core) * HALF), (keep, core * HALF)):
-            columns = pl.ds(pl.multiple_of(start + COLUMNS * n, COLUMNS), COLUMNS)
+    for n in range(X):
+        for ref, side in sides:
+            columns = pl.ds(pl.multiple_of(side * HALF + Y * WIDE * n, Y * WIDE), Y * WIDE)
             both = quick_dot(turned[...], held[:, columns])
             terms = both[:K] + both[K:]
-            for i in range(COLUMNS // WIDE):
-                ref[COLUMNS // WIDE * n + i, :K, :] = terms[:, WIDE * i : WIDE * (i + 1)]
-        return 0
-
-    lax.fori_loop(0, HALF // COLUMNS, step, 0)
-
-
-def start_kernel(core, data, sketch, first, give, keep, held, weights, turned, arrived, ready):
+            for i in range(Y):
+                ref[slot(side, n, i), :K, :] = terms[:, WIDE * i : WIDE * (i + 1)]
+
+
+def start_kernel(core, x, y, data, sketch, first, give, keep, held, turned, arrived):
     copies = fetch(data, held, arrived)
-    get = pltpu.make_async_copy(sketch, weights, ready)
-    get.start()
-    get.wait()
     for b in range(STEPS):
         copies[b].wait()
         rows = pl.ds(b * BLOCK, BLOCK)
-        first[rows, :] = quick_dot(held[rows, :], weights[...])
-    make_message(core[0], held, first, give, keep, turned)
+        first[rows, :] = quick_dot(held[rows, :], sketch[...])
+    make_message((core[0], x[0], y[0]), held, first, give, keep, turned)
 
 
 def factor_kernel(own, inverse):
     inverse[...] = inverse_factor(jnp.concatenate([own[j, K:, :] for j in range(PLANE)], axis=0))
 
 
-def middle_kernel(core, own, other, inverse, data, second, give, keep, held, back, turned, arrived):
-    copies = fetch(data, held, arrived)
+def middle_kernel(core, x, y, own, other, inverse, held, second, give, keep, back, turned):
     scaled = inverse[...] * (1.0 / ROOT_ROWS)
 
     def store(start, terms):
@@ -212,24 +217,29 @@
 
     apply_everywhere(core[0], own, other, scaled, store)
     for b in range(STEPS):
-        copies[b].wait()
         rows = pl.ds(b * BLOCK, BLOCK)
         second[rows, :] = quick_dot(held[rows, :], back[...], ((1,), (1,)))
-    make_message(core[0], held, second, give, keep, turned)
-
-
-def final_kernel(core, own, other, inverse, tall, projected, basis):
+    make_message((core[0], x[0], y[0]), held, second, give, keep, turned)
+
+
+def final_kernel(core, x, y, own, other, inverse, tall, projected, basis, wide, narrow, sent):
     scaled = inverse[...] * (D**0.5 / ROOT_ROWS)
 
     def store(start, terms):
-        projected[:, pl.ds(start, 2 * WIDE)] = terms
+        wide[:, pl.ds(start, 2 * WIDE)] = terms
 
     apply_everywhere(core[0], own, other, scaled, store)
-    basis[...] = exact_dot(tall[...], inverse[...] * ROOT_ROWS, ((1,), (1,)))
-
-
-def params():
-    return pltpu.CompilerParams(vmem_limit_bytes=VMEM)
+    one = pltpu.make_async_copy(wide, projected, sent.at[0])
+    one.start()
+    narrow[...] = exact_dot(tall[...], inverse[...] * ROOT_ROWS, ((1,), (1,)))
+    two = pltpu.make_async_copy(narrow, basis, sent.at[1])
+    two.start()
+    one.wait()
+    two.wait()
+
+
+def params(mebibytes=32):
+    return pltpu.CompilerParams(vmem_limit_bytes=mebibytes * 2**20)
 
 
 VM = pl.BlockSpec(memory_space=pltpu.VMEM)
@@ -239,23 +249,21 @@
 SQUARE = jax.ShapeDtypeStruct((K, K), jnp.float32)
 
 
-def start_call(core, data, sketch):
+def start_call(place, data, sketch):
     rows = data.shape[0]
     return pl.pallas_call(
         start_kernel,
         out_shape=(jax.ShapeDtypeStruct((rows, K), jnp.float32), MESSAGE, MESSAGE),
-        in_specs=[SM, ANY, ANY],
+        in_specs=[SM, SM, SM, ANY, VM],
         out_specs=(VM, VM, VM),
         scratch_shapes=[
             pltpu.VMEM(data.shape, jnp.bfloat16),
-            pltpu.VMEM(sketch.shape, jnp.bfloat16),
             pltpu.VMEM((2 * K, rows), jnp.bfloat16),
             pltpu.SemaphoreType.DMA((STEPS,)),
-            pltpu.SemaphoreType.DMA,
         ],
-        compiler_params=params(),
+        compiler_params=params(48),
         name="start",
-    )(core, data, sketch)
+    )(*place, data, sketch)
 
 
 def factor_call(own):
@@ -270,45 +278,45 @@
     )(own)
 
 
-def middle_call(core, own, other, inverse, data):
-    rows = data.shape[0]
+def middle_call(place, own, other, inverse, held):
+    rows = held.shape[0]
     return pl.pallas_call(
         middle_kernel,
         out_shape=(jax.ShapeDtypeStruct((rows, K), jnp.float32), MESSAGE, MESSAGE),
-        in_specs=[SM, VM, VM, VM, ANY],
+        in_specs=[SM, SM, SM, VM, VM, VM, VM],
         out_specs=(VM, VM, VM),
-        scratch_shapes=[
-            pltpu.VMEM(data.shape, jnp.bfloat16),
-            pltpu.VMEM((K, D), jnp.bfloat16),
-            pltpu.VMEM((2 * K, rows), jnp.bfloat16),
-            pltpu.SemaphoreType.DMA((STEPS,)),
-        ],
+        scratch_shapes=[pltpu.VMEM((K, D), jnp.bfloat16), pltpu.VMEM((2 * K, rows), jnp.bfloat16)],
         compiler_params=params(),
         name="middle",
-    )(core, own, other, inverse, data)
-
-
-def final_call(core, own, other, inverse, tall):
+    )(*place, own, other, inverse, held)
+
+
+def final_call(place, own, other, inverse, tall):
     return pl.pallas_call(
         final_kernel,
         out_shape=(jax.ShapeDtypeStruct((K, D), jnp.float32), jax.ShapeDtypeStruct(tall.shape, jnp.float32)),
-        in_specs=[SM, VM, VM, VM, VM],
-        out_specs=(VM, VM),
+        in_specs=[SM, SM, SM, VM, VM, VM, VM],
+        out_specs=(ANY, ANY),
+        scratch_shapes=[
+            pltpu.VMEM((K, D), jnp.float32),
+            pltpu.VMEM(tall.shape, jnp.float32),
+            pltpu.SemaphoreType.DMA((2,)),
+        ],
         compiler_params=params(),
         name="final",
-    )(core, own, other, inverse, tall)
+    )(*place, own, other, inverse, tall)
 
 
 def on_device(data, sketch):
-    core = lax.axis_index("core").astype(jnp.int32).reshape(1)
-    first, give, keep = start_call(core, data, sketch)
-    own, other = sum_everywhere(give, keep)
+    place = [lax.axis_index(axis).astype(jnp.int32).reshape(1) for axis in ("core", "x", "y")]
+    first, give, keep = start_call(place, data, sketch)
+    own, other, _ = sum_everywhere(give, keep)
     inverse = factor_call(own)
-    second, give, keep = middle_call(core, own, other, inverse, data)
+    second, give, keep = middle_call(place, own, other, inverse, data)
     first_basis = exact_dot(first, ROOT_ROWS * inverse, ((1,), (1,)))
-    own, other = sum_everywhere(give, keep)
+    own, other, first_basis = sum_everywhere(give, keep, first_basis)
     inverse = factor_call(own)
-    projected, basis = final_call(core, own, other, inverse, second)
+    projected, basis = final_call(place, own, other, inverse, second)
     return (first_basis, basis, projected)
 
 

time: 157 us -> 142 us (0.904)
  blocking collectives: 74.8 us -> 34.6 us
  waiting for transfers between devices: 16.9 us -> 40.6 us
  starting transfers between devices: 31.6 us -> 38.8 us
  Pallas kernels: 29.7 us -> 23.6 us
    all_to_all x2 -> x0, blocking collectives: 42.2 us -> none  [sum_everywhere(): lax.all_to_all(half, ('x', 'y'), split_axis=0, concat_axis=0, tiled=True)]
    ppermute x10 -> x24, waiting for transfers between devices: 16.9 us -> 40.6 us  [exchange(): return lax.ppermute(value, AXES, pairs)]
    ppermute x10 -> x24, starting transfers between devices: 31.6 us -> 38.8 us  [exchange(): return lax.ppermute(value, AXES, pairs)]
    pallas_call x1, Pallas kernels: 9.98 us -> 5.65 us  [middle_call(): pl.pallas_call(middle_kernel, out_shape=(jax.ShapeDtypeStruct((rows, K),...]
    all_to_all x2, blocking collectives: 32.6 us -> 34.6 us  [sum_everywhere(): lax.all_to_all(jnp.broadcast_to(part, (PLANE,) + part.shape), ('x', 'y'),...]
  transfers between devices with their start and end apart: 10 -> 24, of which waited for: 8 -> 16; matrix products, arithmetic and copies ran while one was open for 1% -> 1% of each run, Pallas kernels for 5% -> 6%
where the time goes in v2:
time: 142 us
  waiting for transfers between devices  40.6 us (29%)
  starting transfers between devices  38.8 us (27%)
  blocking collectives  34.6 us (24%)
  Pallas kernels  23.6 us (17%)
  local copies, waits for them, and re-layouts  1.52 us (1%)
    ppermute x24, waiting for transfers between devices, exchange(): return lax.ppermute(value, AXES, pairs)  40.6 us
    ppermute x24, starting transfers between devices, exchange(): return lax.ppermute(value, AXES, pairs)  38.8 us
    all_to_all x2, blocking collectives, sum_everywhere(): lax.all_to_all(jnp.broadcast_to(part, (PLANE,) + part.shape), ('x', 'y'),...  34.6 us
    pallas_call x2, Pallas kernels, factor_call(): pl.pallas_call(factor_kernel, out_shape=SQUARE, in_specs=[VM], out_specs=...  8.5 us
    pallas_call x1, Pallas kernels, start_call(): pl.pallas_call(start_kernel, out_shape=(jax.ShapeDtypeStruct((rows, K), j...  7.17 us
    pallas_call x1, Pallas kernels, middle_call(): pl.pallas_call(middle_kernel, out_shape=(jax.ShapeDtypeStruct((rows, K),...  5.65 us
  transfers between devices with their start and end apart: 24, of which 16 were waited for; matrix products, arithmetic and copies ran while one was open for 1% of the time, Pallas kernels for 6%

profile of v2, /device:TPU:1, one launch (start us, length us, event | category | flops | bytes accessed | tf_op | source)
XLA Modules:
  0.0 142.0 jit_solution(1576119761840108057)
XLA Ops:
  0.6 1.2 copy-done
  1.9 7.2 %start.1 = (f32[1024,128]{1,0:T(8,128)S(1)}, f32[16,136,128]{2,1,0:T(8,128)S(1)}, f32[16,136,128]{2,1,0:T(8,128)S(1)}) custom-call(s32[1]{0:T(128)} %bitcast.core, s32[1]{0:T(128)} %bitcast.1.x, s32[1]{0:T(128)} %bitcast.2.y, bf16[1024,4096]{1,0:T(8,128)(2,1)} %held.1, bf16[4096,128]{1,0:T(8,128)(2,1)S(1)} %copy-done), custom_call_target="tpu_custom_call" | custom-call | tf_op jit(solution)/shard_map/start/pallas_call | solution.py:254
  9.0 3.3 %collective-permute-start = (f32[16,136,128]{2,1,0:T(8,128)S(1)}, f32[16,136,128]{2,1,0:T(8,128)S(1)}, u32[]{:S(2)}, u32[]{:S(2)}) collective-permute-start(f32[16,136,128]{2,1,0:T(8,128)S(1)} %get-tuple-element.19), channel_id=1, source_target_pairs={{0,4},{1,5},{2,6},{3,7},{4,0},{5,1},{6,2},{7,3},{8,12},{9,13},{10,... | collective-permute-start | bytes 3342344 | tf_op jit(solution)/shard_map/ppermute | solution.py:33
  12.4 2.4 %collective-permute-done = f32[16,136,128]{2,1,0:T(8,128)S(1)} collective-permute-done((f32[16,136,128]{2,1,0:T(8,128)S(1)}, f32[16,136,128]{2,1,0:T(8,128)S(1)}, u32[]{:S(2)}, u32[]{:S(2)}) %collective-permute-start) | collective-permute-done | bytes 1114144 | tf_op jit(solution)/shard_map/ppermute | solution.py:33
  14.7 0.1 add.66
  14.9 0.1 fusion.15
  14.9 1.1 collective-permute-start.1
  16.0 0.9 collective-permute-start.3
  16.9 0.8 collective-permute-start.2
  17.7 4.6 %collective-permute-done.1 = f32[4,136,128]{2,1,0:T(8,128)S(1)} collective-permute-done((f32[4,136,128]{2,1,0:T(8,128)S(1)}, f32[4,136,128]{2,1,0:T(8,128)S(1)}, u32[]{:S(2)}, u32[]{:S(2)}) %collective-permute-start.1) | collective-permute-done | bytes 278560 | tf_op jit(solution)/shard_map/ppermute | solution.py:33
  22.3 2.9 %collective-permute-done.3 = f32[4,136,128]{2,1,0:T(8,128)S(1)} collective-permute-done((f32[4,136,128]{2,1,0:T(8,128)S(1)}, f32[4,136,128]{2,1,0:T(8,128)S(1)}, u32[]{:S(2)}, u32[]{:S(2)}) %collective-permute-start.3) | collective-permute-done | bytes 278560 | tf_op jit(solution)/shard_map/ppermute | solution.py:33
  25.2 0.0 collective-permute-done.2
  25.2 0.1 fusion.3
  25.3 1.4 collective-permute-start.4
  26.7 0.8 collective-permute-start.6
  27.5 0.6 collective-permute-start.5
  28.0 2.0 %collective-permute-done.4 = f32[1,136,128]{2,1,0:T(8,128)S(1)} collective-permute-done((f32[1,136,128]{2,1,0:T(8,128)S(1)}, f32[1,136,128]{2,1,0:T(8,128)S(1)}, u32[]{:S(2)}, u32[]{:S(2)}) %collective-permute-start.4) | collective-permute-done | bytes 69664 | tf_op jit(solution)/shard_map/ppermute | solution.py:33
  30.1 1.3 collective-permute-done.6
  31.4 0.0 collective-permute-done.5
  31.4 1.3 collective-permute-start.9
  32.7 3.0 %collective-permute-start.8 = (f32[136,128]{1,0:T(8,128)S(1)}, f32[136,128]{1,0:T(8,128)S(1)}, u32[]{:S(2)}, u32[]{:S(2)}) collective-permute-start(f32[136,128]{1,0:T(8,128)S(1)} %fusion.9), channel_id=1, source_target_pairs={{0,64},{1,65},{2,66},{3,67},{4,68},{5,69},{6,70},{7,71},{8,72},{9,... | collective-permute-start | bytes 208904 | tf_op jit(solution)/shard_map/ppermute | solution.py:33
  35.7 0.0 collective-permute-start.7
  35.7 0.0 collective-permute-done.9
  35.7 2.4 %collective-permute-done.8 = f32[136,128]{1,0:T(8,128)S(1)} collective-permute-done((f32[136,128]{1,0:T(8,128)S(1)}, f32[136,128]{1,0:T(8,128)S(1)}, u32[]{:S(2)}, u32[]{:S(2)}) %collective-permute-start.8) | collective-permute-done | bytes 69664 | tf_op jit(solution)/shard_map/ppermute | solution.py:33
  38.2 3.2 %collective-permute-done.7 = f32[136,128]{1,0:T(8,128)S(1)} collective-permute-done((f32[136,128]{1,0:T(8,128)S(1)}, f32[136,128]{1,0:T(8,128)S(1)}, u32[]{:S(2)}, u32[]{:S(2)}) %collective-permute-start.7) | collective-permute-done | bytes 69664 | tf_op jit(solution)/shard_map/ppermute | solution.py:33
  41.4 2.6 %collective-permute-start.10 = (f32[136,128]{1,0:T(8,128)S(1)}, f32[136,128]{1,0:T(8,128)S(1)}, u32[]{:S(2)}, u32[]{:S(2)}) collective-permute-start(f32[136,128]{1,0:T(8,128)S(1)} %add_add_fusion.1), channel_id=1, source_target_pairs={{0,192},{1,193},{2,194},{3,195},{4,196},{5,197},{6,198},{7,199},{8... | collective-permute-start | bytes 208904 | tf_op jit(solution)/shard_map/ppermute | solution.py:33
  43.9 3.5 %collective-permute-done.10 = f32[136,128]{1,0:T(8,128)S(1)} collective-permute-done((f32[136,128]{1,0:T(8,128)S(1)}, f32[136,128]{1,0:T(8,128)S(1)}, u32[]{:S(2)}, u32[]{:S(2)}) %collective-permute-start.10) | collective-permute-done | bytes 69664 | tf_op jit(solution)/shard_map/ppermute | solution.py:33
  47.5 0.1 broadcast_in_dim.6
  47.6 18.1 %all_to_all.10.own = f32[16,136,128]{2,1,0:T(8,128)S(1)} all-to-all(f32[16,136,128]{2,1,0:T(8,128)S(1)} %broadcast_in_dim.6), channel_id=1, replica_groups=mesh['z'=8,'x'=4,'core'=2,'y'=4] {'x','y'}, dimensions={0} | all-to-all | bytes 2228224 | tf_op jit(solution)/shard_map/all_to_all | solution.py:58
  65.7 5.7 %collective-permute-start.11 = (f32[16,136,128]{2,1,0:T(8,128)S(1)}, f32[16,136,128]{2,1,0:T(8,128)S(1)}, u32[]{:S(2)}, u32[]{:S(2)}) collective-permute-start(f32[16,136,128]{2,1,0:T(8,128)S(1)} %all_to_all.10.own), channel_id=1, source_target_pairs={{0,4},{1,5},{2,6},{3,7},{4,0},{5,1},{6,2},{7,3},{8,12},{9,13},{10,... | collective-permute-start | bytes 3342344 | tf_op jit(solution)/shard_map/ppermute | solution.py:33
  71.3 4.3 %factor.2.inverse = f32[128,128]{1,0:T(8,128)S(1)} custom-call(f32[16,136,128]{2,1,0:T(8,128)S(1)} %all_to_all.10.own), custom_call_target="tpu_custom_call" | custom-call | flops 2097152 | bytes 1000000 | tf_op jit(solution)/shard_map/factor/pallas_call | solution.py:270
  75.6 0.0 collective-permute-done.11.other
  75.6 5.7 %middle.1 = (f32[1024,128]{1,0:T(8,128)S(1)}, f32[16,136,128]{2,1,0:T(8,128)S(1)}, f32[16,136,128]{2,1,0:T(8,128)S(1)}) custom-call(s32[1]{0:T(128)} %bitcast.core, s32[1]{0:T(128)} %bitcast.1.x, s32[1]{0:T(128)} %bitcast.2.y, f32[16,136,128]{2,1,0:T(8,128)S(1)} %all_to_all.10.own, f32[16,136,128]{2,1,0:T(8,128)S(1)} %collective-permute-done.11.other, ...), custom_call_target="tpu_custom_call" | custom-call | tf_op jit(solution)/shard_map/middle/pallas_call | solution.py:283
  81.3 0.1 collective-permute-start.12
  81.4 2.7 %collective-permute-done.12 = f32[16,136,128]{2,1,0:T(8,128)S(1)} collective-permute-done((f32[16,136,128]{2,1,0:T(8,128)S(1)}, f32[16,136,128]{2,1,0:T(8,128)S(1)}, u32[]{:S(2)}, u32[]{:S(2)}) %collective-permute-start.12) | collective-permute-done | bytes 1114144 | tf_op jit(solution)/shard_map/ppermute | solution.py:33
  84.1 0.1 add.77
  84.3 0.1 fusion.14
  84.3 1.0 collective-permute-start.13
  85.3 1.7 %collective-permute-start.15 = (f32[4,136,128]{2,1,0:T(8,128)S(1)}, f32[4,136,128]{2,1,0:T(8,128)S(1)}, u32[]{:S(2)}, u32[]{:S(2)}) collective-permute-start(f32[4,136,128]{2,1,0:T(8,128)S(1)} %get-tuple-element.34), channel_id=1, source_target_pairs={{0,3},{1,2},{2,1},{3,0},{4,28},{5,29},{6,30},{7,31},{8,11},{9,10},... | collective-permute-start | bytes 835592 | tf_op jit(solution)/shard_map/ppermute | solution.py:33
  87.0 0.0 collective-permute-start.14
  87.1 4.6 %collective-permute-done.13 = f32[4,136,128]{2,1,0:T(8,128)S(1)} collective-permute-done((f32[4,136,128]{2,1,0:T(8,128)S(1)}, f32[4,136,128]{2,1,0:T(8,128)S(1)}, u32[]{:S(2)}, u32[]{:S(2)}) %collective-permute-start.13) | collective-permute-done | bytes 278560 | tf_op jit(solution)/shard_map/ppermute | solution.py:33
  91.6 2.9 %collective-permute-done.15 = f32[4,136,128]{2,1,0:T(8,128)S(1)} collective-permute-done((f32[4,136,128]{2,1,0:T(8,128)S(1)}, f32[4,136,128]{2,1,0:T(8,128)S(1)}, u32[]{:S(2)}, u32[]{:S(2)}) %collective-permute-start.15) | collective-permute-done | bytes 278560 | tf_op jit(solution)/shard_map/ppermute | solution.py:33
  94.6 0.0 collective-permute-done.14
  94.6 0.1 fusion.1
  94.7 0.9 collective-permute-start.16
  95.6 1.6 %collective-permute-start.18 = (f32[1,136,128]{2,1,0:T(8,128)S(1)}, f32[1,136,128]{2,1,0:T(8,128)S(1)}, u32[]{:S(2)}, u32[]{:S(2)}) collective-permute-start(f32[1,136,128]{2,1,0:T(8,128)S(1)} %get-tuple-element.40), channel_id=1, source_target_pairs={{0,24},{1,25},{2,26},{3,27},{4,7},{5,6},{6,5},{7,4},{8,16},{9,17},... | collective-permute-start | bytes 208904 | tf_op jit(solution)/shard_map/ppermute | solution.py:33
  97.1 0.3 collective-permute-start.17
  97.4 2.0 %collective-permute-done.16 = f32[1,136,128]{2,1,0:T(8,128)S(1)} collective-permute-done((f32[1,136,128]{2,1,0:T(8,128)S(1)}, f32[1,136,128]{2,1,0:T(8,128)S(1)}, u32[]{:S(2)}, u32[]{:S(2)}) %collective-permute-start.16) | collective-permute-done | bytes 69664 | tf_op jit(solution)/shard_map/ppermute | solution.py:33
  99.4 1.0 collective-permute-done.18
  100.5 0.1 collective-permute-done.17
  100.6 0.1 collective-permute-start.21
  100.7 0.7 collective-permute-start.20
  101.4 2.8 %collective-permute-start.19 = (f32[136,128]{1,0:T(8,128)S(1)}, f32[136,128]{1,0:T(8,128)S(1)}, u32[]{:S(2)}, u32[]{:S(2)}) collective-permute-start(f32[136,128]{1,0:T(8,128)S(1)} %fusion.6), channel_id=1, source_target_pairs={{0,96},{1,97},{2,98},{3,99},{4,100},{5,101},{6,102},{7,103},{8,104... | collective-permute-start | bytes 208904 | tf_op jit(solution)/shard_map/ppermute | solution.py:33
  104.3 1.4 fusion.10
  105.6 0.0 collective-permute-done.21
  105.6 1.5 %collective-permute-done.19 = f32[136,128]{1,0:T(8,128)S(1)} collective-permute-done((f32[136,128]{1,0:T(8,128)S(1)}, f32[136,128]{1,0:T(8,128)S(1)}, u32[]{:S(2)}, u32[]{:S(2)}) %collective-permute-start.19) | collective-permute-done | bytes 69664 | tf_op jit(solution)/shard_map/ppermute | solution.py:33
  107.2 2.8 %collective-permute-start.22 = (f32[136,128]{1,0:T(8,128)S(1)}, f32[136,128]{1,0:T(8,128)S(1)}, u32[]{:S(2)}, u32[]{:S(2)}) collective-permute-start(f32[136,128]{1,0:T(8,128)S(1)} %add_add_fusion), channel_id=1, source_target_pairs={{0,192},{1,193},{2,194},{3,195},{4,196},{5,197},{6,198},{7,199},{8... | collective-permute-start | bytes 208904 | tf_op jit(solution)/shard_map/ppermute | solution.py:33
  110.0 3.3 %collective-permute-done.22 = f32[136,128]{1,0:T(8,128)S(1)} collective-permute-done((f32[136,128]{1,0:T(8,128)S(1)}, f32[136,128]{1,0:T(8,128)S(1)}, u32[]{:S(2)}, u32[]{:S(2)}) %collective-permute-start.22) | collective-permute-done | bytes 69664 | tf_op jit(solution)/shard_map/ppermute | solution.py:33
  113.3 0.1 broadcast_in_dim.7
  113.3 16.5 %all_to_all.11.own = f32[16,136,128]{2,1,0:T(8,128)S(1)} all-to-all(f32[16,136,128]{2,1,0:T(8,128)S(1)} %broadcast_in_dim.7), channel_id=1, replica_groups=mesh['z'=8,'x'=4,'core'=2,'y'=4] {'x','y'}, dimensions={0} | all-to-all | bytes 2228224 | tf_op jit(solution)/shard_map/all_to_all | solution.py:58
  129.9 5.4 %collective-permute-start.23 = (f32[16,136,128]{2,1,0:T(8,128)S(1)}, f32[16,136,128]{2,1,0:T(8,128)S(1)}, u32[]{:S(2)}, u32[]{:S(2)}) collective-permute-start(f32[16,136,128]{2,1,0:T(8,128)S(1)} %all_to_all.11.own), channel_id=1, source_target_pairs={{0,4},{1,5},{2,6},{3,7},{4,0},{5,1},{6,2},{7,3},{8,12},{9,13},{10,... | collective-permute-start | bytes 3342344 | tf_op jit(solution)/shard_map/ppermute | solution.py:33
  135.2 4.3 %factor.3.inverse = f32[128,128]{1,0:T(8,128)S(1)} custom-call(f32[16,136,128]{2,1,0:T(8,128)S(1)} %all_to_all.11.own), custom_call_target="tpu_custom_call" | custom-call | flops 2097152 | bytes 1000000 | tf_op jit(solution)/shard_map/factor/pallas_call | solution.py:270
  139.5 0.0 collective-permute-done.23.other
  139.5 2.3 %final.1 = (f32[128,4096]{1,0:T(8,128)}, f32[1024,128]{1,0:T(8,128)}) custom-call(s32[1]{0:T(128)} %bitcast.core, s32[1]{0:T(128)} %bitcast.1.x, s32[1]{0:T(128)} %bitcast.2.y, f32[16,136,128]{2,1,0:T(8,128)S(1)} %all_to_all.11.own, f32[16,136,128]{2,1,0:T(8,128)S(1)} %collective-permute-done.23.other, f32[128,128]{1,0:T(8,128)S(1)} %factor.3.inverse, ...), custom_call_target="tpu_custom_call" | custom-call | tf_op jit(solution)/shard_map/final/pallas_call | solution.py:295
  (15 shorter events, 0.2 us)
Async XLA Ops:
  0.6 1.2 copy-start
  1.9 73.7 %slice-start = ((s8[8388608]{0:T(1024)(128)(4,1)}), s8[4194304]{0:T(1024)(128)(4,1)S(1)}, s32[]{:S(2)}) async-start(s8[8388608]{0:T(1024)(128)(4,1)} %bitcast.8), calls=%async_computation.2 | async-start | bytes 8388608
  9.0 5.7 %collective-permute-start = (f32[16,136,128]{2,1,0:T(8,128)S(1)}, f32[16,136,128]{2,1,0:T(8,128)S(1)}, u32[]{:S(2)}, u32[]{:S(2)}) collective-permute-start(f32[16,136,128]{2,1,0:T(8,128)S(1)} %get-tuple-element.19), channel_id=1, source_target_pairs={{0,4},{1,5},{2,6},{3,7},{4,0},{5,1},{6,2},{7,3},{8,12},{9,13},{10,... | collective-permute-start | bytes 3342344 | tf_op jit(solution)/shard_map/ppermute | solution.py:33
  14.7 60.9 %slice-start.1 = ((s8[8388608]{0:T(1024)(128)(4,1)}), s8[4194304]{0:T(1024)(128)(4,1)S(1)}, s32[]{:S(2)}) async-start(s8[8388608]{0:T(1024)(128)(4,1)} %bitcast.8), calls=%async_computation.3 | async-start | bytes 8388608
  14.9 7.3 %collective-permute-start.1 = (f32[4,136,128]{2,1,0:T(8,128)S(1)}, f32[4,136,128]{2,1,0:T(8,128)S(1)}, u32[]{:S(2)}, u32[]{:S(2)}) collective-permute-start(f32[4,136,128]{2,1,0:T(8,128)S(1)} %get-tuple-element.36), channel_id=1, source_target_pairs={{0,2},{1,3},{2,0},{3,1},{4,20},{5,21},{6,22},{7,23},{8,10},{9,11},... | collective-permute-start | bytes 835592 | tf_op jit(solution)/shard_map/ppermute | solution.py:33
  16.0 9.2 %collective-permute-start.3 = (f32[4,136,128]{2,1,0:T(8,128)S(1)}, f32[4,136,128]{2,1,0:T(8,128)S(1)}, u32[]{:S(2)}, u32[]{:S(2)}) collective-permute-start(f32[4,136,128]{2,1,0:T(8,128)S(1)} %get-tuple-element.37), channel_id=1, source_target_pairs={{0,3},{1,2},{2,1},{3,0},{4,28},{5,29},{6,30},{7,31},{8,11},{9,10},... | collective-permute-start | bytes 835592 | tf_op jit(solution)/shard_map/ppermute | solution.py:33
  16.9 8.3 %collective-permute-start.2 = (f32[4,136,128]{2,1,0:T(8,128)S(1)}, f32[4,136,128]{2,1,0:T(8,128)S(1)}, u32[]{:S(2)}, u32[]{:S(2)}) collective-permute-start(f32[4,136,128]{2,1,0:T(8,128)S(1)} %get-tuple-element.38), channel_id=1, source_target_pairs={{0,1},{1,0},{2,3},{3,2},{4,12},{5,13},{6,14},{7,15},{8,9},{9,8},{1... | collective-permute-start | bytes 835592 | tf_op jit(solution)/shard_map/ppermute | solution.py:33
  25.3 4.8 %collective-permute-start.4 = (f32[1,136,128]{2,1,0:T(8,128)S(1)}, f32[1,136,128]{2,1,0:T(8,128)S(1)}, u32[]{:S(2)}, u32[]{:S(2)}) collective-permute-start(f32[1,136,128]{2,1,0:T(8,128)S(1)} %get-tuple-element.42), channel_id=1, source_target_pairs={{0,16},{1,17},{2,18},{3,19},{4,6},{5,7},{6,4},{7,5},{8,24},{9,25},... | collective-permute-start | bytes 208904 | tf_op jit(solution)/shard_map/ppermute | solution.py:33
  26.7 4.7 %collective-permute-start.6 = (f32[1,136,128]{2,1,0:T(8,128)S(1)}, f32[1,136,128]{2,1,0:T(8,128)S(1)}, u32[]{:S(2)}, u32[]{:S(2)}) collective-permute-start(f32[1,136,128]{2,1,0:T(8,128)S(1)} %get-tuple-element.43), channel_id=1, source_target_pairs={{0,24},{1,25},{2,26},{3,27},{4,7},{5,6},{6,5},{7,4},{8,16},{9,17},... | collective-permute-start | bytes 208904 | tf_op jit(solution)/shard_map/ppermute | solution.py:33
  27.5 3.9 %collective-permute-start.5 = (f32[1,136,128]{2,1,0:T(8,128)S(1)}, f32[1,136,128]{2,1,0:T(8,128)S(1)}, u32[]{:S(2)}, u32[]{:S(2)}) collective-permute-start(f32[1,136,128]{2,1,0:T(8,128)S(1)} %get-tuple-element.44), channel_id=1, source_target_pairs={{0,8},{1,9},{2,10},{3,11},{4,5},{5,4},{6,7},{7,6},{8,0},{9,1},{10,... | collective-permute-start | bytes 208904 | tf_op jit(solution)/shard_map/ppermute | solution.py:33
  31.4 4.3 %collective-permute-start.9 = (f32[136,128]{1,0:T(8,128)S(1)}, f32[136,128]{1,0:T(8,128)S(1)}, u32[]{:S(2)}, u32[]{:S(2)}) collective-permute-start(f32[136,128]{1,0:T(8,128)S(1)} %fusion.9), channel_id=1, source_target_pairs={{0,32},{1,33},{2,34},{3,35},{4,36},{5,37},{6,38},{7,39},{8,40},{9,... | collective-permute-start | bytes 208904 | tf_op jit(solution)/shard_map/ppermute | solution.py:33
  32.7 5.4 %collective-permute-start.8 = (f32[136,128]{1,0:T(8,128)S(1)}, f32[136,128]{1,0:T(8,128)S(1)}, u32[]{:S(2)}, u32[]{:S(2)}) collective-permute-start(f32[136,128]{1,0:T(8,128)S(1)} %fusion.9), channel_id=1, source_target_pairs={{0,64},{1,65},{2,66},{3,67},{4,68},{5,69},{6,70},{7,71},{8,72},{9,... | collective-permute-start | bytes 208904 | tf_op jit(solution)/shard_map/ppermute | solution.py:33
  35.7 5.6 %collective-permute-start.7 = (f32[136,128]{1,0:T(8,128)S(1)}, f32[136,128]{1,0:T(8,128)S(1)}, u32[]{:S(2)}, u32[]{:S(2)}) collective-permute-start(f32[136,128]{1,0:T(8,128)S(1)} %fusion.9), channel_id=1, source_target_pairs={{0,96},{1,97},{2,98},{3,99},{4,100},{5,101},{6,102},{7,103},{8,104... | collective-permute-start | bytes 208904 | tf_op jit(solution)/shard_map/ppermute | solution.py:33
  41.4 6.1 %collective-permute-start.10 = (f32[136,128]{1,0:T(8,128)S(1)}, f32[136,128]{1,0:T(8,128)S(1)}, u32[]{:S(2)}, u32[]{:S(2)}) collective-permute-start(f32[136,128]{1,0:T(8,128)S(1)} %add_add_fusion.1), channel_id=1, source_target_pairs={{0,192},{1,193},{2,194},{3,195},{4,196},{5,197},{6,198},{7,199},{8... | collective-permute-start | bytes 208904 | tf_op jit(solution)/shard_map/ppermute | solution.py:33
  65.7 9.9 %collective-permute-start.11 = (f32[16,136,128]{2,1,0:T(8,128)S(1)}, f32[16,136,128]{2,1,0:T(8,128)S(1)}, u32[]{:S(2)}, u32[]{:S(2)}) collective-permute-start(f32[16,136,128]{2,1,0:T(8,128)S(1)} %all_to_all.10.own), channel_id=1, source_target_pairs={{0,4},{1,5},{2,6},{3,7},{4,0},{5,1},{6,2},{7,3},{8,12},{9,13},{10,... | collective-permute-start | bytes 3342344 | tf_op jit(solution)/shard_map/ppermute | solution.py:33
  81.3 2.8 %collective-permute-start.12 = (f32[16,136,128]{2,1,0:T(8,128)S(1)}, f32[16,136,128]{2,1,0:T(8,128)S(1)}, u32[]{:S(2)}, u32[]{:S(2)}) collective-permute-start(f32[16,136,128]{2,1,0:T(8,128)S(1)} %get-tuple-element.24), channel_id=1, source_target_pairs={{0,4},{1,5},{2,6},{3,7},{4,0},{5,1},{6,2},{7,3},{8,12},{9,13},{10,... | collective-permute-start | bytes 3342344 | tf_op jit(solution)/shard_map/ppermute | solution.py:33
  84.3 7.3 %collective-permute-start.13 = (f32[4,136,128]{2,1,0:T(8,128)S(1)}, f32[4,136,128]{2,1,0:T(8,128)S(1)}, u32[]{:S(2)}, u32[]{:S(2)}) collective-permute-start(f32[4,136,128]{2,1,0:T(8,128)S(1)} %get-tuple-element.33), channel_id=1, source_target_pairs={{0,2},{1,3},{2,0},{3,1},{4,20},{5,21},{6,22},{7,23},{8,10},{9,11},... | collective-permute-start | bytes 835592 | tf_op jit(solution)/shard_map/ppermute | solution.py:33
  85.3 9.2 %collective-permute-start.15 = (f32[4,136,128]{2,1,0:T(8,128)S(1)}, f32[4,136,128]{2,1,0:T(8,128)S(1)}, u32[]{:S(2)}, u32[]{:S(2)}) collective-permute-start(f32[4,136,128]{2,1,0:T(8,128)S(1)} %get-tuple-element.34), channel_id=1, source_target_pairs={{0,3},{1,2},{2,1},{3,0},{4,28},{5,29},{6,30},{7,31},{8,11},{9,10},... | collective-permute-start | bytes 835592 | tf_op jit(solution)/shard_map/ppermute | solution.py:33
  87.0 7.6 %collective-permute-start.14 = (f32[4,136,128]{2,1,0:T(8,128)S(1)}, f32[4,136,128]{2,1,0:T(8,128)S(1)}, u32[]{:S(2)}, u32[]{:S(2)}) collective-permute-start(f32[4,136,128]{2,1,0:T(8,128)S(1)} %get-tuple-element.35), channel_id=1, source_target_pairs={{0,1},{1,0},{2,3},{3,2},{4,12},{5,13},{6,14},{7,15},{8,9},{9,8},{1... | collective-permute-start | bytes 835592 | tf_op jit(solution)/shard_map/ppermute | solution.py:33
  94.7 4.8 %collective-permute-start.16 = (f32[1,136,128]{2,1,0:T(8,128)S(1)}, f32[1,136,128]{2,1,0:T(8,128)S(1)}, u32[]{:S(2)}, u32[]{:S(2)}) collective-permute-start(f32[1,136,128]{2,1,0:T(8,128)S(1)} %get-tuple-element.39), channel_id=1, source_target_pairs={{0,16},{1,17},{2,18},{3,19},{4,6},{5,7},{6,4},{7,5},{8,24},{9,25},... | collective-permute-start | bytes 208904 | tf_op jit(solution)/shard_map/ppermute | solution.py:33
  95.6 4.9 %collective-permute-start.18 = (f32[1,136,128]{2,1,0:T(8,128)S(1)}, f32[1,136,128]{2,1,0:T(8,128)S(1)}, u32[]{:S(2)}, u32[]{:S(2)}) collective-permute-start(f32[1,136,128]{2,1,0:T(8,128)S(1)} %get-tuple-element.40), channel_id=1, source_target_pairs={{0,24},{1,25},{2,26},{3,27},{4,7},{5,6},{6,5},{7,4},{8,16},{9,17},... | collective-permute-start | bytes 208904 | tf_op jit(solution)/shard_map/ppermute | solution.py:33
  97.1 3.5 %collective-permute-start.17 = (f32[1,136,128]{2,1,0:T(8,128)S(1)}, f32[1,136,128]{2,1,0:T(8,128)S(1)}, u32[]{:S(2)}, u32[]{:S(2)}) collective-permute-start(f32[1,136,128]{2,1,0:T(8,128)S(1)} %get-tuple-element.41), channel_id=1, source_target_pairs={{0,8},{1,9},{2,10},{3,11},{4,5},{5,4},{6,7},{7,6},{8,0},{9,1},{10,... | collective-permute-start | bytes 208904 | tf_op jit(solution)/shard_map/ppermute | solution.py:33
  100.6 5.0 %collective-permute-start.21 = (f32[136,128]{1,0:T(8,128)S(1)}, f32[136,128]{1,0:T(8,128)S(1)}, u32[]{:S(2)}, u32[]{:S(2)}) collective-permute-start(f32[136,128]{1,0:T(8,128)S(1)} %fusion.6), channel_id=1, source_target_pairs={{0,32},{1,33},{2,34},{3,35},{4,36},{5,37},{6,38},{7,39},{8,40},{9,... | collective-permute-start | bytes 208904 | tf_op jit(solution)/shard_map/ppermute | solution.py:33
  100.7 4.9 %collective-permute-start.20 = (f32[136,128]{1,0:T(8,128)S(1)}, f32[136,128]{1,0:T(8,128)S(1)}, u32[]{:S(2)}, u32[]{:S(2)}) collective-permute-start(f32[136,128]{1,0:T(8,128)S(1)} %fusion.6), channel_id=1, source_target_pairs={{0,64},{1,65},{2,66},{3,67},{4,68},{5,69},{6,70},{7,71},{8,72},{9,... | collective-permute-start | bytes 208904 | tf_op jit(solution)/shard_map/ppermute | solution.py:33
  101.4 5.7 %collective-permute-start.19 = (f32[136,128]{1,0:T(8,128)S(1)}, f32[136,128]{1,0:T(8,128)S(1)}, u32[]{:S(2)}, u32[]{:S(2)}) collective-permute-start(f32[136,128]{1,0:T(8,128)S(1)} %fusion.6), channel_id=1, source_target_pairs={{0,96},{1,97},{2,98},{3,99},{4,100},{5,101},{6,102},{7,103},{8,104... | collective-permute-start | bytes 208904 | tf_op jit(solution)/shard_map/ppermute | solution.py:33
  107.2 6.1 %collective-permute-start.22 = (f32[136,128]{1,0:T(8,128)S(1)}, f32[136,128]{1,0:T(8,128)S(1)}, u32[]{:S(2)}, u32[]{:S(2)}) collective-permute-start(f32[136,128]{1,0:T(8,128)S(1)} %add_add_fusion), channel_id=1, source_target_pairs={{0,192},{1,193},{2,194},{3,195},{4,196},{5,197},{6,198},{7,199},{8... | collective-permute-start | bytes 208904 | tf_op jit(solution)/shard_map/ppermute | solution.py:33
  129.9 9.6 %collective-permute-start.23 = (f32[16,136,128]{2,1,0:T(8,128)S(1)}, f32[16,136,128]{2,1,0:T(8,128)S(1)}, u32[]{:S(2)}, u32[]{:S(2)}) collective-permute-start(f32[16,136,128]{2,1,0:T(8,128)S(1)} %all_to_all.11.own), channel_id=1, source_target_pairs={{0,4},{1,5},{2,6},{3,7},{4,0},{5,1},{6,2},{7,3},{8,12},{9,13},{10,... | collective-permute-start | bytes 3342344 | tf_op jit(solution)/shard_map/ppermute | solution.py:33

commit v3 on v2

--- a/solution.py
+++ b/solution.py
@@ -44,17 +44,23 @@
     return partner
 
 
+def column_partner(mask):
+    def partner(z, x, core, y):
+        return z ^ mask, x, core, y
+
+    return partner
+
+
 def sum_everywhere(give, keep, beside=()):
-    half = keep + other_core(give)
-    for first in (True, False):
-        half = half.reshape((4, -1) + half.shape[1:])
-        arrived = [exchange(half[mask], plane_partner(mask, first)) for mask in (2, 1, 3)]
-        half = half[0] + arrived[0] + arrived[1] + arrived[2]
-    part = half[0]
-    arrived = [exchange(part, lambda z, x, core, y: (z ^ mask, x, core, y)) for mask in (3, 2, 1)]
+    far, near = [mine + other_core(theirs) for mine, theirs in zip(keep, give)]
+    arrived = [exchange(part, plane_partner(mask, True)) for part, mask in ((far[4:], 3), (near[4:], 1), (far[:4], 2))]
+    half = near[:4] + arrived[0] + arrived[1] + arrived[2]
+    arrived = [exchange(half[mask], plane_partner(mask, False)) for mask in (2, 1, 3)]
+    part = half[0] + arrived[0] + arrived[1] + arrived[2]
+    arrived = [exchange(part, column_partner(mask)) for mask in (3, 2, 1)]
     arrived, beside = lax.optimization_barrier((arrived, beside))
     part = part + arrived[0] + arrived[1] + arrived[2]
-    part = part + exchange(part, lambda z, x, core, y: (z ^ 6, x, core, y))
+    part = part + exchange(part, column_partner(6))
     own = lax.all_to_all(
         jnp.broadcast_to(part, (PLANE,) + part.shape), ("x", "y"), split_axis=0, concat_axis=0, tiled=True
     )
@@ -157,11 +163,18 @@
     return both[:K] + both[K:]
 
 
+def place_of(chunk, side):
+    return jnp.where(side == 0, Y * (chunk % X) + chunk // X, chunk)
+
+
 def apply_everywhere(core, own, other, inverse, store):
     for n in range(PLANE // 2):
-        for ref, start in ((own, core * HALF), (other, (1 - core) * HALF)):
-            terms = jnp.concatenate([ref[2 * n, :K, :], ref[2 * n + 1, :K, :]], axis=1)
-            store(pl.multiple_of(start + 2 * WIDE * n, 2 * WIDE), apply_factor(inverse, terms))
+        for ref, side in ((own, core), (other, 1 - core)):
+            pair = [ref[place_of(2 * n + i, side), :K, :] for i in (0, 1)]
+            store(
+                pl.multiple_of(side * HALF + 2 * WIDE * n, 2 * WIDE),
+                apply_factor(inverse, jnp.concatenate(pair, axis=1)),
+            )
 
 
 def fetch(data, held, arrived):
@@ -174,42 +187,39 @@
     return copies
 
 
-def make_message(place, held, tall, give, keep, turned):
+def make_message(place, held, tall, give, keep, turned, gram):
     core, x, y = place
-    sides = ((give, 1 - core), (keep, core))
-
-    def slot(side, at_x, at_y):
-        over_x, over_y = at_x ^ x, at_y ^ y
-        return jnp.where(side == 0, 4 * over_y + over_x, 4 * over_x + over_y)
-
-    gram = three_term_gram(tall[...])
-    for j in range(PLANE):
-        for ref, side in sides:
-            ref[slot(side, j // Y, j % Y), K:, :] = gram[THIN * j : THIN * (j + 1), :]
+    gram[...] = three_term_gram(tall[...])
     turned[...] = jnp.concatenate(two_terms(tall[...]), axis=1).T
-    for n in range(X):
-        for ref, side in sides:
-            columns = pl.ds(pl.multiple_of(side * HALF + Y * WIDE * n, Y * WIDE), Y * WIDE)
+    for a in (2, 3, 0, 1):
+        for refs, side in ((give, 1 - core), (keep, core)):
+            ref = refs[0] if a >= 2 else refs[1]
+            p = a ^ jnp.where(side == 0, y, x)
+            q = jnp.where(side == 0, x, y)
+            columns = pl.ds(pl.multiple_of(side * HALF + 4 * WIDE * p, 4 * WIDE), 4 * WIDE)
             both = quick_dot(turned[...], held[:, columns])
             terms = both[:K] + both[K:]
-            for i in range(Y):
-                ref[slot(side, n, i), :K, :] = terms[:, WIDE * i : WIDE * (i + 1)]
-
-
-def start_kernel(core, x, y, data, sketch, first, give, keep, held, turned, arrived):
+            for i in range(4):
+                slot = 4 * (a % 2) + (i ^ q)
+                ref[slot, :K, :] = terms[:, WIDE * i : WIDE * (i + 1)]
+                ref[slot, K:, :] = gram[pl.ds(pl.multiple_of(THIN * (4 * p + i), THIN), THIN), :]
+
+
+def start_kernel(core, x, y, data, sketch, first, give2, give0, keep2, keep0, held, turned, gram, arrived):
     copies = fetch(data, held, arrived)
     for b in range(STEPS):
         copies[b].wait()
         rows = pl.ds(b * BLOCK, BLOCK)
         first[rows, :] = quick_dot(held[rows, :], sketch[...])
-    make_message((core[0], x[0], y[0]), held, first, give, keep, turned)
-
-
-def factor_kernel(own, inverse):
-    inverse[...] = inverse_factor(jnp.concatenate([own[j, K:, :] for j in range(PLANE)], axis=0))
-
-
-def middle_kernel(core, x, y, own, other, inverse, held, second, give, keep, back, turned):
+    make_message((core[0], x[0], y[0]), held, first, (give2, give0), (keep2, keep0), turned, gram)
+
+
+def factor_kernel(core, own, inverse):
+    rows = [own[place_of(chunk, core[0]), K:, :] for chunk in range(PLANE)]
+    inverse[...] = inverse_factor(jnp.concatenate(rows, axis=0))
+
+
+def middle_kernel(core, x, y, own, other, inverse, held, second, give2, give0, keep2, keep0, back, turned, gram):
     scaled = inverse[...] * (1.0 / ROOT_ROWS)
 
     def store(start, terms):
@@ -219,7 +229,7 @@
     for b in range(STEPS):
         rows = pl.ds(b * BLOCK, BLOCK)
         second[rows, :] = quick_dot(held[rows, :], back[...], ((1,), (1,)))
-    make_message((core[0], x[0], y[0]), held, second, give, keep, turned)
+    make_message((core[0], x[0], y[0]), held, second, (give2, give0), (keep2, keep0), turned, gram)
 
 
 def final_kernel(core, x, y, own, other, inverse, tall, projected, basis, wide, narrow, sent):
@@ -245,7 +255,7 @@
 VM = pl.BlockSpec(memory_space=pltpu.VMEM)
 SM = pl.BlockSpec(memory_space=pltpu.SMEM)
 ANY = pl.BlockSpec(memory_space=pl.ANY)
-MESSAGE = jax.ShapeDtypeStruct((PLANE, ROWS, K), jnp.float32)
+PART = jax.ShapeDtypeStruct((PLANE // 2, ROWS, K), jnp.float32)
 SQUARE = jax.ShapeDtypeStruct((K, K), jnp.float32)
 
 
@@ -253,12 +263,13 @@
     rows = data.shape[0]
     return pl.pallas_call(
         start_kernel,
-        out_shape=(jax.ShapeDtypeStruct((rows, K), jnp.float32), MESSAGE, MESSAGE),
+        out_shape=(jax.ShapeDtypeStruct((rows, K), jnp.float32), PART, PART, PART, PART),
         in_specs=[SM, SM, SM, ANY, VM],
-        out_specs=(VM, VM, VM),
+        out_specs=(VM,) * 5,
         scratch_shapes=[
             pltpu.VMEM(data.shape, jnp.bfloat16),
             pltpu.VMEM((2 * K, rows), jnp.bfloat16),
+            pltpu.VMEM((K, K), jnp.float32),
             pltpu.SemaphoreType.DMA((STEPS,)),
         ],
         compiler_params=params(48),
@@ -266,26 +277,30 @@
     )(*place, data, sketch)
 
 
-def factor_call(own):
+def factor_call(core, own):
     return pl.pallas_call(
         factor_kernel,
         out_shape=SQUARE,
-        in_specs=[VM],
+        in_specs=[SM, VM],
         out_specs=VM,
         compiler_params=params(),
         cost_estimate=pl.CostEstimate(flops=K**3, bytes_accessed=10**6, transcendentals=0),
         name="factor",
-    )(own)
+    )(core, own)
 
 
 def middle_call(place, own, other, inverse, held):
     rows = held.shape[0]
     return pl.pallas_call(
         middle_kernel,
-        out_shape=(jax.ShapeDtypeStruct((rows, K), jnp.float32), MESSAGE, MESSAGE),
+        out_shape=(jax.ShapeDtypeStruct((rows, K), jnp.float32), PART, PART, PART, PART),
         in_specs=[SM, SM, SM, VM, VM, VM, VM],
-        out_specs=(VM, VM, VM),
-        scratch_shapes=[pltpu.VMEM((K, D), jnp.bfloat16), pltpu.VMEM((2 * K, rows), jnp.bfloat16)],
+        out_specs=(VM,) * 5,
+        scratch_shapes=[
+            pltpu.VMEM((K, D), jnp.bfloat16),
+            pltpu.VMEM((2 * K, rows), jnp.bfloat16),
+            pltpu.VMEM((K, K), jnp.float32),
+        ],
         compiler_params=params(),
         name="middle",
     )(*place, own, other, inverse, held)
@@ -309,13 +324,13 @@
 
 def on_device(data, sketch):
     place = [lax.axis_index(axis).astype(jnp.int32).reshape(1) for axis in ("core", "x", "y")]
-    first, give, keep = start_call(place, data, sketch)
-    own, other, _ = sum_everywhere(give, keep)
-    inverse = factor_call(own)
-    second, give, keep = middle_call(place, own, other, inverse, data)
+    first, *parts = start_call(place, data, sketch)
+    own, other, _ = sum_everywhere(parts[:2], parts[2:])
+    inverse = factor_call(place[0], own)
+    second, *parts = middle_call(place, own, other, inverse, data)
     first_basis = exact_dot(first, ROOT_ROWS * inverse, ((1,), (1,)))
-    own, other, first_basis = sum_everywhere(give, keep, first_basis)
-    inverse = factor_call(own)
+    own, other, first_basis = sum_everywhere(parts[:2], parts[2:], first_basis)
+    inverse = factor_call(place[0], own)
     projected, basis = final_call(place, own, other, inverse, second)
     return (first_basis, basis, projected)
 

time: 142 us -> 141 us (level)
  waiting for transfers between devices: 40.6 us -> 38.8 us
    ppermute x24 -> x26, waiting for transfers between devices: 40.6 us -> 38.8 us  [exchange(): return lax.ppermute(value, AXES, pairs)]
    ppermute x24 -> x26, starting transfers between devices: 38.8 us -> 39.9 us  [exchange(): return lax.ppermute(value, AXES, pairs)]
  transfers between devices with their start and end apart: 24 -> 26, of which waited for: 16 -> 18; matrix products, arithmetic and copies ran while one was open for 1% -> 1% of each run, Pallas kernels for 6% -> 6%
where the time goes in v3:
time: 141 us
  starting transfers between devices  39.9 us (28%)
  waiting for transfers between devices  38.8 us (28%)
  blocking collectives  34.3 us (24%)
  Pallas kernels  23.6 us (17%)
  local copies, waits for them, and re-layouts  1.52 us (1%)
    ppermute x26, starting transfers between devices, exchange(): return lax.ppermute(value, AXES, pairs)  39.9 us
    ppermute x26, waiting for transfers between devices, exchange(): return lax.ppermute(value, AXES, pairs)  38.8 us
    all_to_all x2, blocking collectives, sum_everywhere(): lax.all_to_all(jnp.broadcast_to(part, (PLANE,) + part.shape), ('x', 'y'),...  34.3 us
    pallas_call x2, Pallas kernels, factor_call(): pl.pallas_call(factor_kernel, out_shape=SQUARE, in_specs=[SM, VM], out_sp...  8.51 us
    pallas_call x1, Pallas kernels, start_call(): pl.pallas_call(start_kernel, out_shape=(jax.ShapeDtypeStruct((rows, K), j...  7.17 us
    pallas_call x1, Pallas kernels, middle_call(): pl.pallas_call(middle_kernel, out_shape=(jax.ShapeDtypeStruct((rows, K),...  5.68 us
  transfers between devices with their start and end apart: 26, of which 18 were waited for; matrix products, arithmetic and copies ran while one was open for 1% of the time, Pallas kernels for 6%

profile of v3, /device:TPU:1, one launch (start us, length us, event | category | flops | bytes accessed | tf_op | source)
XLA Modules:
  0.0 141.1 jit_solution(14876502340126777415)
XLA Ops:
  0.6 1.2 copy-done
  1.9 7.2 %start.1 = (f32[1024,128]{1,0:T(8,128)S(1)}, f32[8,136,128]{2,1,0:T(8,128)S(1)}, f32[8,136,128]{2,1,0:T(8,128)S(1)}, f32[8,136,128]{2,1,0:T(8,128)S(1)}, f32[8,136,128]{2,1,0:T(8,128)S(1)}) custom-call(s32[1]{0:T(128)} %bitcast.core, s32[1]{0:T(128)} %bitcast.1.x, s32[1]{0:T(128)} %bitcast.2.y, bf16[1024,4096]{1,0:T(8,128)(2,1)} %held.1, ...), custom_call_target="tpu_custom_call" | custom-call | tf_op jit(solution)/shard_map/start/pallas_call | solution.py:264
  9.0 3.3 %collective-permute-start = (f32[8,136,128]{2,1,0:T(8,128)S(1)}, f32[8,136,128]{2,1,0:T(8,128)S(1)}, u32[]{:S(2)}, u32[]{:S(2)}) collective-permute-start(f32[8,136,128]{2,1,0:T(8,128)S(1)} %get-tuple-element.23), channel_id=1, source_target_pairs={{0,4},{1,5},{2,6},{3,7},{4,0},{5,1},{6,2},{7,3},{8,12},{9,13},{10,... | collective-permute-start | bytes 1671176 | tf_op jit(solution)/shard_map/ppermute | solution.py:33
  12.4 0.1 collective-permute-start.1
  12.5 1.5 %collective-permute-done = f32[8,136,128]{2,1,0:T(8,128)S(1)} collective-permute-done((f32[8,136,128]{2,1,0:T(8,128)S(1)}, f32[8,136,128]{2,1,0:T(8,128)S(1)}, u32[]{:S(2)}, u32[]{:S(2)}) %collective-permute-start) | collective-permute-done | bytes 557088 | tf_op jit(solution)/shard_map/ppermute | solution.py:33
  14.0 0.1 add.72
  14.1 0.1 collective-permute-start.3
  14.2 0.6 collective-permute-done.1
  14.7 0.1 add.73
  14.9 0.8 collective-permute-start.2
  15.7 1.9 %collective-permute-start.4 = (f32[4,136,128]{2,1,0:T(8,128)S(1)}, f32[4,136,128]{2,1,0:T(8,128)S(1)}, u32[]{:S(2)}, u32[]{:S(2)}) collective-permute-start(f32[4,136,128]{2,1,0:T(8,128)S(1)} %get-tuple-element.44), channel_id=1, source_target_pairs={{0,2},{1,3},{2,0},{3,1},{4,20},{5,21},{6,22},{7,23},{8,10},{9,11},... | collective-permute-start | bytes 835592 | tf_op jit(solution)/shard_map/ppermute | solution.py:33
  17.6 2.2 %collective-permute-done.3 = f32[4,136,128]{2,1,0:T(8,128)S(1)} collective-permute-done((f32[4,136,128]{2,1,0:T(8,128)S(1)}, f32[4,136,128]{2,1,0:T(8,128)S(1)}, u32[]{:S(2)}, u32[]{:S(2)}) %collective-permute-start.3) | collective-permute-done | bytes 278560 | tf_op jit(solution)/shard_map/ppermute | solution.py:33
  19.8 5.0 %collective-permute-done.2 = f32[4,136,128]{2,1,0:T(8,128)S(1)} collective-permute-done((f32[4,136,128]{2,1,0:T(8,128)S(1)}, f32[4,136,128]{2,1,0:T(8,128)S(1)}, u32[]{:S(2)}, u32[]{:S(2)}) %collective-permute-start.2) | collective-permute-done | bytes 278560 | tf_op jit(solution)/shard_map/ppermute | solution.py:33
  24.9 0.1 fusion.3
  24.9 1.6 %collective-permute-start.5 = (f32[136,128]{1,0:T(8,128)S(1)}, f32[136,128]{1,0:T(8,128)S(1)}, u32[]{:S(2)}, u32[]{:S(2)}) collective-permute-start(f32[136,128]{1,0:T(8,128)S(1)} %get-tuple-element.48), channel_id=1, source_target_pairs={{0,16},{1,17},{2,18},{3,19},{4,6},{5,7},{6,4},{7,5},{8,24},{9,25},... | collective-permute-start | bytes 208904 | tf_op jit(solution)/shard_map/ppermute | solution.py:33
  26.5 0.9 collective-permute-start.7
  27.4 0.2 collective-permute-start.6
  27.7 2.0 %collective-permute-done.5 = f32[136,128]{1,0:T(8,128)S(1)} collective-permute-done((f32[136,128]{1,0:T(8,128)S(1)}, f32[136,128]{1,0:T(8,128)S(1)}, u32[]{:S(2)}, u32[]{:S(2)}) %collective-permute-start.5) | collective-permute-done | bytes 69664 | tf_op jit(solution)/shard_map/ppermute | solution.py:33
  29.7 1.5 %collective-permute-done.7 = f32[136,128]{1,0:T(8,128)S(1)} collective-permute-done((f32[136,128]{1,0:T(8,128)S(1)}, f32[136,128]{1,0:T(8,128)S(1)}, u32[]{:S(2)}, u32[]{:S(2)}) %collective-permute-start.7) | collective-permute-done | bytes 69664 | tf_op jit(solution)/shard_map/ppermute | solution.py:33
  31.2 0.0 collective-permute-done.6
  31.2 1.4 %collective-permute-start.10 = (f32[136,128]{1,0:T(8,128)S(1)}, f32[136,128]{1,0:T(8,128)S(1)}, u32[]{:S(2)}, u32[]{:S(2)}) collective-permute-start(f32[136,128]{1,0:T(8,128)S(1)} %fusion.9), channel_id=1, source_target_pairs={{0,32},{1,33},{2,34},{3,35},{4,36},{5,37},{6,38},{7,39},{8,40},{9,... | collective-permute-start | bytes 208904 | tf_op jit(solution)/shard_map/ppermute | solution.py:33
  32.7 3.0 %collective-permute-start.9 = (f32[136,128]{1,0:T(8,128)S(1)}, f32[136,128]{1,0:T(8,128)S(1)}, u32[]{:S(2)}, u32[]{:S(2)}) collective-permute-start(f32[136,128]{1,0:T(8,128)S(1)} %fusion.9), channel_id=1, source_target_pairs={{0,64},{1,65},{2,66},{3,67},{4,68},{5,69},{6,70},{7,71},{8,72},{9,... | collective-permute-start | bytes 208904 | tf_op jit(solution)/shard_map/ppermute | solution.py:33
  35.7 0.0 collective-permute-start.8
  35.7 0.0 collective-permute-done.10
  35.7 2.4 %collective-permute-done.9 = f32[136,128]{1,0:T(8,128)S(1)} collective-permute-done((f32[136,128]{1,0:T(8,128)S(1)}, f32[136,128]{1,0:T(8,128)S(1)}, u32[]{:S(2)}, u32[]{:S(2)}) %collective-permute-start.9) | collective-permute-done | bytes 69664 | tf_op jit(solution)/shard_map/ppermute | solution.py:33
  38.1 3.4 %collective-permute-done.8 = f32[136,128]{1,0:T(8,128)S(1)} collective-permute-done((f32[136,128]{1,0:T(8,128)S(1)}, f32[136,128]{1,0:T(8,128)S(1)}, u32[]{:S(2)}, u32[]{:S(2)}) %collective-permute-start.8) | collective-permute-done | bytes 69664 | tf_op jit(solution)/shard_map/ppermute | solution.py:33
  41.5 2.6 %collective-permute-start.11 = (f32[136,128]{1,0:T(8,128)S(1)}, f32[136,128]{1,0:T(8,128)S(1)}, u32[]{:S(2)}, u32[]{:S(2)}) collective-permute-start(f32[136,128]{1,0:T(8,128)S(1)} %add_add_fusion.1), channel_id=1, source_target_pairs={{0,192},{1,193},{2,194},{3,195},{4,196},{5,197},{6,198},{7,199},{8... | collective-permute-start | bytes 208904 | tf_op jit(solution)/shard_map/ppermute | solution.py:33
  44.1 3.5 %collective-permute-done.11 = f32[136,128]{1,0:T(8,128)S(1)} collective-permute-done((f32[136,128]{1,0:T(8,128)S(1)}, f32[136,128]{1,0:T(8,128)S(1)}, u32[]{:S(2)}, u32[]{:S(2)}) %collective-permute-start.11) | collective-permute-done | bytes 69664 | tf_op jit(solution)/shard_map/ppermute | solution.py:33
  47.6 0.1 broadcast_in_dim.6
  47.7 17.5 %all_to_all.10.own = f32[16,136,128]{2,1,0:T(8,128)S(1)} all-to-all(f32[16,136,128]{2,1,0:T(8,128)S(1)} %broadcast_in_dim.6), channel_id=1, replica_groups=mesh['z'=8,'x'=4,'core'=2,'y'=4] {'x','y'}, dimensions={0} | all-to-all | bytes 2228224 | tf_op jit(solution)/shard_map/all_to_all | solution.py:64
  65.2 5.8 %collective-permute-start.12 = (f32[16,136,128]{2,1,0:T(8,128)S(1)}, f32[16,136,128]{2,1,0:T(8,128)S(1)}, u32[]{:S(2)}, u32[]{:S(2)}) collective-permute-start(f32[16,136,128]{2,1,0:T(8,128)S(1)} %all_to_all.10.own), channel_id=1, source_target_pairs={{0,4},{1,5},{2,6},{3,7},{4,0},{5,1},{6,2},{7,3},{8,12},{9,13},{10,... | collective-permute-start | bytes 3342344 | tf_op jit(solution)/shard_map/ppermute | solution.py:33
  71.0 4.3 %factor.2.inverse = f32[128,128]{1,0:T(8,128)S(1)} custom-call(s32[1]{0:T(128)} %bitcast.core, f32[16,136,128]{2,1,0:T(8,128)S(1)} %all_to_all.10.own), custom_call_target="tpu_custom_call" | custom-call | flops 2097152 | bytes 1000000 | tf_op jit(solution)/shard_map/factor/pallas_call | solution.py:281
  75.3 0.0 collective-permute-done.12.other
  75.3 5.7 %middle.1 = (f32[1024,128]{1,0:T(8,128)S(1)}, f32[8,136,128]{2,1,0:T(8,128)S(1)}, f32[8,136,128]{2,1,0:T(8,128)S(1)}, f32[8,136,128]{2,1,0:T(8,128)S(1)}, f32[8,136,128]{2,1,0:T(8,128)S(1)}) custom-call(s32[1]{0:T(128)} %bitcast.core, s32[1]{0:T(128)} %bitcast.1.x, s32[1]{0:T(128)} %bitcast.2.y, f32[16,136,128]{2,1,0:T(8,128)S(1)} %all_to_all.10.own, ...), custom_call_target="tpu_custom_call" | custom-call | tf_op jit(solution)/shard_map/middle/pallas_call | solution.py:294
  81.0 0.1 collective-permute-start.13
  81.1 0.5 collective-permute-start.14
  81.6 1.4 %collective-permute-done.13 = f32[8,136,128]{2,1,0:T(8,128)S(1)} collective-permute-done((f32[8,136,128]{2,1,0:T(8,128)S(1)}, f32[8,136,128]{2,1,0:T(8,128)S(1)}, u32[]{:S(2)}, u32[]{:S(2)}) %collective-permute-start.13) | collective-permute-done | bytes 557088 | tf_op jit(solution)/shard_map/ppermute | solution.py:33
  83.0 0.1 add.84
  83.1 0.3 collective-permute-start.16
  83.4 0.4 collective-permute-done.14
  83.8 0.1 add.85
  83.9 0.9 collective-permute-start.15
  84.9 1.8 %collective-permute-start.17 = (f32[4,136,128]{2,1,0:T(8,128)S(1)}, f32[4,136,128]{2,1,0:T(8,128)S(1)}, u32[]{:S(2)}, u32[]{:S(2)}) collective-permute-start(f32[4,136,128]{2,1,0:T(8,128)S(1)} %get-tuple-element.42), channel_id=1, source_target_pairs={{0,2},{1,3},{2,0},{3,1},{4,20},{5,21},{6,22},{7,23},{8,10},{9,11},... | collective-permute-start | bytes 835592 | tf_op jit(solution)/shard_map/ppermute | solution.py:33
  86.7 2.2 %collective-permute-done.16 = f32[4,136,128]{2,1,0:T(8,128)S(1)} collective-permute-done((f32[4,136,128]{2,1,0:T(8,128)S(1)}, f32[4,136,128]{2,1,0:T(8,128)S(1)}, u32[]{:S(2)}, u32[]{:S(2)}) %collective-permute-start.16) | collective-permute-done | bytes 278560 | tf_op jit(solution)/shard_map/ppermute | solution.py:33
  88.9 5.0 %collective-permute-done.15 = f32[4,136,128]{2,1,0:T(8,128)S(1)} collective-permute-done((f32[4,136,128]{2,1,0:T(8,128)S(1)}, f32[4,136,128]{2,1,0:T(8,128)S(1)}, u32[]{:S(2)}, u32[]{:S(2)}) %collective-permute-start.15) | collective-permute-done | bytes 278560 | tf_op jit(solution)/shard_map/ppermute | solution.py:33
  93.9 0.1 fusion.1
  94.0 1.0 collective-permute-start.18
  95.0 1.4 %collective-permute-start.20 = (f32[136,128]{1,0:T(8,128)S(1)}, f32[136,128]{1,0:T(8,128)S(1)}, u32[]{:S(2)}, u32[]{:S(2)}) collective-permute-start(f32[136,128]{1,0:T(8,128)S(1)} %get-tuple-element.46), channel_id=1, source_target_pairs={{0,24},{1,25},{2,26},{3,27},{4,7},{5,6},{6,5},{7,4},{8,16},{9,17},... | collective-permute-start | bytes 208904 | tf_op jit(solution)/shard_map/ppermute | solution.py:33
  96.5 0.3 collective-permute-start.19
  96.7 2.0 %collective-permute-done.18 = f32[136,128]{1,0:T(8,128)S(1)} collective-permute-done((f32[136,128]{1,0:T(8,128)S(1)}, f32[136,128]{1,0:T(8,128)S(1)}, u32[]{:S(2)}, u32[]{:S(2)}) %collective-permute-start.18) | collective-permute-done | bytes 69664 | tf_op jit(solution)/shard_map/ppermute | solution.py:33
  98.7 1.0 collective-permute-done.20
  99.8 0.1 collective-permute-done.19
  99.9 0.1 collective-permute-start.23
  100.0 0.6 collective-permute-start.22
  100.6 2.9 %collective-permute-start.21 = (f32[136,128]{1,0:T(8,128)S(1)}, f32[136,128]{1,0:T(8,128)S(1)}, u32[]{:S(2)}, u32[]{:S(2)}) collective-permute-start(f32[136,128]{1,0:T(8,128)S(1)} %fusion.6), channel_id=1, source_target_pairs={{0,96},{1,97},{2,98},{3,99},{4,100},{5,101},{6,102},{7,103},{8,104... | collective-permute-start | bytes 208904 | tf_op jit(solution)/shard_map/ppermute | solution.py:33
  103.6 1.4 fusion.10
  105.0 1.3 collective-permute-done.21
  106.3 2.4 %collective-permute-start.24 = (f32[136,128]{1,0:T(8,128)S(1)}, f32[136,128]{1,0:T(8,128)S(1)}, u32[]{:S(2)}, u32[]{:S(2)}) collective-permute-start(f32[136,128]{1,0:T(8,128)S(1)} %add_add_fusion), channel_id=1, source_target_pairs={{0,192},{1,193},{2,194},{3,195},{4,196},{5,197},{6,198},{7,199},{8... | collective-permute-start | bytes 208904 | tf_op jit(solution)/shard_map/ppermute | solution.py:33
  108.7 3.0 %collective-permute-done.24 = f32[136,128]{1,0:T(8,128)S(1)} collective-permute-done((f32[136,128]{1,0:T(8,128)S(1)}, f32[136,128]{1,0:T(8,128)S(1)}, u32[]{:S(2)}, u32[]{:S(2)}) %collective-permute-start.24) | collective-permute-done | bytes 69664 | tf_op jit(solution)/shard_map/ppermute | solution.py:33
  111.8 0.1 broadcast_in_dim.7
  111.9 16.8 %all_to_all.11.own = f32[16,136,128]{2,1,0:T(8,128)S(1)} all-to-all(f32[16,136,128]{2,1,0:T(8,128)S(1)} %broadcast_in_dim.7), channel_id=1, replica_groups=mesh['z'=8,'x'=4,'core'=2,'y'=4] {'x','y'}, dimensions={0} | all-to-all | bytes 2228224 | tf_op jit(solution)/shard_map/all_to_all | solution.py:64
  128.7 5.7 %collective-permute-start.25 = (f32[16,136,128]{2,1,0:T(8,128)S(1)}, f32[16,136,128]{2,1,0:T(8,128)S(1)}, u32[]{:S(2)}, u32[]{:S(2)}) collective-permute-start(f32[16,136,128]{2,1,0:T(8,128)S(1)} %all_to_all.11.own), channel_id=1, source_target_pairs={{0,4},{1,5},{2,6},{3,7},{4,0},{5,1},{6,2},{7,3},{8,12},{9,13},{10,... | collective-permute-start | bytes 3342344 | tf_op jit(solution)/shard_map/ppermute | solution.py:33
  134.4 4.3 %factor.3.inverse = f32[128,128]{1,0:T(8,128)S(1)} custom-call(s32[1]{0:T(128)} %bitcast.core, f32[16,136,128]{2,1,0:T(8,128)S(1)} %all_to_all.11.own), custom_call_target="tpu_custom_call" | custom-call | flops 2097152 | bytes 1000000 | tf_op jit(solution)/shard_map/factor/pallas_call | solution.py:281
  138.6 2.3 %final.1 = (f32[128,4096]{1,0:T(8,128)}, f32[1024,128]{1,0:T(8,128)}) custom-call(s32[1]{0:T(128)} %bitcast.core, s32[1]{0:T(128)} %bitcast.1.x, s32[1]{0:T(128)} %bitcast.2.y, f32[16,136,128]{2,1,0:T(8,128)S(1)} %all_to_all.11.own, f32[16,136,128]{2,1,0:T(8,128)S(1)} %collective-permute-done.25.other, f32[128,128]{1,0:T(8,128)S(1)} %factor.3.inverse, ...), custom_call_target="tpu_custom_call" | custom-call | tf_op jit(solution)/shard_map/final/pallas_call | solution.py:310
  (23 shorter events, 0.3 us)
Async XLA Ops:
  0.6 1.2 copy-start
  1.9 73.4 %slice-start = ((s8[8388608]{0:T(1024)(128)(4,1)}), s8[4194304]{0:T(1024)(128)(4,1)S(1)}, s32[]{:S(2)}) async-start(s8[8388608]{0:T(1024)(128)(4,1)} %bitcast.32), calls=%async_computation.2 | async-start | bytes 8388608
  9.0 4.9 %collective-permute-start = (f32[8,136,128]{2,1,0:T(8,128)S(1)}, f32[8,136,128]{2,1,0:T(8,128)S(1)}, u32[]{:S(2)}, u32[]{:S(2)}) collective-permute-start(f32[8,136,128]{2,1,0:T(8,128)S(1)} %get-tuple-element.23), channel_id=1, source_target_pairs={{0,4},{1,5},{2,6},{3,7},{4,0},{5,1},{6,2},{7,3},{8,12},{9,13},{10,... | collective-permute-start | bytes 1671176 | tf_op jit(solution)/shard_map/ppermute | solution.py:33
  12.4 2.4 %collective-permute-start.1 = (f32[8,136,128]{2,1,0:T(8,128)S(1)}, f32[8,136,128]{2,1,0:T(8,128)S(1)}, u32[]{:S(2)}, u32[]{:S(2)}) collective-permute-start(f32[8,136,128]{2,1,0:T(8,128)S(1)} %get-tuple-element.25), channel_id=1, source_target_pairs={{0,4},{1,5},{2,6},{3,7},{4,0},{5,1},{6,2},{7,3},{8,12},{9,13},{10,... | collective-permute-start | bytes 1671176 | tf_op jit(solution)/shard_map/ppermute | solution.py:33
  14.0 61.3 %slice-start.1 = ((s8[8388608]{0:T(1024)(128)(4,1)}), s8[4194304]{0:T(1024)(128)(4,1)S(1)}, s32[]{:S(2)}) async-start(s8[8388608]{0:T(1024)(128)(4,1)} %bitcast.32), calls=%async_computation.3 | async-start | bytes 8388608
  14.1 5.8 %collective-permute-start.3 = (f32[4,136,128]{2,1,0:T(8,128)S(1)}, f32[4,136,128]{2,1,0:T(8,128)S(1)}, u32[]{:S(2)}, u32[]{:S(2)}) collective-permute-start(f32[4,136,128]{2,1,0:T(8,128)S(1)} %slice.66), channel_id=1, source_target_pairs={{0,1},{1,0},{2,3},{3,2},{4,12},{5,13},{6,14},{7,15},{8,9},{9,8},{1... | collective-permute-start | bytes 835592 | tf_op jit(solution)/shard_map/ppermute | solution.py:33
  14.9 10.0 %collective-permute-start.2 = (f32[4,136,128]{2,1,0:T(8,128)S(1)}, f32[4,136,128]{2,1,0:T(8,128)S(1)}, u32[]{:S(2)}, u32[]{:S(2)}) collective-permute-start(f32[4,136,128]{2,1,0:T(8,128)S(1)} %get-tuple-element.43), channel_id=1, source_target_pairs={{0,3},{1,2},{2,1},{3,0},{4,28},{5,29},{6,30},{7,31},{8,11},{9,10},... | collective-permute-start | bytes 835592 | tf_op jit(solution)/shard_map/ppermute | solution.py:33
  15.7 9.1 %collective-permute-start.4 = (f32[4,136,128]{2,1,0:T(8,128)S(1)}, f32[4,136,128]{2,1,0:T(8,128)S(1)}, u32[]{:S(2)}, u32[]{:S(2)}) collective-permute-start(f32[4,136,128]{2,1,0:T(8,128)S(1)} %get-tuple-element.44), channel_id=1, source_target_pairs={{0,2},{1,3},{2,0},{3,1},{4,20},{5,21},{6,22},{7,23},{8,10},{9,11},... | collective-permute-start | bytes 835592 | tf_op jit(solution)/shard_map/ppermute | solution.py:33
  24.9 4.8 %collective-permute-start.5 = (f32[136,128]{1,0:T(8,128)S(1)}, f32[136,128]{1,0:T(8,128)S(1)}, u32[]{:S(2)}, u32[]{:S(2)}) collective-permute-start(f32[136,128]{1,0:T(8,128)S(1)} %get-tuple-element.48), channel_id=1, source_target_pairs={{0,16},{1,17},{2,18},{3,19},{4,6},{5,7},{6,4},{7,5},{8,24},{9,25},... | collective-permute-start | bytes 208904 | tf_op jit(solution)/shard_map/ppermute | solution.py:33
  26.5 4.7 %collective-permute-start.7 = (f32[136,128]{1,0:T(8,128)S(1)}, f32[136,128]{1,0:T(8,128)S(1)}, u32[]{:S(2)}, u32[]{:S(2)}) collective-permute-start(f32[136,128]{1,0:T(8,128)S(1)} %get-tuple-element.49), channel_id=1, source_target_pairs={{0,24},{1,25},{2,26},{3,27},{4,7},{5,6},{6,5},{7,4},{8,16},{9,17},... | collective-permute-start | bytes 208904 | tf_op jit(solution)/shard_map/ppermute | solution.py:33
  27.4 3.8 %collective-permute-start.6 = (f32[136,128]{1,0:T(8,128)S(1)}, f32[136,128]{1,0:T(8,128)S(1)}, u32[]{:S(2)}, u32[]{:S(2)}) collective-permute-start(f32[136,128]{1,0:T(8,128)S(1)} %get-tuple-element.50), channel_id=1, source_target_pairs={{0,8},{1,9},{2,10},{3,11},{4,5},{5,4},{6,7},{7,6},{8,0},{9,1},{10,... | collective-permute-start | bytes 208904 | tf_op jit(solution)/shard_map/ppermute | solution.py:33
  31.2 4.4 %collective-permute-start.10 = (f32[136,128]{1,0:T(8,128)S(1)}, f32[136,128]{1,0:T(8,128)S(1)}, u32[]{:S(2)}, u32[]{:S(2)}) collective-permute-start(f32[136,128]{1,0:T(8,128)S(1)} %fusion.9), channel_id=1, source_target_pairs={{0,32},{1,33},{2,34},{3,35},{4,36},{5,37},{6,38},{7,39},{8,40},{9,... | collective-permute-start | bytes 208904 | tf_op jit(solution)/shard_map/ppermute | solution.py:33
  32.7 5.4 %collective-permute-start.9 = (f32[136,128]{1,0:T(8,128)S(1)}, f32[136,128]{1,0:T(8,128)S(1)}, u32[]{:S(2)}, u32[]{:S(2)}) collective-permute-start(f32[136,128]{1,0:T(8,128)S(1)} %fusion.9), channel_id=1, source_target_pairs={{0,64},{1,65},{2,66},{3,67},{4,68},{5,69},{6,70},{7,71},{8,72},{9,... | collective-permute-start | bytes 208904 | tf_op jit(solution)/shard_map/ppermute | solution.py:33
  35.7 5.8 %collective-permute-start.8 = (f32[136,128]{1,0:T(8,128)S(1)}, f32[136,128]{1,0:T(8,128)S(1)}, u32[]{:S(2)}, u32[]{:S(2)}) collective-permute-start(f32[136,128]{1,0:T(8,128)S(1)} %fusion.9), channel_id=1, source_target_pairs={{0,96},{1,97},{2,98},{3,99},{4,100},{5,101},{6,102},{7,103},{8,104... | collective-permute-start | bytes 208904 | tf_op jit(solution)/shard_map/ppermute | solution.py:33
  41.5 6.1 %collective-permute-start.11 = (f32[136,128]{1,0:T(8,128)S(1)}, f32[136,128]{1,0:T(8,128)S(1)}, u32[]{:S(2)}, u32[]{:S(2)}) collective-permute-start(f32[136,128]{1,0:T(8,128)S(1)} %add_add_fusion.1), channel_id=1, source_target_pairs={{0,192},{1,193},{2,194},{3,195},{4,196},{5,197},{6,198},{7,199},{8... | collective-permute-start | bytes 208904 | tf_op jit(solution)/shard_map/ppermute | solution.py:33
  65.2 10.1 %collective-permute-start.12 = (f32[16,136,128]{2,1,0:T(8,128)S(1)}, f32[16,136,128]{2,1,0:T(8,128)S(1)}, u32[]{:S(2)}, u32[]{:S(2)}) collective-permute-start(f32[16,136,128]{2,1,0:T(8,128)S(1)} %all_to_all.10.own), channel_id=1, source_target_pairs={{0,4},{1,5},{2,6},{3,7},{4,0},{5,1},{6,2},{7,3},{8,12},{9,13},{10,... | collective-permute-start | bytes 3342344 | tf_op jit(solution)/shard_map/ppermute | solution.py:33
  81.0 2.0 %collective-permute-start.13 = (f32[8,136,128]{2,1,0:T(8,128)S(1)}, f32[8,136,128]{2,1,0:T(8,128)S(1)}, u32[]{:S(2)}, u32[]{:S(2)}) collective-permute-start(f32[8,136,128]{2,1,0:T(8,128)S(1)} %get-tuple-element.30), channel_id=1, source_target_pairs={{0,4},{1,5},{2,6},{3,7},{4,0},{5,1},{6,2},{7,3},{8,12},{9,13},{10,... | collective-permute-start | bytes 1671176 | tf_op jit(solution)/shard_map/ppermute | solution.py:33
  81.1 2.7 %collective-permute-start.14 = (f32[8,136,128]{2,1,0:T(8,128)S(1)}, f32[8,136,128]{2,1,0:T(8,128)S(1)}, u32[]{:S(2)}, u32[]{:S(2)}) collective-permute-start(f32[8,136,128]{2,1,0:T(8,128)S(1)} %get-tuple-element.32), channel_id=1, source_target_pairs={{0,4},{1,5},{2,6},{3,7},{4,0},{5,1},{6,2},{7,3},{8,12},{9,13},{10,... | collective-permute-start | bytes 1671176 | tf_op jit(solution)/shard_map/ppermute | solution.py:33
  83.1 5.8 %collective-permute-start.16 = (f32[4,136,128]{2,1,0:T(8,128)S(1)}, f32[4,136,128]{2,1,0:T(8,128)S(1)}, u32[]{:S(2)}, u32[]{:S(2)}) collective-permute-start(f32[4,136,128]{2,1,0:T(8,128)S(1)} %slice.74), channel_id=1, source_target_pairs={{0,1},{1,0},{2,3},{3,2},{4,12},{5,13},{6,14},{7,15},{8,9},{9,8},{1... | collective-permute-start | bytes 835592 | tf_op jit(solution)/shard_map/ppermute | solution.py:33
  83.9 10.0 %collective-permute-start.15 = (f32[4,136,128]{2,1,0:T(8,128)S(1)}, f32[4,136,128]{2,1,0:T(8,128)S(1)}, u32[]{:S(2)}, u32[]{:S(2)}) collective-permute-start(f32[4,136,128]{2,1,0:T(8,128)S(1)} %get-tuple-element.41), channel_id=1, source_target_pairs={{0,3},{1,2},{2,1},{3,0},{4,28},{5,29},{6,30},{7,31},{8,11},{9,10},... | collective-permute-start | bytes 835592 | tf_op jit(solution)/shard_map/ppermute | solution.py:33
  84.9 9.0 %collective-permute-start.17 = (f32[4,136,128]{2,1,0:T(8,128)S(1)}, f32[4,136,128]{2,1,0:T(8,128)S(1)}, u32[]{:S(2)}, u32[]{:S(2)}) collective-permute-start(f32[4,136,128]{2,1,0:T(8,128)S(1)} %get-tuple-element.42), channel_id=1, source_target_pairs={{0,2},{1,3},{2,0},{3,1},{4,20},{5,21},{6,22},{7,23},{8,10},{9,11},... | collective-permute-start | bytes 835592 | tf_op jit(solution)/shard_map/ppermute | solution.py:33
  94.0 4.8 %collective-permute-start.18 = (f32[136,128]{1,0:T(8,128)S(1)}, f32[136,128]{1,0:T(8,128)S(1)}, u32[]{:S(2)}, u32[]{:S(2)}) collective-permute-start(f32[136,128]{1,0:T(8,128)S(1)} %get-tuple-element.45), channel_id=1, source_target_pairs={{0,16},{1,17},{2,18},{3,19},{4,6},{5,7},{6,4},{7,5},{8,24},{9,25},... | collective-permute-start | bytes 208904 | tf_op jit(solution)/shard_map/ppermute | solution.py:33
  95.0 4.8 %collective-permute-start.20 = (f32[136,128]{1,0:T(8,128)S(1)}, f32[136,128]{1,0:T(8,128)S(1)}, u32[]{:S(2)}, u32[]{:S(2)}) collective-permute-start(f32[136,128]{1,0:T(8,128)S(1)} %get-tuple-element.46), channel_id=1, source_target_pairs={{0,24},{1,25},{2,26},{3,27},{4,7},{5,6},{6,5},{7,4},{8,16},{9,17},... | collective-permute-start | bytes 208904 | tf_op jit(solution)/shard_map/ppermute | solution.py:33
  96.5 3.5 %collective-permute-start.19 = (f32[136,128]{1,0:T(8,128)S(1)}, f32[136,128]{1,0:T(8,128)S(1)}, u32[]{:S(2)}, u32[]{:S(2)}) collective-permute-start(f32[136,128]{1,0:T(8,128)S(1)} %get-tuple-element.47), channel_id=1, source_target_pairs={{0,8},{1,9},{2,10},{3,11},{4,5},{5,4},{6,7},{7,6},{8,0},{9,1},{10,... | collective-permute-start | bytes 208904 | tf_op jit(solution)/shard_map/ppermute | solution.py:33
  99.9 5.0 %collective-permute-start.23 = (f32[136,128]{1,0:T(8,128)S(1)}, f32[136,128]{1,0:T(8,128)S(1)}, u32[]{:S(2)}, u32[]{:S(2)}) collective-permute-start(f32[136,128]{1,0:T(8,128)S(1)} %fusion.6), channel_id=1, source_target_pairs={{0,32},{1,33},{2,34},{3,35},{4,36},{5,37},{6,38},{7,39},{8,40},{9,... | collective-permute-start | bytes 208904 | tf_op jit(solution)/shard_map/ppermute | solution.py:33
  100.0 4.9 %collective-permute-start.22 = (f32[136,128]{1,0:T(8,128)S(1)}, f32[136,128]{1,0:T(8,128)S(1)}, u32[]{:S(2)}, u32[]{:S(2)}) collective-permute-start(f32[136,128]{1,0:T(8,128)S(1)} %fusion.6), channel_id=1, source_target_pairs={{0,64},{1,65},{2,66},{3,67},{4,68},{5,69},{6,70},{7,71},{8,72},{9,... | collective-permute-start | bytes 208904 | tf_op jit(solution)/shard_map/ppermute | solution.py:33
  100.6 5.7 %collective-permute-start.21 = (f32[136,128]{1,0:T(8,128)S(1)}, f32[136,128]{1,0:T(8,128)S(1)}, u32[]{:S(2)}, u32[]{:S(2)}) collective-permute-start(f32[136,128]{1,0:T(8,128)S(1)} %fusion.6), channel_id=1, source_target_pairs={{0,96},{1,97},{2,98},{3,99},{4,100},{5,101},{6,102},{7,103},{8,104... | collective-permute-start | bytes 208904 | tf_op jit(solution)/shard_map/ppermute | solution.py:33
  106.3 5.5 %collective-permute-start.24 = (f32[136,128]{1,0:T(8,128)S(1)}, f32[136,128]{1,0:T(8,128)S(1)}, u32[]{:S(2)}, u32[]{:S(2)}) collective-permute-start(f32[136,128]{1,0:T(8,128)S(1)} %add_add_fusion), channel_id=1, source_target_pairs={{0,192},{1,193},{2,194},{3,195},{4,196},{5,197},{6,198},{7,199},{8... | collective-permute-start | bytes 208904 | tf_op jit(solution)/shard_map/ppermute | solution.py:33
  128.7 9.9 %collective-permute-start.25 = (f32[16,136,128]{2,1,0:T(8,128)S(1)}, f32[16,136,128]{2,1,0:T(8,128)S(1)}, u32[]{:S(2)}, u32[]{:S(2)}) collective-permute-start(f32[16,136,128]{2,1,0:T(8,128)S(1)} %all_to_all.11.own), channel_id=1, source_target_pairs={{0,4},{1,5},{2,6},{3,7},{4,0},{5,1},{6,2},{7,3},{8,12},{9,13},{10,... | collective-permute-start | bytes 3342344 | tf_op jit(solution)/shard_map/ppermute | solution.py:33

commit v4 on v3

--- a/solution.py
+++ b/solution.py
@@ -87,7 +87,7 @@
     return rough * (2.0 - value * rough)
 
 
-def inverse_factor(gram):
+def inverse_factor(gram, panel, spreads):
     row = lax.broadcasted_iota(jnp.int32, (K, K), 0)
     column = lax.broadcasted_iota(jnp.int32, (K, K), 1)
     diagonal = jnp.where(row == column, gram, 0.0)
@@ -105,10 +105,17 @@
         k = 8 * g0
         mine = groups[g0]
         columns = [spread(mine, k + t) for t in range(8)]
-        s = {(i, j): jnp.broadcast_to(columns[j][i : i + 1], (8, K)) for i in range(8) for j in range(i + 1)}
+        panel[...] = mine
+        for j in range(8):
+            spreads[8 * j : 8 * j + 8, :] = columns[j]
+        s = {
+            (i, j): jnp.broadcast_to(spreads[8 * j + i : 8 * j + i + 1, :], (8, K))
+            for i in range(8)
+            for j in range(i + 1)
+        }
         inside = (lane >= k) & (lane < k + 8)
         e = [
-            jnp.where(inside, jnp.where(lane == k + t, 1.0, 0.0), jnp.broadcast_to(mine[t : t + 1], (8, K)))
+            jnp.where(inside, jnp.where(lane == k + t, 1.0, 0.0), jnp.broadcast_to(panel[t : t + 1, :], (8, K)))
             for t in range(8)
         ]
         u, v, done = [None] * 8, {}, [None] * 8
@@ -187,12 +194,17 @@
     return copies
 
 
-def make_message(place, held, tall, give, keep, turned, gram):
-    core, x, y = place
+def prepare(tall, turned, gram):
     gram[...] = three_term_gram(tall[...])
     turned[...] = jnp.concatenate(two_terms(tall[...]), axis=1).T
+
+
+def make_message(place, held, turned, gram, give, keep):
+    core, x, y = place
     for a in (2, 3, 0, 1):
         for refs, side in ((give, 1 - core), (keep, core)):
+            if refs is None:
+                continue
             ref = refs[0] if a >= 2 else refs[1]
             p = a ^ jnp.where(side == 0, y, x)
             q = jnp.where(side == 0, x, y)
@@ -211,15 +223,16 @@
         copies[b].wait()
         rows = pl.ds(b * BLOCK, BLOCK)
         first[rows, :] = quick_dot(held[rows, :], sketch[...])
-    make_message((core[0], x[0], y[0]), held, first, (give2, give0), (keep2, keep0), turned, gram)
-
-
-def factor_kernel(core, own, inverse):
+    prepare(first, turned, gram)
+    make_message((core[0], x[0], y[0]), held, turned, gram, (give2, give0), (keep2, keep0))
+
+
+def factor_kernel(core, own, inverse, panel, spreads):
     rows = [own[place_of(chunk, core[0]), K:, :] for chunk in range(PLANE)]
-    inverse[...] = inverse_factor(jnp.concatenate(rows, axis=0))
-
-
-def middle_kernel(core, x, y, own, other, inverse, held, second, give2, give0, keep2, keep0, back, turned, gram):
+    inverse[...] = inverse_factor(jnp.concatenate(rows, axis=0), panel, spreads)
+
+
+def middle_kernel(core, x, y, own, other, inverse, held, second, turned, gram, give2, give0, back):
     scaled = inverse[...] * (1.0 / ROOT_ROWS)
 
     def store(start, terms):
@@ -229,7 +242,12 @@
     for b in range(STEPS):
         rows = pl.ds(b * BLOCK, BLOCK)
         second[rows, :] = quick_dot(held[rows, :], back[...], ((1,), (1,)))
-    make_message((core[0], x[0], y[0]), held, second, (give2, give0), (keep2, keep0), turned, gram)
+    prepare(second, turned, gram)
+    make_message((core[0], x[0], y[0]), held, turned, gram, (give2, give0), None)
+
+
+def keep_kernel(core, x, y, held, turned, gram, keep2, keep0):
+    make_message((core[0], x[0], y[0]), held, turned, gram, None, (keep2, keep0))
 
 
 def final_kernel(core, x, y, own, other, inverse, tall, projected, basis, wide, narrow, sent):
@@ -283,6 +301,7 @@
         out_shape=SQUARE,
         in_specs=[SM, VM],
         out_specs=VM,
+        scratch_shapes=[pltpu.VMEM((8, K), jnp.float32), pltpu.VMEM((64, K), jnp.float32)],
         compiler_params=params(),
         cost_estimate=pl.CostEstimate(flops=K**3, bytes_accessed=10**6, transcendentals=0),
         name="factor",
@@ -293,17 +312,31 @@
     rows = held.shape[0]
     return pl.pallas_call(
         middle_kernel,
-        out_shape=(jax.ShapeDtypeStruct((rows, K), jnp.float32), PART, PART, PART, PART),
+        out_shape=(
+            jax.ShapeDtypeStruct((rows, K), jnp.float32),
+            jax.ShapeDtypeStruct((2 * K, rows), jnp.bfloat16),
+            SQUARE,
+            PART,
+            PART,
+        ),
         in_specs=[SM, SM, SM, VM, VM, VM, VM],
         out_specs=(VM,) * 5,
-        scratch_shapes=[
-            pltpu.VMEM((K, D), jnp.bfloat16),
-            pltpu.VMEM((2 * K, rows), jnp.bfloat16),
-            pltpu.VMEM((K, K), jnp.float32),
-        ],
+        scratch_shapes=[pltpu.VMEM((K, D), jnp.bfloat16)],
         compiler_params=params(),
         name="middle",
     )(*place, own, other, inverse, held)
+
+
+def keep_call(place, held, turned, gram):
+    return pl.pallas_call(
+        keep_kernel,
+        out_shape=(PART, PART),
+        in_specs=[SM, SM, SM, VM, VM, VM],
+        out_specs=(VM, VM),
+        compiler_params=params(),
+        cost_estimate=pl.CostEstimate(flops=2 * K * held.size, bytes_accessed=10**6, transcendentals=0),
+        name="keep",
+    )(*place, held, turned, gram)
 
 
 def final_call(place, own, other, inverse, tall):
@@ -327,9 +360,10 @@
     first, *parts = start_call(place, data, sketch)
     own, other, _ = sum_everywhere(parts[:2], parts[2:])
     inverse = factor_call(place[0], own)
-    second, *parts = middle_call(place, own, other, inverse, data)
+    second, turned, gram, *give = middle_call(place, own, other, inverse, data)
+    keep = keep_call(place, data, turned, gram)
     first_basis = exact_dot(first, ROOT_ROWS * inverse, ((1,), (1,)))
-    own, other, first_basis = sum_everywhere(parts[:2], parts[2:], first_basis)
+    own, other, first_basis = sum_everywhere(give, keep, first_basis)
     inverse = factor_call(place[0], own)
     projected, basis = final_call(place, own, other, inverse, second)
     return (first_basis, basis, projected)

time: 141 us -> 138 us (0.979)
  Pallas kernels: 23.6 us -> 21.9 us
    pallas_call x2, Pallas kernels: 8.51 us -> 6.64 us  [factor_call(): pl.pallas_call(factor_kernel, out_shape=SQUARE, in_specs=[SM, VM], out_sp...]
where the time goes in v4:
time: 138 us
  starting transfers between devices  40.1 us (29%)
  waiting for transfers between devices  37.5 us (27%)
  blocking collectives  34.3 us (25%)
  Pallas kernels  21.9 us (16%)
  local copies, waits for them, and re-layouts  1.52 us (1%)
    ppermute x26, starting transfers between devices, exchange(): return lax.ppermute(value, AXES, pairs)  40.1 us
    ppermute x26, waiting for transfers between devices, exchange(): return lax.ppermute(value, AXES, pairs)  37.5 us
    all_to_all x2, blocking collectives, sum_everywhere(): lax.all_to_all(jnp.broadcast_to(part, (PLANE,) + part.shape), ('x', 'y'),...  34.3 us
    pallas_call x1, Pallas kernels, start_call(): pl.pallas_call(start_kernel, out_shape=(jax.ShapeDtypeStruct((rows, K), j...  7.17 us
    pallas_call x2, Pallas kernels, factor_call(): pl.pallas_call(factor_kernel, out_shape=SQUARE, in_specs=[SM, VM], out_sp...  6.64 us
    pallas_call x1, Pallas kernels, middle_call(): pl.pallas_call(middle_kernel, out_shape=(jax.ShapeDtypeStruct((rows, K),...  4.56 us
  transfers between devices with their start and end apart: 26, of which 18 were waited for; matrix products, arithmetic and copies ran while one was open for 1% of the time, Pallas kernels for 6%

profile of v4, /device:TPU:1, one launch (start us, length us, event | category | flops | bytes accessed | tf_op | source)
XLA Modules:
  0.0 138.3 jit_solution(7191554288485909302)
XLA Ops:
  0.6 1.2 copy-done
  1.9 7.2 %start.1 = (f32[1024,128]{1,0:T(8,128)S(1)}, f32[8,136,128]{2,1,0:T(8,128)S(1)}, f32[8,136,128]{2,1,0:T(8,128)S(1)}, f32[8,136,128]{2,1,0:T(8,128)S(1)}, f32[8,136,128]{2,1,0:T(8,128)S(1)}) custom-call(s32[1]{0:T(128)} %bitcast.core, s32[1]{0:T(128)} %bitcast.1.x, s32[1]{0:T(128)} %bitcast.2.y, bf16[1024,4096]{1,0:T(8,128)(2,1)} %held.3, ...), custom_call_target="tpu_custom_call" | custom-call | tf_op jit(solution)/shard_map/start/pallas_call | solution.py:282
  9.0 3.3 %collective-permute-start = (f32[8,136,128]{2,1,0:T(8,128)S(1)}, f32[8,136,128]{2,1,0:T(8,128)S(1)}, u32[]{:S(2)}, u32[]{:S(2)}) collective-permute-start(f32[8,136,128]{2,1,0:T(8,128)S(1)} %get-tuple-element.25), channel_id=1, source_target_pairs={{0,4},{1,5},{2,6},{3,7},{4,0},{5,1},{6,2},{7,3},{8,12},{9,13},{10,... | collective-permute-start | bytes 1671176 | tf_op jit(solution)/shard_map/ppermute | solution.py:33
  12.4 0.1 collective-permute-start.1
  12.5 1.5 %collective-permute-done = f32[8,136,128]{2,1,0:T(8,128)S(1)} collective-permute-done((f32[8,136,128]{2,1,0:T(8,128)S(1)}, f32[8,136,128]{2,1,0:T(8,128)S(1)}, u32[]{:S(2)}, u32[]{:S(2)}) %collective-permute-start) | collective-permute-done | bytes 557088 | tf_op jit(solution)/shard_map/ppermute | solution.py:33
  14.0 0.1 add.72
  14.1 0.1 collective-permute-start.3
  14.2 0.6 collective-permute-done.1
  14.7 0.1 add.73
  14.9 0.8 collective-permute-start.2
  15.7 1.9 %collective-permute-start.4 = (f32[4,136,128]{2,1,0:T(8,128)S(1)}, f32[4,136,128]{2,1,0:T(8,128)S(1)}, u32[]{:S(2)}, u32[]{:S(2)}) collective-permute-start(f32[4,136,128]{2,1,0:T(8,128)S(1)} %get-tuple-element.48), channel_id=1, source_target_pairs={{0,2},{1,3},{2,0},{3,1},{4,20},{5,21},{6,22},{7,23},{8,10},{9,11},... | collective-permute-start | bytes 835592 | tf_op jit(solution)/shard_map/ppermute | solution.py:33
  17.6 2.2 %collective-permute-done.3 = f32[4,136,128]{2,1,0:T(8,128)S(1)} collective-permute-done((f32[4,136,128]{2,1,0:T(8,128)S(1)}, f32[4,136,128]{2,1,0:T(8,128)S(1)}, u32[]{:S(2)}, u32[]{:S(2)}) %collective-permute-start.3) | collective-permute-done | bytes 278560 | tf_op jit(solution)/shard_map/ppermute | solution.py:33
  19.8 5.0 %collective-permute-done.2 = f32[4,136,128]{2,1,0:T(8,128)S(1)} collective-permute-done((f32[4,136,128]{2,1,0:T(8,128)S(1)}, f32[4,136,128]{2,1,0:T(8,128)S(1)}, u32[]{:S(2)}, u32[]{:S(2)}) %collective-permute-start.2) | collective-permute-done | bytes 278560 | tf_op jit(solution)/shard_map/ppermute | solution.py:33
  24.8 0.0 collective-permute-done.4
  24.9 0.1 fusion.3
  24.9 1.6 %collective-permute-start.5 = (f32[136,128]{1,0:T(8,128)S(1)}, f32[136,128]{1,0:T(8,128)S(1)}, u32[]{:S(2)}, u32[]{:S(2)}) collective-permute-start(f32[136,128]{1,0:T(8,128)S(1)} %get-tuple-element.52), channel_id=1, source_target_pairs={{0,16},{1,17},{2,18},{3,19},{4,6},{5,7},{6,4},{7,5},{8,24},{9,25},... | collective-permute-start | bytes 208904 | tf_op jit(solution)/shard_map/ppermute | solution.py:33
  26.5 0.9 collective-permute-start.7
  27.4 0.2 collective-permute-start.6
  27.7 2.0 %collective-permute-done.5 = f32[136,128]{1,0:T(8,128)S(1)} collective-permute-done((f32[136,128]{1,0:T(8,128)S(1)}, f32[136,128]{1,0:T(8,128)S(1)}, u32[]{:S(2)}, u32[]{:S(2)}) %collective-permute-start.5) | collective-permute-done | bytes 69664 | tf_op jit(solution)/shard_map/ppermute | solution.py:33
  29.7 1.5 %collective-permute-done.7 = f32[136,128]{1,0:T(8,128)S(1)} collective-permute-done((f32[136,128]{1,0:T(8,128)S(1)}, f32[136,128]{1,0:T(8,128)S(1)}, u32[]{:S(2)}, u32[]{:S(2)}) %collective-permute-start.7) | collective-permute-done | bytes 69664 | tf_op jit(solution)/shard_map/ppermute | solution.py:33
  31.2 0.0 collective-permute-done.6
  31.2 1.4 %collective-permute-start.10 = (f32[136,128]{1,0:T(8,128)S(1)}, f32[136,128]{1,0:T(8,128)S(1)}, u32[]{:S(2)}, u32[]{:S(2)}) collective-permute-start(f32[136,128]{1,0:T(8,128)S(1)} %fusion.9), channel_id=1, source_target_pairs={{0,32},{1,33},{2,34},{3,35},{4,36},{5,37},{6,38},{7,39},{8,40},{9,... | collective-permute-start | bytes 208904 | tf_op jit(solution)/shard_map/ppermute | solution.py:33
  32.7 3.0 %collective-permute-start.9 = (f32[136,128]{1,0:T(8,128)S(1)}, f32[136,128]{1,0:T(8,128)S(1)}, u32[]{:S(2)}, u32[]{:S(2)}) collective-permute-start(f32[136,128]{1,0:T(8,128)S(1)} %fusion.9), channel_id=1, source_target_pairs={{0,64},{1,65},{2,66},{3,67},{4,68},{5,69},{6,70},{7,71},{8,72},{9,... | collective-permute-start | bytes 208904 | tf_op jit(solution)/shard_map/ppermute | solution.py:33
  35.7 0.0 collective-permute-start.8
  35.7 2.4 %collective-permute-done.9 = f32[136,128]{1,0:T(8,128)S(1)} collective-permute-done((f32[136,128]{1,0:T(8,128)S(1)}, f32[136,128]{1,0:T(8,128)S(1)}, u32[]{:S(2)}, u32[]{:S(2)}) %collective-permute-start.9) | collective-permute-done | bytes 69664 | tf_op jit(solution)/shard_map/ppermute | solution.py:33
  38.1 3.4 %collective-permute-done.8 = f32[136,128]{1,0:T(8,128)S(1)} collective-permute-done((f32[136,128]{1,0:T(8,128)S(1)}, f32[136,128]{1,0:T(8,128)S(1)}, u32[]{:S(2)}, u32[]{:S(2)}) %collective-permute-start.8) | collective-permute-done | bytes 69664 | tf_op jit(solution)/shard_map/ppermute | solution.py:33
  41.5 2.6 %collective-permute-start.11 = (f32[136,128]{1,0:T(8,128)S(1)}, f32[136,128]{1,0:T(8,128)S(1)}, u32[]{:S(2)}, u32[]{:S(2)}) collective-permute-start(f32[136,128]{1,0:T(8,128)S(1)} %add_add_fusion.1), channel_id=1, source_target_pairs={{0,192},{1,193},{2,194},{3,195},{4,196},{5,197},{6,198},{7,199},{8... | collective-permute-start | bytes 208904 | tf_op jit(solution)/shard_map/ppermute | solution.py:33
  44.1 3.5 %collective-permute-done.11 = f32[136,128]{1,0:T(8,128)S(1)} collective-permute-done((f32[136,128]{1,0:T(8,128)S(1)}, f32[136,128]{1,0:T(8,128)S(1)}, u32[]{:S(2)}, u32[]{:S(2)}) %collective-permute-start.11) | collective-permute-done | bytes 69664 | tf_op jit(solution)/shard_map/ppermute | solution.py:33
  47.6 0.1 broadcast_in_dim.6
  47.7 17.5 %all_to_all.10.own = f32[16,136,128]{2,1,0:T(8,128)S(1)} all-to-all(f32[16,136,128]{2,1,0:T(8,128)S(1)} %broadcast_in_dim.6), channel_id=1, replica_groups=mesh['z'=8,'x'=4,'core'=2,'y'=4] {'x','y'}, dimensions={0} | all-to-all | bytes 2228224 | tf_op jit(solution)/shard_map/all_to_all | solution.py:64
  65.2 5.8 %collective-permute-start.12 = (f32[16,136,128]{2,1,0:T(8,128)S(1)}, f32[16,136,128]{2,1,0:T(8,128)S(1)}, u32[]{:S(2)}, u32[]{:S(2)}) collective-permute-start(f32[16,136,128]{2,1,0:T(8,128)S(1)} %all_to_all.10.own), channel_id=1, source_target_pairs={{0,4},{1,5},{2,6},{3,7},{4,0},{5,1},{6,2},{7,3},{8,12},{9,13},{10,... | collective-permute-start | bytes 3342344 | tf_op jit(solution)/shard_map/ppermute | solution.py:33
  71.0 3.3 %factor.2.inverse = f32[128,128]{1,0:T(8,128)S(1)} custom-call(s32[1]{0:T(128)} %bitcast.core, f32[16,136,128]{2,1,0:T(8,128)S(1)} %all_to_all.10.own), custom_call_target="tpu_custom_call" | custom-call | flops 2097152 | bytes 1000000 | tf_op jit(solution)/shard_map/factor/pallas_call | solution.py:299
  74.4 4.6 %middle.1 = (f32[1024,128]{1,0:T(8,128)S(1)}, bf16[256,1024]{1,0:T(8,128)(2,1)S(1)}, f32[128,128]{1,0:T(8,128)S(1)}, f32[8,136,128]{2,1,0:T(8,128)S(1)}, f32[8,136,128]{2,1,0:T(8,128)S(1)}) custom-call(s32[1]{0:T(128)} %bitcast.core, s32[1]{0:T(128)} %bitcast.1.x, s32[1]{0:T(128)} %bitcast.2.y, f32[16,136,128]{2,1,0:T(8,128)S(1)} %all_to_all.10.own, ...), custom_call_target="tpu_custom_call" | custom-call | tf_op jit(solution)/shard_map/middle/pallas_call | solution.py:313
  78.9 0.1 collective-permute-start.13
  79.0 0.5 collective-permute-start.14
  79.5 1.3 keep.1
  80.8 0.2 collective-permute-done.13
  81.0 0.1 add.84
  81.1 0.3 collective-permute-start.16
  81.4 0.4 collective-permute-done.14
  81.8 0.1 add.85
  81.9 0.9 collective-permute-start.15
  82.8 1.8 %collective-permute-start.17 = (f32[4,136,128]{2,1,0:T(8,128)S(1)}, f32[4,136,128]{2,1,0:T(8,128)S(1)}, u32[]{:S(2)}, u32[]{:S(2)}) collective-permute-start(f32[4,136,128]{2,1,0:T(8,128)S(1)} %get-tuple-element.46), channel_id=1, source_target_pairs={{0,2},{1,3},{2,0},{3,1},{4,20},{5,21},{6,22},{7,23},{8,10},{9,11},... | collective-permute-start | bytes 835592 | tf_op jit(solution)/shard_map/ppermute | solution.py:33
  84.6 2.2 %collective-permute-done.16 = f32[4,136,128]{2,1,0:T(8,128)S(1)} collective-permute-done((f32[4,136,128]{2,1,0:T(8,128)S(1)}, f32[4,136,128]{2,1,0:T(8,128)S(1)}, u32[]{:S(2)}, u32[]{:S(2)}) %collective-permute-start.16) | collective-permute-done | bytes 278560 | tf_op jit(solution)/shard_map/ppermute | solution.py:33
  86.8 5.0 %collective-permute-done.15 = f32[4,136,128]{2,1,0:T(8,128)S(1)} collective-permute-done((f32[4,136,128]{2,1,0:T(8,128)S(1)}, f32[4,136,128]{2,1,0:T(8,128)S(1)}, u32[]{:S(2)}, u32[]{:S(2)}) %collective-permute-start.15) | collective-permute-done | bytes 278560 | tf_op jit(solution)/shard_map/ppermute | solution.py:33
  91.8 0.1 fusion.1
  91.9 1.0 collective-permute-start.18
  93.0 1.4 %collective-permute-start.20 = (f32[136,128]{1,0:T(8,128)S(1)}, f32[136,128]{1,0:T(8,128)S(1)}, u32[]{:S(2)}, u32[]{:S(2)}) collective-permute-start(f32[136,128]{1,0:T(8,128)S(1)} %get-tuple-element.50), channel_id=1, source_target_pairs={{0,24},{1,25},{2,26},{3,27},{4,7},{5,6},{6,5},{7,4},{8,16},{9,17},... | collective-permute-start | bytes 208904 | tf_op jit(solution)/shard_map/ppermute | solution.py:33
  94.4 0.3 collective-permute-start.19
  94.7 2.0 %collective-permute-done.18 = f32[136,128]{1,0:T(8,128)S(1)} collective-permute-done((f32[136,128]{1,0:T(8,128)S(1)}, f32[136,128]{1,0:T(8,128)S(1)}, u32[]{:S(2)}, u32[]{:S(2)}) %collective-permute-start.18) | collective-permute-done | bytes 69664 | tf_op jit(solution)/shard_map/ppermute | solution.py:33
  96.7 1.0 collective-permute-done.20
  97.7 0.1 collective-permute-done.19
  97.9 0.3 collective-permute-start.23
  98.2 0.6 collective-permute-start.22
  98.8 2.9 %collective-permute-start.21 = (f32[136,128]{1,0:T(8,128)S(1)}, f32[136,128]{1,0:T(8,128)S(1)}, u32[]{:S(2)}, u32[]{:S(2)}) collective-permute-start(f32[136,128]{1,0:T(8,128)S(1)} %fusion.6), channel_id=1, source_target_pairs={{0,96},{1,97},{2,98},{3,99},{4,100},{5,101},{6,102},{7,103},{8,104... | collective-permute-start | bytes 208904 | tf_op jit(solution)/shard_map/ppermute | solution.py:33
  101.7 1.4 fusion.10
  103.1 1.3 collective-permute-done.21
  104.5 2.4 %collective-permute-start.24 = (f32[136,128]{1,0:T(8,128)S(1)}, f32[136,128]{1,0:T(8,128)S(1)}, u32[]{:S(2)}, u32[]{:S(2)}) collective-permute-start(f32[136,128]{1,0:T(8,128)S(1)} %add_add_fusion), channel_id=1, source_target_pairs={{0,192},{1,193},{2,194},{3,195},{4,196},{5,197},{6,198},{7,199},{8... | collective-permute-start | bytes 208904 | tf_op jit(solution)/shard_map/ppermute | solution.py:33
  106.9 3.0 %collective-permute-done.24 = f32[136,128]{1,0:T(8,128)S(1)} collective-permute-done((f32[136,128]{1,0:T(8,128)S(1)}, f32[136,128]{1,0:T(8,128)S(1)}, u32[]{:S(2)}, u32[]{:S(2)}) %collective-permute-start.24) | collective-permute-done | bytes 69664 | tf_op jit(solution)/shard_map/ppermute | solution.py:33
  110.0 0.1 broadcast_in_dim.7
  110.0 16.8 %all_to_all.11.own = f32[16,136,128]{2,1,0:T(8,128)S(1)} all-to-all(f32[16,136,128]{2,1,0:T(8,128)S(1)} %broadcast_in_dim.7), channel_id=1, replica_groups=mesh['z'=8,'x'=4,'core'=2,'y'=4] {'x','y'}, dimensions={0} | all-to-all | bytes 2228224 | tf_op jit(solution)/shard_map/all_to_all | solution.py:64
  126.9 5.7 %collective-permute-start.25 = (f32[16,136,128]{2,1,0:T(8,128)S(1)}, f32[16,136,128]{2,1,0:T(8,128)S(1)}, u32[]{:S(2)}, u32[]{:S(2)}) collective-permute-start(f32[16,136,128]{2,1,0:T(8,128)S(1)} %all_to_all.11.own), channel_id=1, source_target_pairs={{0,4},{1,5},{2,6},{3,7},{4,0},{5,1},{6,2},{7,3},{8,12},{9,13},{10,... | collective-permute-start | bytes 3342344 | tf_op jit(solution)/shard_map/ppermute | solution.py:33
  132.5 3.3 %factor.3.inverse = f32[128,128]{1,0:T(8,128)S(1)} custom-call(s32[1]{0:T(128)} %bitcast.core, f32[16,136,128]{2,1,0:T(8,128)S(1)} %all_to_all.11.own), custom_call_target="tpu_custom_call" | custom-call | flops 2097152 | bytes 1000000 | tf_op jit(solution)/shard_map/factor/pallas_call | solution.py:299
  135.9 2.3 %final.1 = (f32[128,4096]{1,0:T(8,128)}, f32[1024,128]{1,0:T(8,128)}) custom-call(s32[1]{0:T(128)} %bitcast.core, s32[1]{0:T(128)} %bitcast.1.x, s32[1]{0:T(128)} %bitcast.2.y, f32[16,136,128]{2,1,0:T(8,128)S(1)} %all_to_all.11.own, f32[16,136,128]{2,1,0:T(8,128)S(1)} %collective-permute-done.25.other, f32[128,128]{1,0:T(8,128)S(1)} %factor.3.inverse, ...), custom_call_target="tpu_custom_call" | custom-call | tf_op jit(solution)/shard_map/final/pallas_call | solution.py:343
  (24 shorter events, 0.3 us)
Async XLA Ops:
  0.6 1.2 copy-start
  1.9 72.5 %slice-start = ((s8[8388608]{0:T(1024)(128)(4,1)}), s8[4194304]{0:T(1024)(128)(4,1)S(1)}, s32[]{:S(2)}) async-start(s8[8388608]{0:T(1024)(128)(4,1)} %bitcast.32), calls=%async_computation.2 | async-start | bytes 8388608
  9.0 4.9 %collective-permute-start = (f32[8,136,128]{2,1,0:T(8,128)S(1)}, f32[8,136,128]{2,1,0:T(8,128)S(1)}, u32[]{:S(2)}, u32[]{:S(2)}) collective-permute-start(f32[8,136,128]{2,1,0:T(8,128)S(1)} %get-tuple-element.25), channel_id=1, source_target_pairs={{0,4},{1,5},{2,6},{3,7},{4,0},{5,1},{6,2},{7,3},{8,12},{9,13},{10,... | collective-permute-start | bytes 1671176 | tf_op jit(solution)/shard_map/ppermute | solution.py:33
  12.4 2.4 %collective-permute-start.1 = (f32[8,136,128]{2,1,0:T(8,128)S(1)}, f32[8,136,128]{2,1,0:T(8,128)S(1)}, u32[]{:S(2)}, u32[]{:S(2)}) collective-permute-start(f32[8,136,128]{2,1,0:T(8,128)S(1)} %get-tuple-element.27), channel_id=1, source_target_pairs={{0,4},{1,5},{2,6},{3,7},{4,0},{5,1},{6,2},{7,3},{8,12},{9,13},{10,... | collective-permute-start | bytes 1671176 | tf_op jit(solution)/shard_map/ppermute | solution.py:33
  14.0 60.4 %slice-start.1 = ((s8[8388608]{0:T(1024)(128)(4,1)}), s8[4194304]{0:T(1024)(128)(4,1)S(1)}, s32[]{:S(2)}) async-start(s8[8388608]{0:T(1024)(128)(4,1)} %bitcast.32), calls=%async_computation.3 | async-start | bytes 8388608
  14.1 5.8 %collective-permute-start.3 = (f32[4,136,128]{2,1,0:T(8,128)S(1)}, f32[4,136,128]{2,1,0:T(8,128)S(1)}, u32[]{:S(2)}, u32[]{:S(2)}) collective-permute-start(f32[4,136,128]{2,1,0:T(8,128)S(1)} %slice.66), channel_id=1, source_target_pairs={{0,1},{1,0},{2,3},{3,2},{4,12},{5,13},{6,14},{7,15},{8,9},{9,8},{1... | collective-permute-start | bytes 835592 | tf_op jit(solution)/shard_map/ppermute | solution.py:33
  14.9 10.0 %collective-permute-start.2 = (f32[4,136,128]{2,1,0:T(8,128)S(1)}, f32[4,136,128]{2,1,0:T(8,128)S(1)}, u32[]{:S(2)}, u32[]{:S(2)}) collective-permute-start(f32[4,136,128]{2,1,0:T(8,128)S(1)} %get-tuple-element.47), channel_id=1, source_target_pairs={{0,3},{1,2},{2,1},{3,0},{4,28},{5,29},{6,30},{7,31},{8,11},{9,10},... | collective-permute-start | bytes 835592 | tf_op jit(solution)/shard_map/ppermute | solution.py:33
  15.7 9.1 %collective-permute-start.4 = (f32[4,136,128]{2,1,0:T(8,128)S(1)}, f32[4,136,128]{2,1,0:T(8,128)S(1)}, u32[]{:S(2)}, u32[]{:S(2)}) collective-permute-start(f32[4,136,128]{2,1,0:T(8,128)S(1)} %get-tuple-element.48), channel_id=1, source_target_pairs={{0,2},{1,3},{2,0},{3,1},{4,20},{5,21},{6,22},{7,23},{8,10},{9,11},... | collective-permute-start | bytes 835592 | tf_op jit(solution)/shard_map/ppermute | solution.py:33
  24.9 4.8 %collective-permute-start.5 = (f32[136,128]{1,0:T(8,128)S(1)}, f32[136,128]{1,0:T(8,128)S(1)}, u32[]{:S(2)}, u32[]{:S(2)}) collective-permute-start(f32[136,128]{1,0:T(8,128)S(1)} %get-tuple-element.52), channel_id=1, source_target_pairs={{0,16},{1,17},{2,18},{3,19},{4,6},{5,7},{6,4},{7,5},{8,24},{9,25},... | collective-permute-start | bytes 208904 | tf_op jit(solution)/shard_map/ppermute | solution.py:33
  26.5 4.7 %collective-permute-start.7 = (f32[136,128]{1,0:T(8,128)S(1)}, f32[136,128]{1,0:T(8,128)S(1)}, u32[]{:S(2)}, u32[]{:S(2)}) collective-permute-start(f32[136,128]{1,0:T(8,128)S(1)} %get-tuple-element.53), channel_id=1, source_target_pairs={{0,24},{1,25},{2,26},{3,27},{4,7},{5,6},{6,5},{7,4},{8,16},{9,17},... | collective-permute-start | bytes 208904 | tf_op jit(solution)/shard_map/ppermute | solution.py:33
  27.4 3.8 %collective-permute-start.6 = (f32[136,128]{1,0:T(8,128)S(1)}, f32[136,128]{1,0:T(8,128)S(1)}, u32[]{:S(2)}, u32[]{:S(2)}) collective-permute-start(f32[136,128]{1,0:T(8,128)S(1)} %get-tuple-element.54), channel_id=1, source_target_pairs={{0,8},{1,9},{2,10},{3,11},{4,5},{5,4},{6,7},{7,6},{8,0},{9,1},{10,... | collective-permute-start | bytes 208904 | tf_op jit(solution)/shard_map/ppermute | solution.py:33
  31.2 4.4 %collective-permute-start.10 = (f32[136,128]{1,0:T(8,128)S(1)}, f32[136,128]{1,0:T(8,128)S(1)}, u32[]{:S(2)}, u32[]{:S(2)}) collective-permute-start(f32[136,128]{1,0:T(8,128)S(1)} %fusion.9), channel_id=1, source_target_pairs={{0,32},{1,33},{2,34},{3,35},{4,36},{5,37},{6,38},{7,39},{8,40},{9,... | collective-permute-start | bytes 208904 | tf_op jit(solution)/shard_map/ppermute | solution.py:33
  32.7 5.4 %collective-permute-start.9 = (f32[136,128]{1,0:T(8,128)S(1)}, f32[136,128]{1,0:T(8,128)S(1)}, u32[]{:S(2)}, u32[]{:S(2)}) collective-permute-start(f32[136,128]{1,0:T(8,128)S(1)} %fusion.9), channel_id=1, source_target_pairs={{0,64},{1,65},{2,66},{3,67},{4,68},{5,69},{6,70},{7,71},{8,72},{9,... | collective-permute-start | bytes 208904 | tf_op jit(solution)/shard_map/ppermute | solution.py:33
  35.7 5.8 %collective-permute-start.8 = (f32[136,128]{1,0:T(8,128)S(1)}, f32[136,128]{1,0:T(8,128)S(1)}, u32[]{:S(2)}, u32[]{:S(2)}) collective-permute-start(f32[136,128]{1,0:T(8,128)S(1)} %fusion.9), channel_id=1, source_target_pairs={{0,96},{1,97},{2,98},{3,99},{4,100},{5,101},{6,102},{7,103},{8,104... | collective-permute-start | bytes 208904 | tf_op jit(solution)/shard_map/ppermute | solution.py:33
  41.5 6.1 %collective-permute-start.11 = (f32[136,128]{1,0:T(8,128)S(1)}, f32[136,128]{1,0:T(8,128)S(1)}, u32[]{:S(2)}, u32[]{:S(2)}) collective-permute-start(f32[136,128]{1,0:T(8,128)S(1)} %add_add_fusion.1), channel_id=1, source_target_pairs={{0,192},{1,193},{2,194},{3,195},{4,196},{5,197},{6,198},{7,199},{8... | collective-permute-start | bytes 208904 | tf_op jit(solution)/shard_map/ppermute | solution.py:33
  65.2 9.2 %collective-permute-start.12 = (f32[16,136,128]{2,1,0:T(8,128)S(1)}, f32[16,136,128]{2,1,0:T(8,128)S(1)}, u32[]{:S(2)}, u32[]{:S(2)}) collective-permute-start(f32[16,136,128]{2,1,0:T(8,128)S(1)} %all_to_all.10.own), channel_id=1, source_target_pairs={{0,4},{1,5},{2,6},{3,7},{4,0},{5,1},{6,2},{7,3},{8,12},{9,13},{10,... | collective-permute-start | bytes 3342344 | tf_op jit(solution)/shard_map/ppermute | solution.py:33
  78.9 2.0 %collective-permute-start.13 = (f32[8,136,128]{2,1,0:T(8,128)S(1)}, f32[8,136,128]{2,1,0:T(8,128)S(1)}, u32[]{:S(2)}, u32[]{:S(2)}) collective-permute-start(f32[8,136,128]{2,1,0:T(8,128)S(1)} %get-tuple-element.34), channel_id=1, source_target_pairs={{0,4},{1,5},{2,6},{3,7},{4,0},{5,1},{6,2},{7,3},{8,12},{9,13},{10,... | collective-permute-start | bytes 1671176 | tf_op jit(solution)/shard_map/ppermute | solution.py:33
  79.0 2.7 %collective-permute-start.14 = (f32[8,136,128]{2,1,0:T(8,128)S(1)}, f32[8,136,128]{2,1,0:T(8,128)S(1)}, u32[]{:S(2)}, u32[]{:S(2)}) collective-permute-start(f32[8,136,128]{2,1,0:T(8,128)S(1)} %get-tuple-element.36), channel_id=1, source_target_pairs={{0,4},{1,5},{2,6},{3,7},{4,0},{5,1},{6,2},{7,3},{8,12},{9,13},{10,... | collective-permute-start | bytes 1671176 | tf_op jit(solution)/shard_map/ppermute | solution.py:33
  81.1 5.8 %collective-permute-start.16 = (f32[4,136,128]{2,1,0:T(8,128)S(1)}, f32[4,136,128]{2,1,0:T(8,128)S(1)}, u32[]{:S(2)}, u32[]{:S(2)}) collective-permute-start(f32[4,136,128]{2,1,0:T(8,128)S(1)} %slice.74), channel_id=1, source_target_pairs={{0,1},{1,0},{2,3},{3,2},{4,12},{5,13},{6,14},{7,15},{8,9},{9,8},{1... | collective-permute-start | bytes 835592 | tf_op jit(solution)/shard_map/ppermute | solution.py:33
  81.9 10.0 %collective-permute-start.15 = (f32[4,136,128]{2,1,0:T(8,128)S(1)}, f32[4,136,128]{2,1,0:T(8,128)S(1)}, u32[]{:S(2)}, u32[]{:S(2)}) collective-permute-start(f32[4,136,128]{2,1,0:T(8,128)S(1)} %get-tuple-element.45), channel_id=1, source_target_pairs={{0,3},{1,2},{2,1},{3,0},{4,28},{5,29},{6,30},{7,31},{8,11},{9,10},... | collective-permute-start | bytes 835592 | tf_op jit(solution)/shard_map/ppermute | solution.py:33
  82.8 9.0 %collective-permute-start.17 = (f32[4,136,128]{2,1,0:T(8,128)S(1)}, f32[4,136,128]{2,1,0:T(8,128)S(1)}, u32[]{:S(2)}, u32[]{:S(2)}) collective-permute-start(f32[4,136,128]{2,1,0:T(8,128)S(1)} %get-tuple-element.46), channel_id=1, source_target_pairs={{0,2},{1,3},{2,0},{3,1},{4,20},{5,21},{6,22},{7,23},{8,10},{9,11},... | collective-permute-start | bytes 835592 | tf_op jit(solution)/shard_map/ppermute | solution.py:33
  91.9 4.8 %collective-permute-start.18 = (f32[136,128]{1,0:T(8,128)S(1)}, f32[136,128]{1,0:T(8,128)S(1)}, u32[]{:S(2)}, u32[]{:S(2)}) collective-permute-start(f32[136,128]{1,0:T(8,128)S(1)} %get-tuple-element.49), channel_id=1, source_target_pairs={{0,16},{1,17},{2,18},{3,19},{4,6},{5,7},{6,4},{7,5},{8,24},{9,25},... | collective-permute-start | bytes 208904 | tf_op jit(solution)/shard_map/ppermute | solution.py:33
  93.0 4.8 %collective-permute-start.20 = (f32[136,128]{1,0:T(8,128)S(1)}, f32[136,128]{1,0:T(8,128)S(1)}, u32[]{:S(2)}, u32[]{:S(2)}) collective-permute-start(f32[136,128]{1,0:T(8,128)S(1)} %get-tuple-element.50), channel_id=1, source_target_pairs={{0,24},{1,25},{2,26},{3,27},{4,7},{5,6},{6,5},{7,4},{8,16},{9,17},... | collective-permute-start | bytes 208904 | tf_op jit(solution)/shard_map/ppermute | solution.py:33
  94.4 3.5 %collective-permute-start.19 = (f32[136,128]{1,0:T(8,128)S(1)}, f32[136,128]{1,0:T(8,128)S(1)}, u32[]{:S(2)}, u32[]{:S(2)}) collective-permute-start(f32[136,128]{1,0:T(8,128)S(1)} %get-tuple-element.51), channel_id=1, source_target_pairs={{0,8},{1,9},{2,10},{3,11},{4,5},{5,4},{6,7},{7,6},{8,0},{9,1},{10,... | collective-permute-start | bytes 208904 | tf_op jit(solution)/shard_map/ppermute | solution.py:33
  97.9 5.2 %collective-permute-start.23 = (f32[136,128]{1,0:T(8,128)S(1)}, f32[136,128]{1,0:T(8,128)S(1)}, u32[]{:S(2)}, u32[]{:S(2)}) collective-permute-start(f32[136,128]{1,0:T(8,128)S(1)} %fusion.6), channel_id=1, source_target_pairs={{0,32},{1,33},{2,34},{3,35},{4,36},{5,37},{6,38},{7,39},{8,40},{9,... | collective-permute-start | bytes 208904 | tf_op jit(solution)/shard_map/ppermute | solution.py:33
  98.2 4.9 %collective-permute-start.22 = (f32[136,128]{1,0:T(8,128)S(1)}, f32[136,128]{1,0:T(8,128)S(1)}, u32[]{:S(2)}, u32[]{:S(2)}) collective-permute-start(f32[136,128]{1,0:T(8,128)S(1)} %fusion.6), channel_id=1, source_target_pairs={{0,64},{1,65},{2,66},{3,67},{4,68},{5,69},{6,70},{7,71},{8,72},{9,... | collective-permute-start | bytes 208904 | tf_op jit(solution)/shard_map/ppermute | solution.py:33
  98.8 5.7 %collective-permute-start.21 = (f32[136,128]{1,0:T(8,128)S(1)}, f32[136,128]{1,0:T(8,128)S(1)}, u32[]{:S(2)}, u32[]{:S(2)}) collective-permute-start(f32[136,128]{1,0:T(8,128)S(1)} %fusion.6), channel_id=1, source_target_pairs={{0,96},{1,97},{2,98},{3,99},{4,100},{5,101},{6,102},{7,103},{8,104... | collective-permute-start | bytes 208904 | tf_op jit(solution)/shard_map/ppermute | solution.py:33
  104.5 5.5 %collective-permute-start.24 = (f32[136,128]{1,0:T(8,128)S(1)}, f32[136,128]{1,0:T(8,128)S(1)}, u32[]{:S(2)}, u32[]{:S(2)}) collective-permute-start(f32[136,128]{1,0:T(8,128)S(1)} %add_add_fusion), channel_id=1, source_target_pairs={{0,192},{1,193},{2,194},{3,195},{4,196},{5,197},{6,198},{7,199},{8... | collective-permute-start | bytes 208904 | tf_op jit(solution)/shard_map/ppermute | solution.py:33
  126.9 9.0 %collective-permute-start.25 = (f32[16,136,128]{2,1,0:T(8,128)S(1)}, f32[16,136,128]{2,1,0:T(8,128)S(1)}, u32[]{:S(2)}, u32[]{:S(2)}) collective-permute-start(f32[16,136,128]{2,1,0:T(8,128)S(1)} %all_to_all.11.own), channel_id=1, source_target_pairs={{0,4},{1,5},{2,6},{3,7},{4,0},{5,1},{6,2},{7,3},{8,12},{9,13},{10,... | collective-permute-start | bytes 3342344 | tf_op jit(solution)/shard_map/ppermute | solution.py:33

commit v5 on v4

--- a/solution.py
+++ b/solution.py
@@ -52,9 +52,10 @@
 
 
 def sum_everywhere(give, keep, beside=()):
-    far, near = [mine + other_core(theirs) for mine, theirs in zip(keep, give)]
-    arrived = [exchange(part, plane_partner(mask, True)) for part, mask in ((far[4:], 3), (near[4:], 1), (far[:4], 2))]
-    half = near[:4] + arrived[0] + arrived[1] + arrived[2]
+    far, near = [[(mine[i : i + 4], other[i : i + 4]) for i in (0, 4)] for mine, other in zip(keep, map(other_core, give))]
+    far, near = [[mine + other for mine, other in pair] for pair in (far, near)]
+    arrived = [exchange(part, plane_partner(mask, True)) for part, mask in ((far[1], 3), (near[1], 1), (far[0], 2))]
+    half = [near[0][b] + arrived[0][b] + arrived[1][b] + arrived[2][b] for b in range(4)]
     arrived = [exchange(half[mask], plane_partner(mask, False)) for mask in (2, 1, 3)]
     part = half[0] + arrived[0] + arrived[1] + arrived[2]
     arrived = [exchange(part, column_partner(mask)) for mask in (3, 2, 1)]

time: 138 us -> 138 us (level)
  no operation moved by 1% of the time
where the time goes in v5:
time: 138 us
  starting transfers between devices  39.9 us (29%)
  waiting for transfers between devices  37.9 us (27%)
  blocking collectives  34 us (25%)
  Pallas kernels  21.9 us (16%)
    ppermute x26, starting transfers between devices, exchange(): return lax.ppermute(value, AXES, pairs)  39.9 us
    ppermute x26, waiting for transfers between devices, exchange(): return lax.ppermute(value, AXES, pairs)  37.9 us
    all_to_all x2, blocking collectives, sum_everywhere(): lax.all_to_all(jnp.broadcast_to(part, (PLANE,) + part.shape), ('x', 'y'),...  34 us
    pallas_call x1, Pallas kernels, start_call(): pl.pallas_call(start_kernel, out_shape=(jax.ShapeDtypeStruct((rows, K), j...  7.17 us
    pallas_call x2, Pallas kernels, factor_call(): pl.pallas_call(factor_kernel, out_shape=SQUARE, in_specs=[SM, VM], out_sp...  6.64 us
    pallas_call x1, Pallas kernels, middle_call(): pl.pallas_call(middle_kernel, out_shape=(jax.ShapeDtypeStruct((rows, K),...  4.56 us
  transfers between devices with their start and end apart: 26, of which 18 were waited for; matrix products, arithmetic and copies ran while one was open for 1% of the time, Pallas kernels for 6%

profile of v5, /device:TPU:1, one launch (start us, length us, event | category | flops | bytes accessed | tf_op | source)
XLA Modules:
  0.0 138.0 jit_solution(11438541720271720161)
XLA Ops:
  0.6 1.2 copy-done
  1.9 7.2 %start.1 = (f32[1024,128]{1,0:T(8,128)S(1)}, f32[8,136,128]{2,1,0:T(8,128)S(1)}, f32[8,136,128]{2,1,0:T(8,128)S(1)}, f32[8,136,128]{2,1,0:T(8,128)S(1)}, f32[8,136,128]{2,1,0:T(8,128)S(1)}) custom-call(s32[1]{0:T(128)} %bitcast.core, s32[1]{0:T(128)} %bitcast.1.x, s32[1]{0:T(128)} %bitcast.2.y, bf16[1024,4096]{1,0:T(8,128)(2,1)} %held.3, ...), custom_call_target="tpu_custom_call" | custom-call | tf_op jit(solution)/shard_map/start/pallas_call | solution.py:283
  9.0 3.3 %collective-permute-start = (f32[8,136,128]{2,1,0:T(8,128)S(1)}, f32[8,136,128]{2,1,0:T(8,128)S(1)}, u32[]{:S(2)}, u32[]{:S(2)}) collective-permute-start(f32[8,136,128]{2,1,0:T(8,128)S(1)} %get-tuple-element.25), channel_id=1, source_target_pairs={{0,4},{1,5},{2,6},{3,7},{4,0},{5,1},{6,2},{7,3},{8,12},{9,13},{10,... | collective-permute-start | bytes 1671176 | tf_op jit(solution)/shard_map/ppermute | solution.py:33
  12.4 0.1 collective-permute-start.1
  12.5 1.5 %collective-permute-done = f32[8,136,128]{2,1,0:T(8,128)S(1)} collective-permute-done((f32[8,136,128]{2,1,0:T(8,128)S(1)}, f32[8,136,128]{2,1,0:T(8,128)S(1)}, u32[]{:S(2)}, u32[]{:S(2)}) %collective-permute-start) | collective-permute-done | bytes 557088 | tf_op jit(solution)/shard_map/ppermute | solution.py:33
  14.0 0.1 slice_add_fusion.7
  14.0 0.1 collective-permute-start.3
  14.1 0.6 collective-permute-done.1
  14.7 0.1 slice_add_fusion.6
  14.8 0.8 collective-permute-start.2
  15.7 1.9 %collective-permute-start.4 = (f32[4,136,128]{2,1,0:T(8,128)S(1)}, f32[4,136,128]{2,1,0:T(8,128)S(1)}, u32[]{:S(2)}, u32[]{:S(2)}) collective-permute-start(f32[4,136,128]{2,1,0:T(8,128)S(1)} %get-tuple-element.58), channel_id=1, source_target_pairs={{0,2},{1,3},{2,0},{3,1},{4,20},{5,21},{6,22},{7,23},{8,10},{9,11},... | collective-permute-start | bytes 835592 | tf_op jit(solution)/shard_map/ppermute | solution.py:33
  17.5 2.3 %collective-permute-done.3 = f32[4,136,128]{2,1,0:T(8,128)S(1)} collective-permute-done((f32[4,136,128]{2,1,0:T(8,128)S(1)}, f32[4,136,128]{2,1,0:T(8,128)S(1)}, u32[]{:S(2)}, u32[]{:S(2)}) %collective-permute-start.3) | collective-permute-done | bytes 278560 | tf_op jit(solution)/shard_map/ppermute | solution.py:33
  19.8 5.0 %collective-permute-done.2 = f32[4,136,128]{2,1,0:T(8,128)S(1)} collective-permute-done((f32[4,136,128]{2,1,0:T(8,128)S(1)}, f32[4,136,128]{2,1,0:T(8,128)S(1)}, u32[]{:S(2)}, u32[]{:S(2)}) %collective-permute-start.2) | collective-permute-done | bytes 278560 | tf_op jit(solution)/shard_map/ppermute | solution.py:33
  24.8 0.0 collective-permute-done.4
  24.8 0.1 fusion.9
  24.9 1.6 %collective-permute-start.5 = (f32[136,128]{1,0:T(8,128)S(1)}, f32[136,128]{1,0:T(8,128)S(1)}, u32[]{:S(2)}, u32[]{:S(2)}) collective-permute-start(f32[136,128]{1,0:T(8,128)S(1)} %get-tuple-element.52), channel_id=1, source_target_pairs={{0,16},{1,17},{2,18},{3,19},{4,6},{5,7},{6,4},{7,5},{8,24},{9,25},... | collective-permute-start | bytes 208904 | tf_op jit(solution)/shard_map/ppermute | solution.py:33
  26.4 0.9 collective-permute-start.7
  27.3 0.3 collective-permute-start.6
  27.6 2.0 %collective-permute-done.5 = f32[136,128]{1,0:T(8,128)S(1)} collective-permute-done((f32[136,128]{1,0:T(8,128)S(1)}, f32[136,128]{1,0:T(8,128)S(1)}, u32[]{:S(2)}, u32[]{:S(2)}) %collective-permute-start.5) | collective-permute-done | bytes 69664 | tf_op jit(solution)/shard_map/ppermute | solution.py:33
  29.6 1.5 %collective-permute-done.7 = f32[136,128]{1,0:T(8,128)S(1)} collective-permute-done((f32[136,128]{1,0:T(8,128)S(1)}, f32[136,128]{1,0:T(8,128)S(1)}, u32[]{:S(2)}, u32[]{:S(2)}) %collective-permute-start.7) | collective-permute-done | bytes 69664 | tf_op jit(solution)/shard_map/ppermute | solution.py:33
  31.1 0.0 collective-permute-done.6
  31.1 1.4 %collective-permute-start.10 = (f32[136,128]{1,0:T(8,128)S(1)}, f32[136,128]{1,0:T(8,128)S(1)}, u32[]{:S(2)}, u32[]{:S(2)}) collective-permute-start(f32[136,128]{1,0:T(8,128)S(1)} %fusion.13), channel_id=1, source_target_pairs={{0,32},{1,33},{2,34},{3,35},{4,36},{5,37},{6,38},{7,39},{8,40},{9,... | collective-permute-start | bytes 208904 | tf_op jit(solution)/shard_map/ppermute | solution.py:33
  32.6 3.0 %collective-permute-start.9 = (f32[136,128]{1,0:T(8,128)S(1)}, f32[136,128]{1,0:T(8,128)S(1)}, u32[]{:S(2)}, u32[]{:S(2)}) collective-permute-start(f32[136,128]{1,0:T(8,128)S(1)} %fusion.13), channel_id=1, source_target_pairs={{0,64},{1,65},{2,66},{3,67},{4,68},{5,69},{6,70},{7,71},{8,72},{9,... | collective-permute-start | bytes 208904 | tf_op jit(solution)/shard_map/ppermute | solution.py:33
  35.6 0.0 collective-permute-done.10
  35.6 2.4 %collective-permute-done.9 = f32[136,128]{1,0:T(8,128)S(1)} collective-permute-done((f32[136,128]{1,0:T(8,128)S(1)}, f32[136,128]{1,0:T(8,128)S(1)}, u32[]{:S(2)}, u32[]{:S(2)}) %collective-permute-start.9) | collective-permute-done | bytes 69664 | tf_op jit(solution)/shard_map/ppermute | solution.py:33
  38.0 3.4 %collective-permute-done.8 = f32[136,128]{1,0:T(8,128)S(1)} collective-permute-done((f32[136,128]{1,0:T(8,128)S(1)}, f32[136,128]{1,0:T(8,128)S(1)}, u32[]{:S(2)}, u32[]{:S(2)}) %collective-permute-start.8) | collective-permute-done | bytes 69664 | tf_op jit(solution)/shard_map/ppermute | solution.py:33
  41.4 2.6 %collective-permute-start.11 = (f32[136,128]{1,0:T(8,128)S(1)}, f32[136,128]{1,0:T(8,128)S(1)}, u32[]{:S(2)}, u32[]{:S(2)}) collective-permute-start(f32[136,128]{1,0:T(8,128)S(1)} %add_add_fusion.1), channel_id=1, source_target_pairs={{0,192},{1,193},{2,194},{3,195},{4,196},{5,197},{6,198},{7,199},{8... | collective-permute-start | bytes 208904 | tf_op jit(solution)/shard_map/ppermute | solution.py:33
  44.0 3.5 %collective-permute-done.11 = f32[136,128]{1,0:T(8,128)S(1)} collective-permute-done((f32[136,128]{1,0:T(8,128)S(1)}, f32[136,128]{1,0:T(8,128)S(1)}, u32[]{:S(2)}, u32[]{:S(2)}) %collective-permute-start.11) | collective-permute-done | bytes 69664 | tf_op jit(solution)/shard_map/ppermute | solution.py:33
  47.5 0.1 broadcast_in_dim.6
  47.6 17.5 %all_to_all.10.own = f32[16,136,128]{2,1,0:T(8,128)S(1)} all-to-all(f32[16,136,128]{2,1,0:T(8,128)S(1)} %broadcast_in_dim.6), channel_id=1, replica_groups=mesh['z'=8,'x'=4,'core'=2,'y'=4] {'x','y'}, dimensions={0} | all-to-all | bytes 2228224 | tf_op jit(solution)/shard_map/all_to_all | solution.py:65
  65.1 5.8 %collective-permute-start.12 = (f32[16,136,128]{2,1,0:T(8,128)S(1)}, f32[16,136,128]{2,1,0:T(8,128)S(1)}, u32[]{:S(2)}, u32[]{:S(2)}) collective-permute-start(f32[16,136,128]{2,1,0:T(8,128)S(1)} %all_to_all.10.own), channel_id=1, source_target_pairs={{0,4},{1,5},{2,6},{3,7},{4,0},{5,1},{6,2},{7,3},{8,12},{9,13},{10,... | collective-permute-start | bytes 3342344 | tf_op jit(solution)/shard_map/ppermute | solution.py:33
  70.9 3.3 %factor.2.inverse = f32[128,128]{1,0:T(8,128)S(1)} custom-call(s32[1]{0:T(128)} %bitcast.core, f32[16,136,128]{2,1,0:T(8,128)S(1)} %all_to_all.10.own), custom_call_target="tpu_custom_call" | custom-call | flops 2097152 | bytes 1000000 | tf_op jit(solution)/shard_map/factor/pallas_call | solution.py:300
  74.3 4.6 %middle.1 = (f32[1024,128]{1,0:T(8,128)S(1)}, bf16[256,1024]{1,0:T(8,128)(2,1)S(1)}, f32[128,128]{1,0:T(8,128)S(1)}, f32[8,136,128]{2,1,0:T(8,128)S(1)}, f32[8,136,128]{2,1,0:T(8,128)S(1)}) custom-call(s32[1]{0:T(128)} %bitcast.core, s32[1]{0:T(128)} %bitcast.1.x, s32[1]{0:T(128)} %bitcast.2.y, f32[16,136,128]{2,1,0:T(8,128)S(1)} %all_to_all.10.own, ...), custom_call_target="tpu_custom_call" | custom-call | tf_op jit(solution)/shard_map/middle/pallas_call | solution.py:314
  78.9 0.1 collective-permute-start.13
  79.0 0.5 collective-permute-start.14
  79.5 1.3 keep.1
  80.7 0.2 collective-permute-done.13
  80.9 0.1 slice_add_fusion.3
  81.0 0.3 collective-permute-start.16
  81.3 0.4 collective-permute-done.14
  81.7 0.1 slice_add_fusion.2
  81.8 0.9 collective-permute-start.15
  82.7 1.8 %collective-permute-start.17 = (f32[4,136,128]{2,1,0:T(8,128)S(1)}, f32[4,136,128]{2,1,0:T(8,128)S(1)}, u32[]{:S(2)}, u32[]{:S(2)}) collective-permute-start(f32[4,136,128]{2,1,0:T(8,128)S(1)} %get-tuple-element.51), channel_id=1, source_target_pairs={{0,2},{1,3},{2,0},{3,1},{4,20},{5,21},{6,22},{7,23},{8,10},{9,11},... | collective-permute-start | bytes 835592 | tf_op jit(solution)/shard_map/ppermute | solution.py:33
  84.5 2.3 %collective-permute-done.16 = f32[4,136,128]{2,1,0:T(8,128)S(1)} collective-permute-done((f32[4,136,128]{2,1,0:T(8,128)S(1)}, f32[4,136,128]{2,1,0:T(8,128)S(1)}, u32[]{:S(2)}, u32[]{:S(2)}) %collective-permute-start.16) | collective-permute-done | bytes 278560 | tf_op jit(solution)/shard_map/ppermute | solution.py:33
  86.7 5.0 %collective-permute-done.15 = f32[4,136,128]{2,1,0:T(8,128)S(1)} collective-permute-done((f32[4,136,128]{2,1,0:T(8,128)S(1)}, f32[4,136,128]{2,1,0:T(8,128)S(1)}, u32[]{:S(2)}, u32[]{:S(2)}) %collective-permute-start.15) | collective-permute-done | bytes 278560 | tf_op jit(solution)/shard_map/ppermute | solution.py:33
  91.8 1.0 collective-permute-start.18
  92.8 1.4 %collective-permute-start.20 = (f32[136,128]{1,0:T(8,128)S(1)}, f32[136,128]{1,0:T(8,128)S(1)}, u32[]{:S(2)}, u32[]{:S(2)}) collective-permute-start(f32[136,128]{1,0:T(8,128)S(1)} %get-tuple-element.46), channel_id=1, source_target_pairs={{0,24},{1,25},{2,26},{3,27},{4,7},{5,6},{6,5},{7,4},{8,16},{9,17},... | collective-permute-start | bytes 208904 | tf_op jit(solution)/shard_map/ppermute | solution.py:33
  94.3 0.3 collective-permute-start.19
  94.5 2.0 %collective-permute-done.18 = f32[136,128]{1,0:T(8,128)S(1)} collective-permute-done((f32[136,128]{1,0:T(8,128)S(1)}, f32[136,128]{1,0:T(8,128)S(1)}, u32[]{:S(2)}, u32[]{:S(2)}) %collective-permute-start.18) | collective-permute-done | bytes 69664 | tf_op jit(solution)/shard_map/ppermute | solution.py:33
  96.5 1.0 collective-permute-done.20
  97.6 0.1 collective-permute-done.19
  97.7 0.1 collective-permute-start.23
  97.8 0.8 collective-permute-start.22
  98.6 2.7 %collective-permute-start.21 = (f32[136,128]{1,0:T(8,128)S(1)}, f32[136,128]{1,0:T(8,128)S(1)}, u32[]{:S(2)}, u32[]{:S(2)}) collective-permute-start(f32[136,128]{1,0:T(8,128)S(1)} %fusion.6), channel_id=1, source_target_pairs={{0,96},{1,97},{2,98},{3,99},{4,100},{5,101},{6,102},{7,103},{8,104... | collective-permute-start | bytes 208904 | tf_op jit(solution)/shard_map/ppermute | solution.py:33
  101.4 1.4 fusion.14
  102.8 0.0 collective-permute-done.23
  102.8 1.4 collective-permute-done.21
  104.2 2.8 %collective-permute-start.24 = (f32[136,128]{1,0:T(8,128)S(1)}, f32[136,128]{1,0:T(8,128)S(1)}, u32[]{:S(2)}, u32[]{:S(2)}) collective-permute-start(f32[136,128]{1,0:T(8,128)S(1)} %add_add_fusion), channel_id=1, source_target_pairs={{0,192},{1,193},{2,194},{3,195},{4,196},{5,197},{6,198},{7,199},{8... | collective-permute-start | bytes 208904 | tf_op jit(solution)/shard_map/ppermute | solution.py:33
  106.9 3.3 %collective-permute-done.24 = f32[136,128]{1,0:T(8,128)S(1)} collective-permute-done((f32[136,128]{1,0:T(8,128)S(1)}, f32[136,128]{1,0:T(8,128)S(1)}, u32[]{:S(2)}, u32[]{:S(2)}) %collective-permute-start.24) | collective-permute-done | bytes 69664 | tf_op jit(solution)/shard_map/ppermute | solution.py:33
  110.3 0.1 broadcast_in_dim.7
  110.4 16.5 %all_to_all.11.own = f32[16,136,128]{2,1,0:T(8,128)S(1)} all-to-all(f32[16,136,128]{2,1,0:T(8,128)S(1)} %broadcast_in_dim.7), channel_id=1, replica_groups=mesh['z'=8,'x'=4,'core'=2,'y'=4] {'x','y'}, dimensions={0} | all-to-all | bytes 2228224 | tf_op jit(solution)/shard_map/all_to_all | solution.py:65
  126.8 5.4 %collective-permute-start.25 = (f32[16,136,128]{2,1,0:T(8,128)S(1)}, f32[16,136,128]{2,1,0:T(8,128)S(1)}, u32[]{:S(2)}, u32[]{:S(2)}) collective-permute-start(f32[16,136,128]{2,1,0:T(8,128)S(1)} %all_to_all.11.own), channel_id=1, source_target_pairs={{0,4},{1,5},{2,6},{3,7},{4,0},{5,1},{6,2},{7,3},{8,12},{9,13},{10,... | collective-permute-start | bytes 3342344 | tf_op jit(solution)/shard_map/ppermute | solution.py:33
  132.3 3.3 %factor.3.inverse = f32[128,128]{1,0:T(8,128)S(1)} custom-call(s32[1]{0:T(128)} %bitcast.core, f32[16,136,128]{2,1,0:T(8,128)S(1)} %all_to_all.11.own), custom_call_target="tpu_custom_call" | custom-call | flops 2097152 | bytes 1000000 | tf_op jit(solution)/shard_map/factor/pallas_call | solution.py:300
  135.6 2.3 %final.1 = (f32[128,4096]{1,0:T(8,128)}, f32[1024,128]{1,0:T(8,128)}) custom-call(s32[1]{0:T(128)} %bitcast.core, s32[1]{0:T(128)} %bitcast.1.x, s32[1]{0:T(128)} %bitcast.2.y, f32[16,136,128]{2,1,0:T(8,128)S(1)} %all_to_all.11.own, f32[16,136,128]{2,1,0:T(8,128)S(1)} %collective-permute-done.25.other, f32[128,128]{1,0:T(8,128)S(1)} %factor.3.inverse, ...), custom_call_target="tpu_custom_call" | custom-call | tf_op jit(solution)/shard_map/final/pallas_call | solution.py:344
  (18 shorter events, 0.2 us)
Async XLA Ops:
  0.6 1.2 copy-start
  1.9 72.4 %slice-start = ((s8[8388608]{0:T(1024)(128)(4,1)}), s8[4194304]{0:T(1024)(128)(4,1)S(1)}, s32[]{:S(2)}) async-start(s8[8388608]{0:T(1024)(128)(4,1)} %bitcast.32), calls=%async_computation.2 | async-start | bytes 8388608
  9.0 4.9 %collective-permute-start = (f32[8,136,128]{2,1,0:T(8,128)S(1)}, f32[8,136,128]{2,1,0:T(8,128)S(1)}, u32[]{:S(2)}, u32[]{:S(2)}) collective-permute-start(f32[8,136,128]{2,1,0:T(8,128)S(1)} %get-tuple-element.25), channel_id=1, source_target_pairs={{0,4},{1,5},{2,6},{3,7},{4,0},{5,1},{6,2},{7,3},{8,12},{9,13},{10,... | collective-permute-start | bytes 1671176 | tf_op jit(solution)/shard_map/ppermute | solution.py:33
  12.4 2.4 %collective-permute-start.1 = (f32[8,136,128]{2,1,0:T(8,128)S(1)}, f32[8,136,128]{2,1,0:T(8,128)S(1)}, u32[]{:S(2)}, u32[]{:S(2)}) collective-permute-start(f32[8,136,128]{2,1,0:T(8,128)S(1)} %get-tuple-element.27), channel_id=1, source_target_pairs={{0,4},{1,5},{2,6},{3,7},{4,0},{5,1},{6,2},{7,3},{8,12},{9,13},{10,... | collective-permute-start | bytes 1671176 | tf_op jit(solution)/shard_map/ppermute | solution.py:33
  14.0 60.3 %slice-start.1 = ((s8[8388608]{0:T(1024)(128)(4,1)}), s8[4194304]{0:T(1024)(128)(4,1)S(1)}, s32[]{:S(2)}) async-start(s8[8388608]{0:T(1024)(128)(4,1)} %bitcast.32), calls=%async_computation.3 | async-start | bytes 8388608
  14.0 5.8 %collective-permute-start.3 = (f32[4,136,128]{2,1,0:T(8,128)S(1)}, f32[4,136,128]{2,1,0:T(8,128)S(1)}, u32[]{:S(2)}, u32[]{:S(2)}) collective-permute-start(f32[4,136,128]{2,1,0:T(8,128)S(1)} %get-tuple-element.56), channel_id=1, source_target_pairs={{0,1},{1,0},{2,3},{3,2},{4,12},{5,13},{6,14},{7,15},{8,9},{9,8},{1... | collective-permute-start | bytes 835592 | tf_op jit(solution)/shard_map/ppermute | solution.py:33
  14.8 10.0 %collective-permute-start.2 = (f32[4,136,128]{2,1,0:T(8,128)S(1)}, f32[4,136,128]{2,1,0:T(8,128)S(1)}, u32[]{:S(2)}, u32[]{:S(2)}) collective-permute-start(f32[4,136,128]{2,1,0:T(8,128)S(1)} %get-tuple-element.57), channel_id=1, source_target_pairs={{0,3},{1,2},{2,1},{3,0},{4,28},{5,29},{6,30},{7,31},{8,11},{9,10},... | collective-permute-start | bytes 835592 | tf_op jit(solution)/shard_map/ppermute | solution.py:33
  15.7 9.1 %collective-permute-start.4 = (f32[4,136,128]{2,1,0:T(8,128)S(1)}, f32[4,136,128]{2,1,0:T(8,128)S(1)}, u32[]{:S(2)}, u32[]{:S(2)}) collective-permute-start(f32[4,136,128]{2,1,0:T(8,128)S(1)} %get-tuple-element.58), channel_id=1, source_target_pairs={{0,2},{1,3},{2,0},{3,1},{4,20},{5,21},{6,22},{7,23},{8,10},{9,11},... | collective-permute-start | bytes 835592 | tf_op jit(solution)/shard_map/ppermute | solution.py:33
  24.9 4.8 %collective-permute-start.5 = (f32[136,128]{1,0:T(8,128)S(1)}, f32[136,128]{1,0:T(8,128)S(1)}, u32[]{:S(2)}, u32[]{:S(2)}) collective-permute-start(f32[136,128]{1,0:T(8,128)S(1)} %get-tuple-element.52), channel_id=1, source_target_pairs={{0,16},{1,17},{2,18},{3,19},{4,6},{5,7},{6,4},{7,5},{8,24},{9,25},... | collective-permute-start | bytes 208904 | tf_op jit(solution)/shard_map/ppermute | solution.py:33
  26.4 4.7 %collective-permute-start.7 = (f32[136,128]{1,0:T(8,128)S(1)}, f32[136,128]{1,0:T(8,128)S(1)}, u32[]{:S(2)}, u32[]{:S(2)}) collective-permute-start(f32[136,128]{1,0:T(8,128)S(1)} %get-tuple-element.53), channel_id=1, source_target_pairs={{0,24},{1,25},{2,26},{3,27},{4,7},{5,6},{6,5},{7,4},{8,16},{9,17},... | collective-permute-start | bytes 208904 | tf_op jit(solution)/shard_map/ppermute | solution.py:33
  27.3 3.8 %collective-permute-start.6 = (f32[136,128]{1,0:T(8,128)S(1)}, f32[136,128]{1,0:T(8,128)S(1)}, u32[]{:S(2)}, u32[]{:S(2)}) collective-permute-start(f32[136,128]{1,0:T(8,128)S(1)} %get-tuple-element.54), channel_id=1, source_target_pairs={{0,8},{1,9},{2,10},{3,11},{4,5},{5,4},{6,7},{7,6},{8,0},{9,1},{10,... | collective-permute-start | bytes 208904 | tf_op jit(solution)/shard_map/ppermute | solution.py:33
  31.1 4.4 %collective-permute-start.10 = (f32[136,128]{1,0:T(8,128)S(1)}, f32[136,128]{1,0:T(8,128)S(1)}, u32[]{:S(2)}, u32[]{:S(2)}) collective-permute-start(f32[136,128]{1,0:T(8,128)S(1)} %fusion.13), channel_id=1, source_target_pairs={{0,32},{1,33},{2,34},{3,35},{4,36},{5,37},{6,38},{7,39},{8,40},{9,... | collective-permute-start | bytes 208904 | tf_op jit(solution)/shard_map/ppermute | solution.py:33
  32.6 5.4 %collective-permute-start.9 = (f32[136,128]{1,0:T(8,128)S(1)}, f32[136,128]{1,0:T(8,128)S(1)}, u32[]{:S(2)}, u32[]{:S(2)}) collective-permute-start(f32[136,128]{1,0:T(8,128)S(1)} %fusion.13), channel_id=1, source_target_pairs={{0,64},{1,65},{2,66},{3,67},{4,68},{5,69},{6,70},{7,71},{8,72},{9,... | collective-permute-start | bytes 208904 | tf_op jit(solution)/shard_map/ppermute | solution.py:33
  35.6 5.8 %collective-permute-start.8 = (f32[136,128]{1,0:T(8,128)S(1)}, f32[136,128]{1,0:T(8,128)S(1)}, u32[]{:S(2)}, u32[]{:S(2)}) collective-permute-start(f32[136,128]{1,0:T(8,128)S(1)} %fusion.13), channel_id=1, source_target_pairs={{0,96},{1,97},{2,98},{3,99},{4,100},{5,101},{6,102},{7,103},{8,104... | collective-permute-start | bytes 208904 | tf_op jit(solution)/shard_map/ppermute | solution.py:33
  41.4 6.1 %collective-permute-start.11 = (f32[136,128]{1,0:T(8,128)S(1)}, f32[136,128]{1,0:T(8,128)S(1)}, u32[]{:S(2)}, u32[]{:S(2)}) collective-permute-start(f32[136,128]{1,0:T(8,128)S(1)} %add_add_fusion.1), channel_id=1, source_target_pairs={{0,192},{1,193},{2,194},{3,195},{4,196},{5,197},{6,198},{7,199},{8... | collective-permute-start | bytes 208904 | tf_op jit(solution)/shard_map/ppermute | solution.py:33
  65.1 9.1 %collective-permute-start.12 = (f32[16,136,128]{2,1,0:T(8,128)S(1)}, f32[16,136,128]{2,1,0:T(8,128)S(1)}, u32[]{:S(2)}, u32[]{:S(2)}) collective-permute-start(f32[16,136,128]{2,1,0:T(8,128)S(1)} %all_to_all.10.own), channel_id=1, source_target_pairs={{0,4},{1,5},{2,6},{3,7},{4,0},{5,1},{6,2},{7,3},{8,12},{9,13},{10,... | collective-permute-start | bytes 3342344 | tf_op jit(solution)/shard_map/ppermute | solution.py:33
  78.9 2.0 %collective-permute-start.13 = (f32[8,136,128]{2,1,0:T(8,128)S(1)}, f32[8,136,128]{2,1,0:T(8,128)S(1)}, u32[]{:S(2)}, u32[]{:S(2)}) collective-permute-start(f32[8,136,128]{2,1,0:T(8,128)S(1)} %get-tuple-element.34), channel_id=1, source_target_pairs={{0,4},{1,5},{2,6},{3,7},{4,0},{5,1},{6,2},{7,3},{8,12},{9,13},{10,... | collective-permute-start | bytes 1671176 | tf_op jit(solution)/shard_map/ppermute | solution.py:33
  79.0 2.7 %collective-permute-start.14 = (f32[8,136,128]{2,1,0:T(8,128)S(1)}, f32[8,136,128]{2,1,0:T(8,128)S(1)}, u32[]{:S(2)}, u32[]{:S(2)}) collective-permute-start(f32[8,136,128]{2,1,0:T(8,128)S(1)} %get-tuple-element.36), channel_id=1, source_target_pairs={{0,4},{1,5},{2,6},{3,7},{4,0},{5,1},{6,2},{7,3},{8,12},{9,13},{10,... | collective-permute-start | bytes 1671176 | tf_op jit(solution)/shard_map/ppermute | solution.py:33
  81.0 5.8 %collective-permute-start.16 = (f32[4,136,128]{2,1,0:T(8,128)S(1)}, f32[4,136,128]{2,1,0:T(8,128)S(1)}, u32[]{:S(2)}, u32[]{:S(2)}) collective-permute-start(f32[4,136,128]{2,1,0:T(8,128)S(1)} %get-tuple-element.49), channel_id=1, source_target_pairs={{0,1},{1,0},{2,3},{3,2},{4,12},{5,13},{6,14},{7,15},{8,9},{9,8},{1... | collective-permute-start | bytes 835592 | tf_op jit(solution)/shard_map/ppermute | solution.py:33
  81.8 10.0 %collective-permute-start.15 = (f32[4,136,128]{2,1,0:T(8,128)S(1)}, f32[4,136,128]{2,1,0:T(8,128)S(1)}, u32[]{:S(2)}, u32[]{:S(2)}) collective-permute-start(f32[4,136,128]{2,1,0:T(8,128)S(1)} %get-tuple-element.50), channel_id=1, source_target_pairs={{0,3},{1,2},{2,1},{3,0},{4,28},{5,29},{6,30},{7,31},{8,11},{9,10},... | collective-permute-start | bytes 835592 | tf_op jit(solution)/shard_map/ppermute | solution.py:33
  82.7 9.0 %collective-permute-start.17 = (f32[4,136,128]{2,1,0:T(8,128)S(1)}, f32[4,136,128]{2,1,0:T(8,128)S(1)}, u32[]{:S(2)}, u32[]{:S(2)}) collective-permute-start(f32[4,136,128]{2,1,0:T(8,128)S(1)} %get-tuple-element.51), channel_id=1, source_target_pairs={{0,2},{1,3},{2,0},{3,1},{4,20},{5,21},{6,22},{7,23},{8,10},{9,11},... | collective-permute-start | bytes 835592 | tf_op jit(solution)/shard_map/ppermute | solution.py:33
  91.8 4.8 %collective-permute-start.18 = (f32[136,128]{1,0:T(8,128)S(1)}, f32[136,128]{1,0:T(8,128)S(1)}, u32[]{:S(2)}, u32[]{:S(2)}) collective-permute-start(f32[136,128]{1,0:T(8,128)S(1)} %get-tuple-element.45), channel_id=1, source_target_pairs={{0,16},{1,17},{2,18},{3,19},{4,6},{5,7},{6,4},{7,5},{8,24},{9,25},... | collective-permute-start | bytes 208904 | tf_op jit(solution)/shard_map/ppermute | solution.py:33
  92.8 4.8 %collective-permute-start.20 = (f32[136,128]{1,0:T(8,128)S(1)}, f32[136,128]{1,0:T(8,128)S(1)}, u32[]{:S(2)}, u32[]{:S(2)}) collective-permute-start(f32[136,128]{1,0:T(8,128)S(1)} %get-tuple-element.46), channel_id=1, source_target_pairs={{0,24},{1,25},{2,26},{3,27},{4,7},{5,6},{6,5},{7,4},{8,16},{9,17},... | collective-permute-start | bytes 208904 | tf_op jit(solution)/shard_map/ppermute | solution.py:33
  94.3 3.5 %collective-permute-start.19 = (f32[136,128]{1,0:T(8,128)S(1)}, f32[136,128]{1,0:T(8,128)S(1)}, u32[]{:S(2)}, u32[]{:S(2)}) collective-permute-start(f32[136,128]{1,0:T(8,128)S(1)} %get-tuple-element.47), channel_id=1, source_target_pairs={{0,8},{1,9},{2,10},{3,11},{4,5},{5,4},{6,7},{7,6},{8,0},{9,1},{10,... | collective-permute-start | bytes 208904 | tf_op jit(solution)/shard_map/ppermute | solution.py:33
  97.7 5.0 %collective-permute-start.23 = (f32[136,128]{1,0:T(8,128)S(1)}, f32[136,128]{1,0:T(8,128)S(1)}, u32[]{:S(2)}, u32[]{:S(2)}) collective-permute-start(f32[136,128]{1,0:T(8,128)S(1)} %fusion.6), channel_id=1, source_target_pairs={{0,32},{1,33},{2,34},{3,35},{4,36},{5,37},{6,38},{7,39},{8,40},{9,... | collective-permute-start | bytes 208904 | tf_op jit(solution)/shard_map/ppermute | solution.py:33
  97.8 4.9 %collective-permute-start.22 = (f32[136,128]{1,0:T(8,128)S(1)}, f32[136,128]{1,0:T(8,128)S(1)}, u32[]{:S(2)}, u32[]{:S(2)}) collective-permute-start(f32[136,128]{1,0:T(8,128)S(1)} %fusion.6), channel_id=1, source_target_pairs={{0,64},{1,65},{2,66},{3,67},{4,68},{5,69},{6,70},{7,71},{8,72},{9,... | collective-permute-start | bytes 208904 | tf_op jit(solution)/shard_map/ppermute | solution.py:33
  98.6 5.5 %collective-permute-start.21 = (f32[136,128]{1,0:T(8,128)S(1)}, f32[136,128]{1,0:T(8,128)S(1)}, u32[]{:S(2)}, u32[]{:S(2)}) collective-permute-start(f32[136,128]{1,0:T(8,128)S(1)} %fusion.6), channel_id=1, source_target_pairs={{0,96},{1,97},{2,98},{3,99},{4,100},{5,101},{6,102},{7,103},{8,104... | collective-permute-start | bytes 208904 | tf_op jit(solution)/shard_map/ppermute | solution.py:33
  104.2 6.1 %collective-permute-start.24 = (f32[136,128]{1,0:T(8,128)S(1)}, f32[136,128]{1,0:T(8,128)S(1)}, u32[]{:S(2)}, u32[]{:S(2)}) collective-permute-start(f32[136,128]{1,0:T(8,128)S(1)} %add_add_fusion), channel_id=1, source_target_pairs={{0,192},{1,193},{2,194},{3,195},{4,196},{5,197},{6,198},{7,199},{8... | collective-permute-start | bytes 208904 | tf_op jit(solution)/shard_map/ppermute | solution.py:33
  126.8 8.8 %collective-permute-start.25 = (f32[16,136,128]{2,1,0:T(8,128)S(1)}, f32[16,136,128]{2,1,0:T(8,128)S(1)}, u32[]{:S(2)}, u32[]{:S(2)}) collective-permute-start(f32[16,136,128]{2,1,0:T(8,128)S(1)} %all_to_all.11.own), channel_id=1, source_target_pairs={{0,4},{1,5},{2,6},{3,7},{4,0},{5,1},{6,2},{7,3},{8,12},{9,13},{10,... | collective-permute-start | bytes 3342344 | tf_op jit(solution)/shard_map/ppermute | solution.py:33
